TPU v7x, 256 devices: a whole 4x4x8 slice. The times are simulated.
256 devices in a mesh: head: 4 (over x), expert: 64 (over y, z, core).
Axes of the slice: x: 4, y: 4, z: 8, core: 2. Of those that a mesh axis runs over, the one named last changes fastest.
Arguments:
- query_rows: bfloat16 [4, 256, 4096], P(None, 'expert', 'head'), may hold values from -0.59765625 to 0.59765625
- key_rows: bfloat16 [4, 256, 4096], P(None, 'expert', 'head'), may hold values from -6 to 6
- value_rows: bfloat16 [4, 256, 4096], P(None, 'expert', 'head'), may hold values from -6 to 6
- forget: float32 [32], P('head'), may hold values from 0.02 to 2
- head_state: bfloat16 [256, 32, 128, 128], P('expert', 'head'), may hold values from -6 to 6
- out_weight: bfloat16 [4096, 6144], P('head', 'expert'), may hold values from -0.09375 to 0.09375
- route_ids: int32 [4, 256, 2], P(None, 'expert'), may hold values from 0 to 15, as said below
- route_gate: float32 [4, 256, 2], P(None, 'expert'), may hold values from 0.1 to 0.9
- gate_weight: bfloat16 [64, 6144, 1152], P('expert', None, 'head'), may hold values from -0.078125 to 0.078125
- up_weight: bfloat16 [64, 6144, 1152], P('expert', None, 'head'), may hold values from -0.078125 to 0.078125
- down_weight: bfloat16 [64, 1152, 6144], P('expert', 'head'), may hold values from -0.09375 to 0.09375
Outputs:
- mixed: bfloat16 [4, 256, 6144], P(None, 'expert')
- moe_out: bfloat16 [4, 256, 6144], P(None, 'expert')
- state_out: bfloat16 [256, 32, 128, 128], P('expert', 'head')
Inputs may be any that keep to these rules, and one draw needn't show every extreme that they name: `route_ids`: each row names two different experts. In each step at most 2 of the 4 rows of one device name the same expert, and one expert, drawn anew for each step, is named by exactly 2 rows of every device.
All inputs are finite; a program needn't handle non-finite values.
Results may differ from a plain program's by a relative error of at most 0.008.
Values may be sent and summed in bfloat16 or wider, within the bound.
No kernel may reach another device: no remote copies, remote signals or barrier semaphores. Data moves between devices by JAX's collectives and lax.ppermute only.
A program may use at most 128 MiB of HBM per device.

v0:
```python
import jax
import jax.numpy as jnp
from jax import lax
from jax.sharding import PartitionSpec as P


def expert_ffn(row_block, gate_local, up_local, down_local):
    feature_count = row_block.shape[-1]
    flat_rows = row_block.reshape(-1, feature_count)
    gated = jnp.dot(flat_rows, gate_local, preferred_element_type=jnp.float32)
    lifted = jnp.dot(flat_rows, up_local, preferred_element_type=jnp.float32)
    hidden = (jax.nn.silu(gated) * lifted).astype(jnp.bfloat16)
    result = jnp.dot(hidden, down_local, preferred_element_type=jnp.float32)
    return result.reshape(row_block.shape[:-1] + (down_local.shape[1],))


def mixture(inputs, route_ids, route_gate, gate_local, up_local, down_local):
    steps_here, row_count, feature_count = inputs.shape
    devices = lax.axis_size("expert")
    experts = max(4, devices // 4)
    slices = devices // experts
    capacity = row_count // 2
    onehot = (route_ids[..., None] == jnp.arange(experts, dtype=jnp.int32)).astype(jnp.int32)
    ranked = (jnp.cumsum(onehot.reshape(steps_here, row_count * 2, experts), axis=1) - 1).reshape(
        steps_here, row_count, 2, experts
    )
    landed = onehot[..., None] * (
        ranked[..., None] == jnp.arange(capacity, dtype=jnp.int32)
    ).astype(jnp.int32)
    placed = jnp.sum(landed, axis=2).astype(jnp.bfloat16)
    weights = jnp.sum(landed.astype(jnp.float32) * route_gate[..., None, None], axis=2)
    packed = jnp.einsum(
        "srec,srd->escd", placed, inputs, preferred_element_type=jnp.float32
    ).astype(jnp.bfloat16)
    packed = jnp.repeat(
        packed.reshape(experts, steps_here * capacity, feature_count), slices, axis=0
    )
    partial_out = expert_ffn(
        lax.all_to_all(packed, "expert", split_axis=0, concat_axis=0, tiled=True),
        gate_local,
        up_local,
        down_local,
    )
    returned = lax.all_to_all(partial_out, "expert", split_axis=0, concat_axis=0, tiled=True)
    summed = jnp.sum(
        returned.reshape(experts, slices, steps_here, capacity, returned.shape[-1]), axis=1
    )
    combined = jnp.einsum("srec,escd->srd", weights, summed, precision=lax.Precision.HIGHEST)
    return lax.psum(combined, "head").astype(jnp.bfloat16)


def shards(
    query_rows,
    key_rows,
    value_rows,
    forget,
    head_state,
    out_weight,
    route_ids,
    route_gate,
    gate_weight,
    up_weight,
    down_weight,
):
    steps_total, row_count, head_width = query_rows.shape
    head_count = forget.shape[0]
    head_size = head_width // head_count
    split_shape = (steps_total, row_count, head_count, head_size)
    query_float = query_rows.astype(jnp.float32).reshape(split_shape)
    key_split = key_rows.reshape(split_shape)
    value_split = value_rows.reshape(split_shape)
    decay_rate = jnp.exp(-forget)[None, :, None, None]
    carried = head_state.astype(jnp.float32)
    gate_local = gate_weight[0]
    up_local = up_weight[0]
    down_local = down_weight[0]
    mixed_rows = []
    outputs = []
    for step_index in range(steps_total):
        carried = decay_rate * carried + jnp.einsum(
            "rhi,rhj->rhij",
            key_split[step_index],
            value_split[step_index],
            preferred_element_type=jnp.float32,
        )
        attended = jnp.einsum(
            "rhi,rhij->rhj", query_float[step_index], carried, precision=lax.Precision.HIGHEST
        )
        attended = attended.astype(jnp.bfloat16).reshape(row_count, head_width)
        projected = jnp.dot(
            lax.all_gather(attended, "expert", axis=0, tiled=True),
            out_weight,
            preferred_element_type=jnp.float32,
        )
        projected = lax.psum(projected, "head").astype(jnp.bfloat16)
        mixed_step = lax.all_to_all(projected, "expert", split_axis=0, concat_axis=1, tiled=True)
        mixed_rows.append(mixed_step)
        outputs.append(
            mixture(
                mixed_step[None],
                route_ids[step_index : step_index + 1],
                route_gate[step_index : step_index + 1],
                gate_local,
                up_local,
                down_local,
            )
        )
    mixed_all = jnp.stack(mixed_rows)
    return (mixed_all, jnp.concatenate(outputs, axis=0), carried.astype(jnp.bfloat16))


def solution(mesh):
    return jax.shard_map(
        shards,
        mesh=mesh,
        in_specs=(
            P(None, "expert", "head"),
            P(None, "expert", "head"),
            P(None, "expert", "head"),
            P("head"),
            P("expert", "head", None, None),
            P("head", "expert"),
            P(None, "expert", None),
            P(None, "expert", None),
            P("expert", None, "head"),
            P("expert", None, "head"),
            P("expert", "head", None),
        ),
        out_specs=(
            P(None, "expert", None),
            P(None, "expert", None),
            P("expert", "head", None, None),
        ),
        check_vma=False,
    )
```

profile of v0, /device:TPU:2, one launch (start us, length us, event | category | flops | bytes accessed | tf_op | source)
XLA Modules:
  0.0 898.5 jit_solution(7126500913705491614)
XLA Ops:
  5.1 4.2 fusion.31
  11.2 58.5 %all-gather.3 = bf16[64,4,1024]{2,1,0:T(4,128)(2,1)} all-gather(bf16[1,4,1024]{2,1,0:T(4,128)(2,1)} %reshape.592), channel_id=1, replica_groups=mesh['head'=4,'expert'=64] {'expert'}, dimensions={0}, use_global_device_ids=true | all-gather | bytes 532480 | tf_op jit(solution)/shard_map/all_gather | solution.py:91
  69.7 2.0 reshape.593
  71.6 2.0 fusion.101
  75.0 3.6 fusion.95
  80.5 53.2 %all-gather.2 = bf16[64,4,1024]{2,1,0:T(4,128)(2,1)} all-gather(bf16[1,4,1024]{2,1,0:T(4,128)(2,1)} %reshape.590), channel_id=1, replica_groups=mesh['head'=4,'expert'=64] {'expert'}, dimensions={0}, use_global_device_ids=true | all-gather | bytes 532480 | tf_op jit(solution)/shard_map/all_gather | solution.py:91
  133.7 2.0 reshape.591
  135.6 2.0 fusion.100
  139.0 3.1 fusion.29
  144.0 53.3 %all-gather.1 = bf16[64,4,1024]{2,1,0:T(4,128)(2,1)} all-gather(bf16[1,4,1024]{2,1,0:T(4,128)(2,1)} %reshape.588), channel_id=1, replica_groups=mesh['head'=4,'expert'=64] {'expert'}, dimensions={0}, use_global_device_ids=true | all-gather | bytes 532480 | tf_op jit(solution)/shard_map/all_gather | solution.py:91
  197.3 2.0 reshape.589
  199.2 2.0 fusion.99
  202.6 2.6 fusion.28
  207.1 53.2 %all-gather = bf16[64,4,1024]{2,1,0:T(4,128)(2,1)} all-gather(bf16[1,4,1024]{2,1,0:T(4,128)(2,1)} %reshape.586), channel_id=1, replica_groups=mesh['head'=4,'expert'=64] {'expert'}, dimensions={0}, use_global_device_ids=true | all-gather | bytes 532480 | tf_op jit(solution)/shard_map/all_gather | solution.py:91
  260.3 2.0 reshape.587
  262.2 2.0 fusion.98
  264.3 19.8 %all-reduce.4 = (bf16[256,96]{0,1:T(8,128)(2,1)}, bf16[256,96]{0,1:T(8,128)(2,1)}, bf16[256,96]{0,1:T(8,128)(2,1)}, bf16[256,96]{0,1:T(8,128)(2,1)}) all-reduce(f32[256,96]{0,1:T(8,128)} %fusion.101, f32[256,96]{0,1:T(8,128)} %fusion.100, f32[256,96]{0,1:T(8,128)} %fusion.99, ...), channel_id=1, replica_groups=mesh['head'=4,'expert'=64] {'head'}, use_global_device_ids=true, to_apply=%region_3.4 | all-reduce | flops 98304 | bytes 589824 | tf_op jit(solution)/shard_map/psum | solution.py:95
  285.6 6.7 all-to-all-start.3
  301.9 10.4 %all-to-all-start.2 = ((bf16[64,4,96]{2,1,0:T(4,128)(2,1)}), bf16[64,4,96]{2,1,0:T(4,128)(2,1)}, u32[]{:S(2)}, u32[]{:S(2)}) async-start(bf16[64,4,96]{2,1,0:T(4,128)(2,1)} %bitcast.202), calls=%async_computation.2 | async-start | bytes 131072 | tf_op jit(solution)/shard_map/all_to_all | solution.py:96
  317.9 3.9 all-to-all-done.2
  321.8 6.6 all-to-all-start.1
  332.8 5.2 all-to-all-done.1
  338.0 5.5 all-to-all-start
  345.8 7.4 all-to-all-done
  353.2 3.1 broadcast_in_dim.11
  356.3 5.5 all-to-all-start.10
  374.9 26.2 %all-to-all-done.10 = bf16[64,2,6144]{2,1,0:T(2,128)(2,1)} async-done(((bf16[64,2,6144]{2,1,0:T(2,128)(2,1)}), bf16[64,2,6144]{2,1,0:T(2,128)(2,1)}, u32[]{:S(2)}, u32[]{:S(2)}) %all-to-all-start.10) | async-done | bytes 1572896 | tf_op jit(solution)/shard_map/all_to_all | solution.py:39
  401.2 3.1 broadcast_in_dim.10
  404.3 6.6 all-to-all-start.8
  424.1 26.2 %all-to-all-done.8 = bf16[64,2,6144]{2,1,0:T(2,128)(2,1)} async-done(((bf16[64,2,6144]{2,1,0:T(2,128)(2,1)}), bf16[64,2,6144]{2,1,0:T(2,128)(2,1)}, u32[]{:S(2)}, u32[]{:S(2)}) %all-to-all-start.8) | async-done | bytes 1572896 | tf_op jit(solution)/shard_map/all_to_all | solution.py:39
  450.3 3.2 broadcast_in_dim.9
  453.5 6.6 all-to-all-start.6
  473.3 26.2 %all-to-all-done.6 = bf16[64,2,6144]{2,1,0:T(2,128)(2,1)} async-done(((bf16[64,2,6144]{2,1,0:T(2,128)(2,1)}), bf16[64,2,6144]{2,1,0:T(2,128)(2,1)}, u32[]{:S(2)}, u32[]{:S(2)}) %all-to-all-start.6) | async-done | bytes 1572896 | tf_op jit(solution)/shard_map/all_to_all | solution.py:39
  499.5 3.1 broadcast_in_dim.8
  502.6 6.9 all-to-all-start.4
  509.5 4.5 reshape.576
  514.1 3.7 fusion.20
  524.9 4.1 copy.232
  529.0 19.9 %all-to-all-done.4 = bf16[64,2,6144]{2,1,0:T(2,128)(2,1)} async-done(((bf16[64,2,6144]{2,1,0:T(2,128)(2,1)}), bf16[64,2,6144]{2,1,0:T(2,128)(2,1)}, u32[]{:S(2)}, u32[]{:S(2)}) %all-to-all-start.4) | async-done | bytes 1572896 | tf_op jit(solution)/shard_map/all_to_all | solution.py:39
  548.9 6.9 all-to-all-start.11
  555.8 4.5 reshape.571
  560.3 3.7 fusion.22
  569.3 1.9 fusion.6
  571.1 4.1 copy.224
  575.3 53.6 %all-to-all-done.11 = f32[64,2,6144]{2,1,0:T(2,128)} async-done(((f32[64,2,6144]{2,1,0:T(2,128)}), f32[64,2,6144]{2,1,0:T(2,128)}, u32[]{:S(2)}, u32[]{:S(2)}) %all-to-all-start.11) | async-done | bytes 3145760 | tf_op jit(solution)/shard_map/all_to_all | solution.py:44
  628.9 7.1 all-to-all-start.9
  636.0 4.5 reshape.566
  640.5 3.7 fusion.24
  649.4 1.9 fusion.8
  651.3 4.1 copy.216
  655.4 53.7 %all-to-all-done.9 = f32[64,2,6144]{2,1,0:T(2,128)} async-done(((f32[64,2,6144]{2,1,0:T(2,128)}), f32[64,2,6144]{2,1,0:T(2,128)}, u32[]{:S(2)}, u32[]{:S(2)}) %all-to-all-start.9) | async-done | bytes 3145760 | tf_op jit(solution)/shard_map/all_to_all | solution.py:44
  709.1 6.8 all-to-all-start.7
  715.9 4.5 reshape.561
  720.4 3.7 fusion.26
  731.2 4.1 copy.208
  735.3 53.7 %all-to-all-done.7 = f32[64,2,6144]{2,1,0:T(2,128)} async-done(((f32[64,2,6144]{2,1,0:T(2,128)}), f32[64,2,6144]{2,1,0:T(2,128)}, u32[]{:S(2)}, u32[]{:S(2)}) %all-to-all-start.7) | async-done | bytes 3145760 | tf_op jit(solution)/shard_map/all_to_all | solution.py:44
  789.0 6.6 all-to-all-start.5
  799.1 5.0 fusion.30
  812.2 3.6 bitcast_reduce_fusion
  817.4 3.6 bitcast_reduce_fusion.1
  822.6 3.6 bitcast_reduce_fusion.2
  827.7 41.0 %all-to-all-done.5 = f32[64,2,6144]{2,1,0:T(2,128)} async-done(((f32[64,2,6144]{2,1,0:T(2,128)}), f32[64,2,6144]{2,1,0:T(2,128)}, u32[]{:S(2)}, u32[]{:S(2)}) %all-to-all-start.5) | async-done | bytes 3145760 | tf_op jit(solution)/shard_map/all_to_all | solution.py:44
  868.8 3.6 bitcast_reduce_fusion.3
  873.9 22.6 %all-reduce.5 = (bf16[1,4,6144]{2,1,0:T(4,128)(2,1)}, bf16[1,4,6144]{2,1,0:T(4,128)(2,1)}, bf16[1,4,6144]{2,1,0:T(4,128)(2,1)}, bf16[1,4,6144]{2,1,0:T(4,128)(2,1)}) all-reduce(f32[1,4,6144]{2,1,0:T(4,128)} %convolution_bitcast_fusion, f32[1,4,6144]{2,1,0:T(4,128)} %convolution_bitcast_fusion.1, ...), channel_id=1, replica_groups=mesh['head'=4,'expert'=64] {'head'}, use_global_device_ids=true, to_apply=%region_23.24 | all-reduce | flops 98304 | bytes 589824 | tf_op jit(solution)/shard_map/psum | solution.py:49
  (155 shorter events, 122.8 us)
Async XLA Ops:
  0.6 522.4 %copy-start = (bf16[1,288,6144]{2,1,0:T(8,128)(2,1)S(1)}, bf16[1,288,6144]{2,1,0:T(8,128)(2,1)}, u32[]{:S(2)}) copy-start(bf16[1,288,6144]{2,1,0:T(8,128)(2,1)} %param.21) | copy-start | bytes 10616836
  4.9 4.3 copy-start.26
  5.0 4.3 copy-start.9
  5.0 4.3 copy-start.10
  5.0 4.3 copy-start.11
  5.0 4.3 copy-start.12
  5.0 4.3 copy-start.13
  5.0 4.3 copy-start.14
  5.0 4.3 copy-start.15
  285.6 16.3 %all-to-all-start.3 = ((bf16[64,4,96]{2,1,0:T(4,128)(2,1)}), bf16[64,4,96]{2,1,0:T(4,128)(2,1)}, u32[]{:S(2)}, u32[]{:S(2)}) async-start(bf16[64,4,96]{2,1,0:T(4,128)(2,1)} %bitcast.201), calls=%async_computation.3 | async-start | bytes 131072 | tf_op jit(solution)/shard_map/all_to_all | solution.py:96
  301.9 19.9 %all-to-all-start.2 = ((bf16[64,4,96]{2,1,0:T(4,128)(2,1)}), bf16[64,4,96]{2,1,0:T(4,128)(2,1)}, u32[]{:S(2)}, u32[]{:S(2)}) async-start(bf16[64,4,96]{2,1,0:T(4,128)(2,1)} %bitcast.202), calls=%async_computation.2 | async-start | bytes 131072 | tf_op jit(solution)/shard_map/all_to_all | solution.py:96
  321.8 16.1 %all-to-all-start.1 = ((bf16[64,4,96]{2,1,0:T(4,128)(2,1)}), bf16[64,4,96]{2,1,0:T(4,128)(2,1)}, u32[]{:S(2)}, u32[]{:S(2)}) async-start(bf16[64,4,96]{2,1,0:T(4,128)(2,1)} %bitcast.203), calls=%async_computation.1 | async-start | bytes 131072 | tf_op jit(solution)/shard_map/all_to_all | solution.py:96
  338.0 15.2 %all-to-all-start = ((bf16[64,4,96]{2,1,0:T(4,128)(2,1)}), bf16[64,4,96]{2,1,0:T(4,128)(2,1)}, u32[]{:S(2)}, u32[]{:S(2)}) async-start(bf16[64,4,96]{2,1,0:T(4,128)(2,1)} %bitcast.200), calls=%async_computation | async-start | bytes 131072 | tf_op jit(solution)/shard_map/all_to_all | solution.py:96
  356.3 44.9 %all-to-all-start.10 = ((bf16[64,2,6144]{2,1,0:T(2,128)(2,1)}), bf16[64,2,6144]{2,1,0:T(2,128)(2,1)}, u32[]{:S(2)}, u32[]{:S(2)}) async-start(bf16[64,2,6144]{2,1,0:T(2,128)(2,1)} %bitcast.197), calls=%async_computation.10 | async-start | bytes 3145728 | tf_op jit(solution)/shard_map/all_to_all | solution.py:39
  367.7 1.9 copy-start.19
  368.4 0.6 copy-start.16
  404.3 46.0 %all-to-all-start.8 = ((bf16[64,2,6144]{2,1,0:T(2,128)(2,1)}), bf16[64,2,6144]{2,1,0:T(2,128)(2,1)}, u32[]{:S(2)}, u32[]{:S(2)}) async-start(bf16[64,2,6144]{2,1,0:T(2,128)(2,1)} %bitcast.198), calls=%async_computation.8 | async-start | bytes 3145728 | tf_op jit(solution)/shard_map/all_to_all | solution.py:39
  416.9 1.9 copy-start.20
  417.5 0.6 copy-start.17
  453.5 46.0 %all-to-all-start.6 = ((bf16[64,2,6144]{2,1,0:T(2,128)(2,1)}), bf16[64,2,6144]{2,1,0:T(2,128)(2,1)}, u32[]{:S(2)}, u32[]{:S(2)}) async-start(bf16[64,2,6144]{2,1,0:T(2,128)(2,1)} %bitcast.196), calls=%async_computation.6 | async-start | bytes 3145728 | tf_op jit(solution)/shard_map/all_to_all | solution.py:39
  466.0 2.0 copy-start.21
  466.8 0.6 copy-start.18
  502.6 46.2 %all-to-all-start.4 = ((bf16[64,2,6144]{2,1,0:T(2,128)(2,1)}), bf16[64,2,6144]{2,1,0:T(2,128)(2,1)}, u32[]{:S(2)}, u32[]{:S(2)}) async-start(bf16[64,2,6144]{2,1,0:T(2,128)(2,1)} %bitcast.199), calls=%async_computation.4 | async-start | bytes 3145728 | tf_op jit(solution)/shard_map/all_to_all | solution.py:39
  514.1 3.7 copy-start.1
  514.1 4.0 copy-start.5
  548.9 80.0 %all-to-all-start.11 = ((f32[64,2,6144]{2,1,0:T(2,128)}), f32[64,2,6144]{2,1,0:T(2,128)}, u32[]{:S(2)}, u32[]{:S(2)}) async-start(f32[64,2,6144]{2,1,0:T(2,128)} %copy.232), calls=%async_computation.11 | async-start | bytes 6291456 | tf_op jit(solution)/shard_map/all_to_all | solution.py:44
  560.3 3.7 copy-start.2
  560.3 4.0 copy-start.6
  628.9 80.2 %all-to-all-start.9 = ((f32[64,2,6144]{2,1,0:T(2,128)}), f32[64,2,6144]{2,1,0:T(2,128)}, u32[]{:S(2)}, u32[]{:S(2)}) async-start(f32[64,2,6144]{2,1,0:T(2,128)} %copy.224), calls=%async_computation.9 | async-start | bytes 6291456 | tf_op jit(solution)/shard_map/all_to_all | solution.py:44
  640.5 3.7 copy-start.3
  640.5 4.0 copy-start.7
  709.1 79.9 %all-to-all-start.7 = ((f32[64,2,6144]{2,1,0:T(2,128)}), f32[64,2,6144]{2,1,0:T(2,128)}, u32[]{:S(2)}, u32[]{:S(2)}) async-start(f32[64,2,6144]{2,1,0:T(2,128)} %copy.216), calls=%async_computation.7 | async-start | bytes 6291456 | tf_op jit(solution)/shard_map/all_to_all | solution.py:44
  720.4 3.7 copy-start.4
  720.4 4.0 copy-start.8
  789.0 79.8 %all-to-all-start.5 = ((f32[64,2,6144]{2,1,0:T(2,128)}), f32[64,2,6144]{2,1,0:T(2,128)}, u32[]{:S(2)}, u32[]{:S(2)}) async-start(f32[64,2,6144]{2,1,0:T(2,128)} %copy.208), calls=%async_computation.5 | async-start | bytes 6291456 | tf_op jit(solution)/shard_map/all_to_all | solution.py:44
  810.5 5.3 copy-start.25
  817.4 3.6 copy-start.23
  822.6 3.6 copy-start.24
  827.7 44.6 %copy-start.22 = (f32[4,16,2]{1,0,2:T(4,128)S(1)}, f32[4,16,2]{1,0,2:T(4,128)}, u32[]{:S(2)}) copy-start(f32[4,16,2]{1,0,2:T(4,128)} %get-tuple-element.43) | copy-start | bytes 1540
where the time goes:
time: 911 us; the launch traced here: 899 us
  waiting for transfers between devices  317 us (35%)
  blocking collectives  261 us (29%)
  local copies, waits for them, and re-layouts  125 us (14%)
  starting transfers between devices  82.3 us (9%)
  matrix products  61.3 us (7%)
  other arithmetic  50.5 us (6%)
    all_gather x4, blocking collectives, shards(): lax.all_gather(attended, 'expert', axis=0, tiled=True)  218 us
    all_to_all x4, waiting for transfers between devices, mixture(): lax.all_to_all(partial_out, 'expert', split_axis=0, concat_axis=0, tiled=...  202 us
    all_to_all x4, waiting for transfers between devices, mixture(): lax.all_to_all(packed, 'expert', split_axis=0, concat_axis=0, tiled=True)  98.6 us
    all_to_all x4, starting transfers between devices, shards(): lax.all_to_all(projected, 'expert', split_axis=0, concat_axis=1, tiled=True)  29.2 us
    all_to_all x4, starting transfers between devices, mixture(): lax.all_to_all(partial_out, 'expert', split_axis=0, concat_axis=0, tiled=...  27.4 us
    all_to_all x4, starting transfers between devices, mixture(): lax.all_to_all(packed, 'expert', split_axis=0, concat_axis=0, tiled=True)  25.7 us
    dot_general x8, local copies, waits for them, and re-layouts, expert_ffn(): result = jnp.dot(hidden, down_local, preferred_element_type=jnp.float32)  22.7 us
    psum x1, blocking collectives, mixture(): return lax.psum(combined, 'head').astype(jnp.bfloat16)  22.6 us
  transfers between devices with their start and end apart: 12, of which 12 were waited for; matrix products, arithmetic and copies ran while one was open for 19% of the time, Pallas kernels for 0%

commit v1 on v0

v1 whole, which is shorter than its diff:
```python
import jax
import jax.numpy as jnp
from jax import lax
from jax.sharding import Mesh, PartitionSpec as P

BLOCKS = ("y", "zp")
EXPERT = ("y", "zp", "zl", "core")
BF16 = jnp.bfloat16
F32 = jnp.float32
EXACT = lax.Precision.HIGHEST


def shift(array, axis, distance):
    size = lax.axis_size(axis)
    pairs = [(i, (i + distance) % size) for i in range(size)]
    return lax.ppermute(array, axis, pairs)


def spread(array, axis):
    size = lax.axis_size(axis)
    copies = jnp.broadcast_to(array[None], (size,) + array.shape)
    return lax.all_to_all(copies, axis, split_axis=0, concat_axis=0, tiled=True)


def attention(query_rows, key_rows, value_rows, forget, head_state):
    steps, rows, width = query_rows.shape
    heads = forget.shape[0]
    size = width // heads
    shape = (steps, rows, heads, size)
    query, key, value = (a.reshape(shape) for a in (query_rows, key_rows, value_rows))
    times = jnp.arange(steps, dtype=F32)
    power = jnp.exp(-forget[None, :] * jnp.arange(steps + 1, dtype=F32)[:, None])
    lag = times[:, None] - times[None, :]
    causal = jnp.where(
        lag[..., None] >= 0, jnp.exp(-forget * jnp.maximum(lag, 0.0)[..., None]), 0.0
    )
    from_state = jnp.einsum("trhi,rhij->trhj", query, head_state, preferred_element_type=F32)
    scores = jnp.einsum("trhi,srhi->tsrh", query, key, preferred_element_type=F32)
    scores = scores * causal[:, :, None, :]
    value_float = value.astype(F32)
    from_steps = sum(scores[:, s, :, :, None] * value_float[s][None] for s in range(steps))
    attended = power[1:, None, :, None] * from_state + from_steps
    attended = attended.astype(BF16).reshape(steps * rows, width)
    scaled_key = key.astype(F32) * power[steps - 1 :: -1][:steps, None, :, None]
    state = power[steps][None, :, None, None] * head_state.astype(F32) + jnp.einsum(
        "trhi,trhj->rhij", scaled_key, value_float, precision=EXACT
    )
    return attended, state.astype(BF16)


def place(ids, experts, capacity):
    rows = ids.shape[-2]
    flat = ids.reshape(ids.shape[:-2] + (rows * 2,))
    onehot = (flat[..., None] == jnp.arange(experts, dtype=jnp.int32)).astype(jnp.int32)
    ranked = jnp.cumsum(onehot, axis=-2) - 1
    landed = onehot[..., None] * (
        ranked[..., None] == jnp.arange(capacity, dtype=jnp.int32)
    ).astype(jnp.int32)
    landed = jnp.moveaxis(landed, (-2, -1), (0, 1)).astype(F32)
    return landed.reshape(landed.shape[:-1] + (rows, 2))


def gather_block(own):
    across = shift(own, "zl", 1)
    left, right, far = shift(own, "head", 1), shift(own, "head", -1), shift(own, "head", 2)
    across_left, across_right = shift(across, "head", 1), shift(across, "head", -1)
    across_far = shift(far, "zl", 1)
    return [own, left, right, far, across, across_left, across_right, across_far]


def scatter_block(parts):
    own, left, right, far, across, across_left, across_right, across_far = parts

    def add(*terms):
        return sum(t.astype(F32) for t in terms)

    from_right = shift(across_left, "head", -1)
    from_left = shift(across_right, "head", 1)
    from_far = shift(across_far, "zl", 1)
    got_left = shift(right, "head", 1)
    got_right = shift(left, "head", -1)
    got_far = shift(add(far, from_far).astype(BF16), "head", 2)
    got_across = shift(add(across, from_right, from_left).astype(BF16), "zl", 1)
    return add(own, got_left, got_right, got_far, got_across).astype(BF16)


def expert_ffn(rows, weights):
    total = 0.0
    for gate, up, down in weights:
        gated = jnp.dot(rows, gate, preferred_element_type=F32)
        lifted = jnp.dot(rows, up, preferred_element_type=F32)
        hidden = (jax.nn.silu(gated) * lifted).astype(BF16)
        total = total + jnp.dot(hidden, down, preferred_element_type=F32)
    return total.astype(BF16)


def shards(
    query_rows,
    key_rows,
    value_rows,
    forget,
    head_state,
    out_weight,
    route_ids,
    route_gate,
    gate_weight,
    up_weight,
    down_weight,
):
    steps, rows, _ = query_rows.shape
    blocks = lax.axis_size("y") * lax.axis_size("zp")
    experts = blocks
    capacity = rows // 2
    head = lax.axis_index("head")

    own_weights = (gate_weight[0], up_weight[0], down_weight[0])
    other_weights = tuple(shift(w, "core", 1) for w in own_weights)
    columns = lax.all_gather(out_weight, ("zl", "core"), axis=1, tiled=True)
    width = columns.shape[1]
    features = width * blocks

    own_ids = lax.dynamic_index_in_dim(route_ids, head, 0, keepdims=False)
    own_gate = lax.dynamic_index_in_dim(route_gate, head, 0, keepdims=False)
    peer_ids = lax.all_gather(own_ids, BLOCKS, axis=0, tiled=False)

    attended, state_out = attention(query_rows, key_rows, value_rows, forget, head_state)

    peers = spread(attended, BLOCKS).reshape(blocks, steps, rows, -1)
    peers = jnp.transpose(peers, (1, 2, 0, 3)).reshape(steps * rows * blocks, -1)
    partial = jnp.dot(peers, columns, preferred_element_type=F32)
    partial = partial.reshape(steps, rows * blocks, width)
    projected = lax.dynamic_index_in_dim(partial, head, 0, keepdims=False)
    for distance in range(1, steps):
        there = lax.rem(head + distance, steps)
        projected = projected + shift(
            lax.dynamic_index_in_dim(partial, there, 0, keepdims=False), "head", distance
        )
    projected = projected.astype(BF16).reshape(rows, blocks, width)

    returned = lax.all_to_all(
        jnp.transpose(projected, (1, 0, 2)), BLOCKS, split_axis=0, concat_axis=0, tiled=True
    )
    mixed = spread(jnp.transpose(returned, (1, 0, 2)).reshape(rows, features), "head")

    placed = jnp.sum(place(peer_ids, experts, capacity), axis=-1)
    packed = sum(
        placed[:, :, :, r, None] * projected[r].astype(F32)[None, None] for r in range(rows)
    ).astype(BF16)
    packed = lax.all_to_all(packed, BLOCKS, split_axis=0, concat_axis=0, tiled=True)
    piece = jnp.transpose(packed, (1, 2, 0, 3)).reshape(capacity * blocks, features)

    pieces = gather_block(piece)
    count = len(pieces)
    result = expert_ffn(jnp.concatenate(pieces, axis=0), (own_weights, other_weights))
    result = scatter_block(list(result.reshape(count, capacity * blocks, features)))

    result = jnp.transpose(result.reshape(capacity, blocks, features), (1, 0, 2))
    result = lax.all_to_all(result, BLOCKS, split_axis=0, concat_axis=0, tiled=True)
    weights = jnp.sum(place(own_ids, experts, capacity) * own_gate, axis=-1)
    combined = jnp.einsum(
        "esr,esd->rd", weights, result.astype(F32), precision=EXACT
    ).astype(BF16)
    moe_out = spread(combined, "head")
    return mixed, moe_out, state_out


def solution(mesh):
    shape = dict(mesh.shape)
    heads, peers = shape["head"], shape["expert"]
    split = (4, peers // 16, 2, 2)
    fine = Mesh(mesh.devices.reshape((heads,) + split), ("head",) + EXPERT)
    return jax.shard_map(
        shards,
        mesh=fine,
        in_specs=(
            P(None, EXPERT, "head"),
            P(None, EXPERT, "head"),
            P(None, EXPERT, "head"),
            P("head"),
            P(EXPERT, "head", None, None),
            P("head", EXPERT),
            P(None, EXPERT, None),
            P(None, EXPERT, None),
            P(EXPERT, None, "head"),
            P(EXPERT, None, "head"),
            P(EXPERT, "head", None),
        ),
        out_specs=(
            P(None, EXPERT, None),
            P(None, EXPERT, None),
            P(EXPERT, "head", None, None),
        ),
        check_vma=False,
    )
```

time: 911 us -> 251 us (0.28); the launches traced: 899 us -> 250 us
  waiting for transfers between devices: 317 us -> 83.1 us
  blocking collectives: 261 us -> 57.4 us
  local copies, waits for them, and re-layouts: 125 us -> 12.4 us
  other arithmetic: 50.5 us -> 5.57 us
  matrix products: 61.3 us -> 31.7 us
  starting transfers between devices: 82.3 us -> 59 us
    all_to_all x12 -> x6, waiting for transfers between devices: 317 us -> 41.8 us  [the longest x1 14.4 us: shards(): lax.all_to_all(packed, BLOCKS, split_axis=0, concat_axis=0, tiled=True)]
    all_gather x4 -> x2, blocking collectives: 218 us -> 57.4 us  [the longest x1 48 us: shards(): peer_ids = lax.all_gather(own_ids, BLOCKS, axis=0, tiled=False)]
    all_to_all x12 -> x6, starting transfers between devices: 82.3 us -> 35.4 us  [the longest x3 21.6 us: spread(): return lax.all_to_all(copies, axis, split_axis=0, concat_axis=0, tiled=True)]
    psum x2 -> x0, blocking collectives: 42.4 us -> none  [the longest x1 22.6 us: mixture(): return lax.psum(combined, 'head').astype(jnp.bfloat16)]
    ppermute x0 -> x20, waiting for transfers between devices: none -> 41.3 us  [shift(): return lax.ppermute(array, axis, pairs)]
    dot_general x28 -> x9, matrix products: 61.3 us -> 31.7 us  [the longest x2 21.7 us: expert_ffn(): total = total + jnp.dot(hidden, down, preferred_element_type=F32)]
    ppermute x0 -> x20, starting transfers between devices: none -> 23.6 us  [shift(): return lax.ppermute(array, axis, pairs)]
    dot_general x8 -> x0, local copies, waits for them, and re-layouts: 22.7 us -> none  [expert_ffn(): result = jnp.dot(hidden, down_local, preferred_element_type=jnp.float32)]
  transfers between devices with their start and end apart: 12 -> 26, of which waited for: 12 -> 18; matrix products, arithmetic and copies ran while one was open for 19% -> 10% of each run, Pallas kernels for 0% -> 0%
where the time goes in v1:
time: 251 us; the launch traced here: 250 us
  waiting for transfers between devices  83.1 us (33%)
  starting transfers between devices  59 us (24%)
  blocking collectives  57.4 us (23%)
  matrix products  31.7 us (13%)
  local copies, waits for them, and re-layouts  12.4 us (5%)
  other arithmetic  5.57 us (2%)
    all_gather x1, blocking collectives, shards(): peer_ids = lax.all_gather(own_ids, BLOCKS, axis=0, tiled=False)  48 us
    ppermute x20, waiting for transfers between devices, shift(): return lax.ppermute(array, axis, pairs)  41.3 us
    ppermute x20, starting transfers between devices, shift(): return lax.ppermute(array, axis, pairs)  23.6 us
    dot_general x2, matrix products, expert_ffn(): total = total + jnp.dot(hidden, down, preferred_element_type=F32)  21.7 us
    all_to_all x3, starting transfers between devices, spread(): return lax.all_to_all(copies, axis, split_axis=0, concat_axis=0, tiled=True)  21.6 us
    all_to_all x1, waiting for transfers between devices, shards(): lax.all_to_all(packed, BLOCKS, split_axis=0, concat_axis=0, tiled=True)  14.4 us
    all_to_all x1, waiting for transfers between devices, shards(): lax.all_to_all(result, BLOCKS, split_axis=0, concat_axis=0, tiled=True)  12.8 us
    all_gather x1, blocking collectives, shards(): columns = lax.all_gather(out_weight, ('zl', 'core'), axis=1, tiled=True)  9.41 us
  transfers between devices with their start and end apart: 26, of which 18 were waited for; matrix products, arithmetic and copies ran while one was open for 10% of the time, Pallas kernels for 0%

profile of v1, /device:TPU:2, one launch (start us, length us, event | category | flops | bytes accessed | tf_op | source)
XLA Modules:
  0.0 250.1 jit_solution(9803183465058561077)
XLA Ops:
  0.7 0.8 reshape.195
  1.5 0.8 reshape.196
  2.3 0.7 neg.12
  3.3 0.8 reshape.197
  4.2 1.6 fusion.5
  5.9 0.9 broadcast_in_dim.25
  6.7 11.2 %all-to-all-start = ((bf16[16,16,1024]{2,1,0:T(8,128)(2,1)}), bf16[16,16,1024]{2,1,0:T(8,128)(2,1)S(1)}, u32[]{:S(2)}, u32[]{:S(2)}) async-start(bf16[16,16,1024]{2,1,0:T(8,128)(2,1)} %broadcast_in_dim.25), calls=%async_computation | async-start | bytes 1048576 | tf_op jit(solution)/shard_map/all_to_all | solution.py:22
  18.0 48.0 %all_gather.8 = s32[16,4,2]{1,2,0:T(2,128)S(1)} all-gather(s32[1,4,2]{1,2,0:T(2,128)S(1)} %constant_dynamic-slice_fusion.1), channel_id=1, replica_groups=mesh['head'=4,'y'=4,'zp'=4,'zl'=2,'core'=2] {'y','zp'}, dimensions={0}, use_global_device_ids=true | all-gather | bytes 544 | tf_op jit(solution)/shard_map/all_gather | solution.py:124
  66.1 9.4 %all_gather.7 = bf16[1024,384]{0,1:T(8,128)(2,1)S(1)} all-gather(bf16[1024,96]{0,1:T(8,128)(2,1)S(1)} %copy-done.2), channel_id=1, replica_groups=mesh['head'=4,'y'=4,'zp'=4,'zl'=2,'core'=2] {'zl','core'}, dimensions={1}, use_global_device_ids=true | all-gather | bytes 983040 | tf_op jit(solution)/shard_map/all_gather | solution.py:118
  75.8 0.5 fusion.6
  76.3 1.6 collective-permute-start
  77.9 1.1 collective-permute-start.1
  79.0 2.2 collective-permute-start.2
  81.4 3.6 %collective-permute-done.1 = f32[64,384]{1,0:T(8,128)S(1)} collective-permute-done((f32[64,384]{1,0:T(8,128)S(1)}, f32[64,384]{1,0:T(8,128)S(1)}, u32[]{:S(2)}, u32[]{:S(2)}) %collective-permute-start.1) | collective-permute-done | bytes 98336 | tf_op jit(solution)/shard_map/ppermute | solution.py:16
  85.1 0.5 collective-permute-done.2
  85.6 1.1 add_convert_fusion.4
  86.7 3.6 %all-to-all-start.3 = ((bf16[16,2,16,384]{3,2,1,0:T(8,128)(2,1)}), bf16[16,2,16,384]{3,2,1,0:T(8,128)(2,1)S(1)}, u32[]{:S(2)}, u32[]{:S(2)}) async-start(bf16[16,2,16,384]{3,2,1,0:T(8,128)(2,1)} %add_convert_fusion.4), calls=%async_computation.3 | async-start | bytes 786432 | tf_op jit(solution)/shard_map/all_to_all | solution.py:149
  90.4 0.5 collective-permute-start.11
  91.0 14.4 %all-to-all-done.3 = bf16[16,2,16,384]{3,2,1,0:T(8,128)(2,1)S(1)} async-done(((bf16[16,2,16,384]{3,2,1,0:T(8,128)(2,1)}), bf16[16,2,16,384]{3,2,1,0:T(8,128)(2,1)S(1)}, u32[]{:S(2)}, u32[]{:S(2)}) %all-to-all-start.3) | async-done | bytes 393248 | tf_op jit(solution)/shard_map/all_to_all | solution.py:149
  105.6 1.6 collective-permute-start.3
  107.2 0.5 collective-permute-start.4
  107.7 7.5 %collective-permute-done.3 = bf16[32,6144]{1,0:T(8,128)(2,1)S(1)} collective-permute-done((bf16[32,6144]{1,0:T(8,128)(2,1)S(1)}, bf16[32,6144]{1,0:T(8,128)(2,1)S(1)}, u32[]{:S(2)}, u32[]{:S(2)}) %collective-permute-start.3) | collective-permute-done | bytes 393248 | tf_op jit(solution)/shard_map/ppermute | solution.py:16
  115.2 1.3 collective-permute-done.4
  116.5 2.8 %collective-permute-start.5 = (bf16[32,6144]{1,0:T(8,128)(2,1)S(1)}, bf16[32,6144]{1,0:T(8,128)(2,1)S(1)}, u32[]{:S(2)}, u32[]{:S(2)}) collective-permute-start(bf16[32,6144]{1,0:T(8,128)(2,1)S(1)} %bitcast.118), channel_id=1, source_target_pairs={{0,128},{64,192},{128,0},{192,64},{1,129},{65,193},{129,1},{193,65... | collective-permute-start | bytes 1179656 | tf_op jit(solution)/shard_map/ppermute | solution.py:16
  119.3 4.5 %collective-permute-done.6 = bf16[32,6144]{1,0:T(8,128)(2,1)S(1)} collective-permute-done((bf16[32,6144]{1,0:T(8,128)(2,1)S(1)}, bf16[32,6144]{1,0:T(8,128)(2,1)S(1)}, u32[]{:S(2)}, u32[]{:S(2)}) %collective-permute-start.6) | collective-permute-done | bytes 393248 | tf_op jit(solution)/shard_map/ppermute | solution.py:16
  123.8 1.7 collective-permute-start.7
  125.5 1.2 collective-permute-done.5
  126.8 2.5 %collective-permute-start.8 = (bf16[32,6144]{1,0:T(8,128)(2,1)S(1)}, bf16[32,6144]{1,0:T(8,128)(2,1)S(1)}, u32[]{:S(2)}, u32[]{:S(2)}) collective-permute-start(bf16[32,6144]{1,0:T(8,128)(2,1)S(1)} %collective-permute-done.6), channel_id=1, source_target_pairs={{0,192},{64,0},{128,64},{192,128},{1,193},{65,1},{129,65},{193,129... | collective-permute-start | bytes 1179656 | tf_op jit(solution)/shard_map/ppermute | solution.py:16
  129.3 5.0 %collective-permute-done.7 = bf16[32,6144]{1,0:T(8,128)(2,1)S(1)} collective-permute-done((bf16[32,6144]{1,0:T(8,128)(2,1)S(1)}, bf16[32,6144]{1,0:T(8,128)(2,1)S(1)}, u32[]{:S(2)}, u32[]{:S(2)}) %collective-permute-start.7) | collective-permute-done | bytes 393248 | tf_op jit(solution)/shard_map/ppermute | solution.py:16
  134.3 1.5 collective-permute-start.9
  135.9 7.0 %collective-permute-done.9 = bf16[32,6144]{1,0:T(8,128)(2,1)S(1)} collective-permute-done((bf16[32,6144]{1,0:T(8,128)(2,1)S(1)}, bf16[32,6144]{1,0:T(8,128)(2,1)S(1)}, u32[]{:S(2)}, u32[]{:S(2)}) %collective-permute-start.9) | collective-permute-done | bytes 393248 | tf_op jit(solution)/shard_map/ppermute | solution.py:16
  143.0 1.4 fusion.38
  144.4 10.5 %fusion.9 = f32[256,6144]{1,0:T(8,128)} fusion(f32[256,288]{0,1:T(8,128)S(1)} %fusion.38, bf16[1,288,6144]{2,1,0:T(8,128)(2,1)} %param.21, bf16[256,6144]{1,0:T(8,128)(2,1)S(1)} %constant_dynamic-update-slice_fusion, bf16[1,6144,288]{1,2,0:T(8,128)(2,1)} %param.20), kind=kOutput, calls=%fused_computation.22 | convolution fusion | flops 1812381696 | bytes 16809984 | tf_op jit(solution)/shard_map/dot_general | solution.py:93
  154.8 3.1 %fusion.47 = f32[256,288]{0,1:T(8,128)S(1)} fusion(bf16[256,6144]{1,0:T(8,128)(2,1)S(1)} %constant_dynamic-update-slice_fusion, bf16[6144,288]{0,1:T(8,128)(2,1)} %collective-permute-done.10), kind=kOutput, calls=%fused_computation.95 | convolution fusion | flops 905969664 | bytes 6979584 | tf_op jit(solution)/shard_map/dot_general | solution.py:90
  158.0 11.3 %fusion = bf16[256,6144]{1,0:T(8,128)(2,1)} fusion(f32[256,6144]{1,0:T(8,128)} %fusion.9, bf16[288,6144]{1,0:T(8,128)(2,1)} %collective-permute-done.12, f32[256,288]{0,1:T(8,128)S(1)} %fusion.47, bf16[256,6144]{1,0:T(8,128)(2,1)S(1)} %constant_dynamic-update-slice_fusion, bf16[6144,288]{0,1:T(8,128)(2,1)} %collective-permute-done.11), kind=kOutput, calls=%fused_computation.1 | convolution fusion | flops 1815527424 | bytes 19955712 | tf_op jit(solution)/shard_map/dot_general | solution.py:93
  169.2 2.5 %fusion.42 = (bf16[32,6144]{1,0:T(8,128)(2,1)}, bf16[32,6144]{1,0:T(8,128)(2,1)S(1)}, bf16[32,6144]{1,0:T(8,128)(2,1)S(1)}, bf16[32,6144]{1,0:T(8,128)(2,1)}, bf16[32,6144]{1,0:T(8,128)(2,1)}) fusion(bf16[256,6144]{1,0:T(8,128)(2,1)} %fusion), kind=kLoop, calls=%fused_computation.91 | loop fusion | bytes 3932160 | tf_op jit(solution)/shard_map/unstack | solution.py:155
  171.7 1.0 collective-permute-start.15
  172.7 3.0 %collective-permute-start.17 = (bf16[32,6144]{1,0:T(8,128)(2,1)S(1)}, bf16[32,6144]{1,0:T(8,128)(2,1)S(1)}, u32[]{:S(2)}, u32[]{:S(2)}) collective-permute-start(bf16[32,6144]{1,0:T(8,128)(2,1)S(1)} %get-tuple-element.5), channel_id=1, source_target_pairs={{0,192},{64,0},{128,64},{192,128},{1,193},{65,1},{129,65},{193,129... | collective-permute-start | bytes 1179656 | tf_op jit(solution)/shard_map/ppermute | solution.py:16
  175.9 1.5 collective-permute-start.13
  177.4 0.6 collective-permute-start.14
  178.0 1.7 collective-permute-done.15
  179.7 5.6 %collective-permute-done.17 = bf16[32,6144]{1,0:T(8,128)(2,1)S(1)} collective-permute-done((bf16[32,6144]{1,0:T(8,128)(2,1)S(1)}, bf16[32,6144]{1,0:T(8,128)(2,1)S(1)}, u32[]{:S(2)}, u32[]{:S(2)}) %collective-permute-start.17) | collective-permute-done | bytes 393248 | tf_op jit(solution)/shard_map/ppermute | solution.py:16
  185.3 2.5 collective-permute-done.18
  187.8 2.1 add_convert_fusion.3
  189.9 1.0 collective-permute-start.16
  190.8 0.4 collective-permute-start.19
  191.5 0.6 copy.144
  192.1 6.6 %all-to-all-start.1 = ((bf16[16,4,384]{2,1,0:T(4,128)(2,1)}), bf16[16,4,384]{2,1,0:T(4,128)(2,1)S(1)}, u32[]{:S(2)}, u32[]{:S(2)}) async-start(bf16[16,4,384]{2,1,0:T(4,128)(2,1)} %copy.144), calls=%async_computation.1 | async-start | bytes 98304 | tf_op jit(solution)/shard_map/all_to_all | solution.py:140
  198.8 0.6 collective-permute-done.16
  199.4 1.2 add_convert_fusion.1
  200.6 1.2 copy.182
  201.8 7.1 %all-to-all-done.1 = bf16[16,4,384]{2,1,0:T(4,128)(2,1)S(1)} async-done(((bf16[16,4,384]{2,1,0:T(4,128)(2,1)}), bf16[16,4,384]{2,1,0:T(4,128)(2,1)S(1)}, u32[]{:S(2)}, u32[]{:S(2)}) %all-to-all-start.1) | async-done | bytes 49184 | tf_op jit(solution)/shard_map/all_to_all | solution.py:140
  208.9 3.6 %all-to-all-start.4 = ((bf16[16,2,6144]{2,1,0:T(2,128)(2,1)}), bf16[16,2,6144]{2,1,0:T(2,128)(2,1)S(1)}, u32[]{:S(2)}, u32[]{:S(2)}) async-start(bf16[16,2,6144]{2,1,0:T(2,128)(2,1)} %bitcast.111), calls=%async_computation.4 | async-start | bytes 786432 | tf_op jit(solution)/shard_map/all_to_all | solution.py:158
  212.5 0.7 fusion.30
  213.4 12.8 %all-to-all-done.4 = bf16[16,2,6144]{2,1,0:T(2,128)(2,1)S(1)} async-done(((bf16[16,2,6144]{2,1,0:T(2,128)(2,1)}), bf16[16,2,6144]{2,1,0:T(2,128)(2,1)S(1)}, u32[]{:S(2)}, u32[]{:S(2)}) %all-to-all-start.4) | async-done | bytes 393248 | tf_op jit(solution)/shard_map/all_to_all | solution.py:158
  226.1 0.7 broadcast_in_dim.27
  226.8 5.7 %all-to-all-start.2 = ((bf16[4,4,6144]{2,1,0:T(4,128)(2,1)}), bf16[4,4,6144]{2,1,0:T(4,128)(2,1)S(1)}, u32[]{:S(2)}, u32[]{:S(2)}) async-start(bf16[4,4,6144]{2,1,0:T(4,128)(2,1)} %broadcast_in_dim.27), calls=%async_computation.2 | async-start | bytes 393216 | tf_op jit(solution)/shard_map/all_to_all | solution.py:22
  232.9 5.5 %all-to-all-done.2 = bf16[4,4,6144]{2,1,0:T(4,128)(2,1)S(1)} async-done(((bf16[4,4,6144]{2,1,0:T(4,128)(2,1)}), bf16[4,4,6144]{2,1,0:T(4,128)(2,1)S(1)}, u32[]{:S(2)}, u32[]{:S(2)}) %all-to-all-start.2) | async-done | bytes 196640 | tf_op jit(solution)/shard_map/all_to_all | solution.py:22
  238.4 0.7 broadcast_in_dim.28
  239.1 4.8 %all-to-all-start.5 = ((bf16[4,4,6144]{2,1,0:T(4,128)(2,1)}), bf16[4,4,6144]{2,1,0:T(4,128)(2,1)S(1)}, u32[]{:S(2)}, u32[]{:S(2)}) async-start(bf16[4,4,6144]{2,1,0:T(4,128)(2,1)} %broadcast_in_dim.28), calls=%async_computation.5 | async-start | bytes 393216 | tf_op jit(solution)/shard_map/all_to_all | solution.py:22
  243.9 2.9 %add_convert_fusion = bf16[4,8,128,128]{3,2,1,0:T(8,128)(2,1)} fusion(bf16[4,8,128,128]{3,2,1,0:T(8,128)(2,1)S(1)} %copy-done.1, f32[8]{0:T(128)S(1)} %slice_bitcast_fusion.8, bf16[4,4,8,128]{3,2,1,0:T(8,128)(2,1)S(1)} %reshape.197, f32[4,8]{0,1:T(8,128)S(1)} %copy.157, bf16[4,4,8,128]{3,2,1,0:T(8,128)(2,1)S(1)} %copy-done.4), kind=kOutput, calls=%fused_computation.4 | convolution fusion | flops 27295744 | bytes 2162848 | tf_op jit(solution)/shard_map/trhi,trhj->rhij/dot_general | solution.py:45
  246.8 2.0 all-to-all-done.5
  248.8 0.7 copy.193
  249.5 0.7 copy.194
  (74 shorter events, 2.8 us)
Async XLA Ops:
  0.6 17.3 %copy-start = (s32[4,4,2]{1,2,0:T(2,128)S(1)}, s32[4,4,2]{1,2,0:T(2,128)}, u32[]{:S(2)}) copy-start(s32[4,4,2]{1,2,0:T(2,128)} %param.17) | copy-start | bytes 388
  0.6 65.4 %copy-start.2 = (bf16[1024,96]{0,1:T(8,128)(2,1)S(1)}, bf16[1024,96]{0,1:T(8,128)(2,1)}, u32[]{:S(2)}) copy-start(bf16[1024,96]{0,1:T(8,128)(2,1)} %param.16) | copy-start | bytes 589828
  2.3 63.8 %copy-start.3 = (bf16[4,4,8,128]{3,2,1,0:T(8,128)(2,1)}, bf16[4,4,8,128]{3,2,1,0:T(8,128)(2,1)S(1)}, u32[]{:S(2)}) copy-start(bf16[4,4,8,128]{3,2,1,0:T(8,128)(2,1)S(1)} %reshape.196) | copy-start | bytes 98308
  6.7 68.8 %all-to-all-start = ((bf16[16,16,1024]{2,1,0:T(8,128)(2,1)}), bf16[16,16,1024]{2,1,0:T(8,128)(2,1)S(1)}, u32[]{:S(2)}, u32[]{:S(2)}) async-start(bf16[16,16,1024]{2,1,0:T(8,128)(2,1)} %broadcast_in_dim.25), calls=%async_computation | async-start | bytes 1048576 | tf_op jit(solution)/shard_map/all_to_all | solution.py:22
  76.3 5.1 %collective-permute-start = (f32[64,384]{1,0:T(8,128)S(1)}, f32[64,384]{1,0:T(8,128)S(1)}, u32[]{:S(2)}, u32[]{:S(2)}) collective-permute-start(f32[64,384]{1,0:T(8,128)S(1)} %get-tuple-element.10), channel_id=1, source_target_pairs={{0,64},{64,128},{128,192},{192,0},{1,65},{65,129},{129,193},{193,1... | collective-permute-start | bytes 294920 | tf_op jit(solution)/shard_map/ppermute | solution.py:16
  77.9 7.2 %collective-permute-start.1 = (f32[64,384]{1,0:T(8,128)S(1)}, f32[64,384]{1,0:T(8,128)S(1)}, u32[]{:S(2)}, u32[]{:S(2)}) collective-permute-start(f32[64,384]{1,0:T(8,128)S(1)} %get-tuple-element.12), channel_id=1, source_target_pairs={{0,128},{64,192},{128,0},{192,64},{1,129},{65,193},{129,1},{193,65... | collective-permute-start | bytes 294920 | tf_op jit(solution)/shard_map/ppermute | solution.py:16
  79.0 6.6 %collective-permute-start.2 = (f32[64,384]{1,0:T(8,128)S(1)}, f32[64,384]{1,0:T(8,128)S(1)}, u32[]{:S(2)}, u32[]{:S(2)}) collective-permute-start(f32[64,384]{1,0:T(8,128)S(1)} %get-tuple-element.11), channel_id=1, source_target_pairs={{0,192},{64,0},{128,64},{192,128},{1,193},{65,1},{129,65},{193,129... | collective-permute-start | bytes 294920 | tf_op jit(solution)/shard_map/ppermute | solution.py:16
  86.7 18.6 %all-to-all-start.3 = ((bf16[16,2,16,384]{3,2,1,0:T(8,128)(2,1)}), bf16[16,2,16,384]{3,2,1,0:T(8,128)(2,1)S(1)}, u32[]{:S(2)}, u32[]{:S(2)}) async-start(bf16[16,2,16,384]{3,2,1,0:T(8,128)(2,1)} %add_convert_fusion.4), calls=%async_computation.3 | async-start | bytes 786432 | tf_op jit(solution)/shard_map/all_to_all | solution.py:149
  90.3 64.5 %collective-permute-start.10 = (bf16[6144,288]{0,1:T(8,128)(2,1)}, bf16[6144,288]{0,1:T(8,128)(2,1)}, u32[]{:S(2)}, u32[]{:S(2)}) collective-permute-start(bf16[6144,288]{0,1:T(8,128)(2,1)} %bitcast.133), channel_id=1, source_target_pairs={{0,1},{1,0},{2,3},{3,2},{4,5},{5,4},{6,7},{7,6},{8,9},{9,8},{10,11... | collective-permute-start | bytes 10616840 | tf_op jit(solution)/shard_map/ppermute | solution.py:16
  90.4 67.6 %collective-permute-start.11 = (bf16[6144,288]{0,1:T(8,128)(2,1)}, bf16[6144,288]{0,1:T(8,128)(2,1)}, u32[]{:S(2)}, u32[]{:S(2)}) collective-permute-start(bf16[6144,288]{0,1:T(8,128)(2,1)} %bitcast.35), channel_id=1, source_target_pairs={{0,1},{1,0},{2,3},{3,2},{4,5},{5,4},{6,7},{7,6},{8,9},{9,8},{10,11... | collective-permute-start | bytes 10616840 | tf_op jit(solution)/shard_map/ppermute | solution.py:16
  90.9 67.1 %collective-permute-start.12 = (bf16[288,6144]{1,0:T(8,128)(2,1)}, bf16[288,6144]{1,0:T(8,128)(2,1)}, u32[]{:S(2)}, u32[]{:S(2)}) collective-permute-start(bf16[288,6144]{1,0:T(8,128)(2,1)} %bitcast.36), channel_id=1, source_target_pairs={{0,1},{1,0},{2,3},{3,2},{4,5},{5,4},{6,7},{7,6},{8,9},{9,8},{10,11... | collective-permute-start | bytes 10616840 | tf_op jit(solution)/shard_map/ppermute | solution.py:16
  105.6 37.4 %copy-start.5 = (bf16[1,6144,288]{1,2,0:T(8,128)(2,1)S(1)}, bf16[1,6144,288]{1,2,0:T(8,128)(2,1)}, u32[]{:S(2)}) copy-start(bf16[1,6144,288]{1,2,0:T(8,128)(2,1)} %param.19) | copy-start | bytes 10616836
  105.6 9.6 %collective-permute-start.3 = (bf16[32,6144]{1,0:T(8,128)(2,1)S(1)}, bf16[32,6144]{1,0:T(8,128)(2,1)S(1)}, u32[]{:S(2)}, u32[]{:S(2)}) collective-permute-start(bf16[32,6144]{1,0:T(8,128)(2,1)S(1)} %bitcast.114), channel_id=1, source_target_pairs={{0,64},{64,128},{128,192},{192,0},{1,65},{65,129},{129,193},{193,1... | collective-permute-start | bytes 1179656 | tf_op jit(solution)/shard_map/ppermute | solution.py:16
  107.2 9.3 %collective-permute-start.4 = (bf16[32,6144]{1,0:T(8,128)(2,1)S(1)}, bf16[32,6144]{1,0:T(8,128)(2,1)S(1)}, u32[]{:S(2)}, u32[]{:S(2)}) collective-permute-start(bf16[32,6144]{1,0:T(8,128)(2,1)S(1)} %bitcast.115), channel_id=1, source_target_pairs={{0,192},{64,0},{128,64},{192,128},{1,193},{65,1},{129,65},{193,129... | collective-permute-start | bytes 1179656 | tf_op jit(solution)/shard_map/ppermute | solution.py:16
  115.2 8.6 %collective-permute-start.6 = (bf16[32,6144]{1,0:T(8,128)(2,1)S(1)}, bf16[32,6144]{1,0:T(8,128)(2,1)S(1)}, u32[]{:S(2)}, u32[]{:S(2)}) collective-permute-start(bf16[32,6144]{1,0:T(8,128)(2,1)S(1)} %bitcast.117), channel_id=1, source_target_pairs={{0,2},{2,0},{1,3},{3,1},{4,6},{6,4},{5,7},{7,5},{8,10},{10,8},{9,1... | collective-permute-start | bytes 1179656 | tf_op jit(solution)/shard_map/ppermute | solution.py:16
  116.5 10.2 %collective-permute-start.5 = (bf16[32,6144]{1,0:T(8,128)(2,1)S(1)}, bf16[32,6144]{1,0:T(8,128)(2,1)S(1)}, u32[]{:S(2)}, u32[]{:S(2)}) collective-permute-start(bf16[32,6144]{1,0:T(8,128)(2,1)S(1)} %bitcast.118), channel_id=1, source_target_pairs={{0,128},{64,192},{128,0},{192,64},{1,129},{65,193},{129,1},{193,65... | collective-permute-start | bytes 1179656 | tf_op jit(solution)/shard_map/ppermute | solution.py:16
  123.8 10.6 %collective-permute-start.7 = (bf16[32,6144]{1,0:T(8,128)(2,1)S(1)}, bf16[32,6144]{1,0:T(8,128)(2,1)S(1)}, u32[]{:S(2)}, u32[]{:S(2)}) collective-permute-start(bf16[32,6144]{1,0:T(8,128)(2,1)S(1)} %collective-permute-done.6), channel_id=1, source_target_pairs={{0,64},{64,128},{128,192},{192,0},{1,65},{65,129},{129,193},{193,1... | collective-permute-start | bytes 1179656 | tf_op jit(solution)/shard_map/ppermute | solution.py:16
  126.8 9.1 %collective-permute-start.8 = (bf16[32,6144]{1,0:T(8,128)(2,1)S(1)}, bf16[32,6144]{1,0:T(8,128)(2,1)S(1)}, u32[]{:S(2)}, u32[]{:S(2)}) collective-permute-start(bf16[32,6144]{1,0:T(8,128)(2,1)S(1)} %collective-permute-done.6), channel_id=1, source_target_pairs={{0,192},{64,0},{128,64},{192,128},{1,193},{65,1},{129,65},{193,129... | collective-permute-start | bytes 1179656 | tf_op jit(solution)/shard_map/ppermute | solution.py:16
  134.3 8.6 %collective-permute-start.9 = (bf16[32,6144]{1,0:T(8,128)(2,1)S(1)}, bf16[32,6144]{1,0:T(8,128)(2,1)S(1)}, u32[]{:S(2)}, u32[]{:S(2)}) collective-permute-start(bf16[32,6144]{1,0:T(8,128)(2,1)S(1)} %collective-permute-done.5), channel_id=1, source_target_pairs={{0,2},{2,0},{1,3},{3,1},{4,6},{6,4},{5,7},{7,5},{8,10},{10,8},{9,1... | collective-permute-start | bytes 1179656 | tf_op jit(solution)/shard_map/ppermute | solution.py:16
  171.7 8.0 %collective-permute-start.15 = (bf16[32,6144]{1,0:T(8,128)(2,1)}, bf16[32,6144]{1,0:T(8,128)(2,1)S(1)}, u32[]{:S(2)}, u32[]{:S(2)}) collective-permute-start(bf16[32,6144]{1,0:T(8,128)(2,1)} %get-tuple-element.6), channel_id=1, source_target_pairs={{0,2},{2,0},{1,3},{3,1},{4,6},{6,4},{5,7},{7,5},{8,10},{10,8},{9,1... | collective-permute-start | bytes 1179656 | tf_op jit(solution)/shard_map/ppermute | solution.py:16
  172.7 12.6 %collective-permute-start.17 = (bf16[32,6144]{1,0:T(8,128)(2,1)S(1)}, bf16[32,6144]{1,0:T(8,128)(2,1)S(1)}, u32[]{:S(2)}, u32[]{:S(2)}) collective-permute-start(bf16[32,6144]{1,0:T(8,128)(2,1)S(1)} %get-tuple-element.5), channel_id=1, source_target_pairs={{0,192},{64,0},{128,64},{192,128},{1,193},{65,1},{129,65},{193,129... | collective-permute-start | bytes 1179656 | tf_op jit(solution)/shard_map/ppermute | solution.py:16
  175.7 12.1 %collective-permute-start.18 = (bf16[32,6144]{1,0:T(8,128)(2,1)S(1)}, bf16[32,6144]{1,0:T(8,128)(2,1)S(1)}, u32[]{:S(2)}, u32[]{:S(2)}) collective-permute-start(bf16[32,6144]{1,0:T(8,128)(2,1)S(1)} %get-tuple-element.4), channel_id=1, source_target_pairs={{0,64},{64,128},{128,192},{192,0},{1,65},{65,129},{129,193},{193,1... | collective-permute-start | bytes 1179656 | tf_op jit(solution)/shard_map/ppermute | solution.py:16
  175.9 22.8 %collective-permute-start.13 = (bf16[32,6144]{1,0:T(8,128)(2,1)}, bf16[32,6144]{1,0:T(8,128)(2,1)S(1)}, u32[]{:S(2)}, u32[]{:S(2)}) collective-permute-start(bf16[32,6144]{1,0:T(8,128)(2,1)} %get-tuple-element.3), channel_id=1, source_target_pairs={{0,64},{64,128},{128,192},{192,0},{1,65},{65,129},{129,193},{193,1... | collective-permute-start | bytes 1179656 | tf_op jit(solution)/shard_map/ppermute | solution.py:16
  177.4 21.3 %collective-permute-start.14 = (bf16[32,6144]{1,0:T(8,128)(2,1)}, bf16[32,6144]{1,0:T(8,128)(2,1)S(1)}, u32[]{:S(2)}, u32[]{:S(2)}) collective-permute-start(bf16[32,6144]{1,0:T(8,128)(2,1)} %get-tuple-element.7), channel_id=1, source_target_pairs={{0,192},{64,0},{128,64},{192,128},{1,193},{65,1},{129,65},{193,129... | collective-permute-start | bytes 1179656 | tf_op jit(solution)/shard_map/ppermute | solution.py:16
  189.9 54.0 %copy-start.1 = (bf16[4,8,128,128]{3,2,1,0:T(8,128)(2,1)S(1)}, bf16[4,8,128,128]{3,2,1,0:T(8,128)(2,1)}, u32[]{:S(2)}) copy-start(bf16[4,8,128,128]{3,2,1,0:T(8,128)(2,1)} %param.15) | copy-start | bytes 3145732
  189.9 54.0 %copy-start.4 = (bf16[4,4,8,128]{3,2,1,0:T(8,128)(2,1)S(1)}, bf16[4,4,8,128]{3,2,1,0:T(8,128)(2,1)}, u32[]{:S(2)}) copy-start(bf16[4,4,8,128]{3,2,1,0:T(8,128)(2,1)} %copy-done.3) | copy-start | bytes 98308
  189.9 9.5 %collective-permute-start.16 = (bf16[32,6144]{1,0:T(8,128)(2,1)}, bf16[32,6144]{1,0:T(8,128)(2,1)S(1)}, u32[]{:S(2)}, u32[]{:S(2)}) collective-permute-start(bf16[32,6144]{1,0:T(8,128)(2,1)} %get-tuple-element.8), channel_id=1, source_target_pairs={{0,128},{64,192},{128,0},{192,64},{1,129},{65,193},{129,1},{193,65... | collective-permute-start | bytes 1179656 | tf_op jit(solution)/shard_map/ppermute | solution.py:16
  190.8 8.6 %collective-permute-start.19 = (bf16[32,6144]{1,0:T(8,128)(2,1)S(1)}, bf16[32,6144]{1,0:T(8,128)(2,1)S(1)}, u32[]{:S(2)}, u32[]{:S(2)}) collective-permute-start(bf16[32,6144]{1,0:T(8,128)(2,1)S(1)} %get-tuple-element.9), channel_id=1, source_target_pairs={{0,2},{2,0},{1,3},{3,1},{4,6},{6,4},{5,7},{7,5},{8,10},{10,8},{9,1... | collective-permute-start | bytes 1179656 | tf_op jit(solution)/shard_map/ppermute | solution.py:16
  192.1 16.8 %all-to-all-start.1 = ((bf16[16,4,384]{2,1,0:T(4,128)(2,1)}), bf16[16,4,384]{2,1,0:T(4,128)(2,1)S(1)}, u32[]{:S(2)}, u32[]{:S(2)}) async-start(bf16[16,4,384]{2,1,0:T(4,128)(2,1)} %copy.144), calls=%async_computation.1 | async-start | bytes 98304 | tf_op jit(solution)/shard_map/all_to_all | solution.py:140
  208.9 17.2 %all-to-all-start.4 = ((bf16[16,2,6144]{2,1,0:T(2,128)(2,1)}), bf16[16,2,6144]{2,1,0:T(2,128)(2,1)S(1)}, u32[]{:S(2)}, u32[]{:S(2)}) async-start(bf16[16,2,6144]{2,1,0:T(2,128)(2,1)} %bitcast.111), calls=%async_computation.4 | async-start | bytes 786432 | tf_op jit(solution)/shard_map/all_to_all | solution.py:158
  226.8 11.6 %all-to-all-start.2 = ((bf16[4,4,6144]{2,1,0:T(4,128)(2,1)}), bf16[4,4,6144]{2,1,0:T(4,128)(2,1)S(1)}, u32[]{:S(2)}, u32[]{:S(2)}) async-start(bf16[4,4,6144]{2,1,0:T(4,128)(2,1)} %broadcast_in_dim.27), calls=%async_computation.2 | async-start | bytes 393216 | tf_op jit(solution)/shard_map/all_to_all | solution.py:22
  239.1 9.7 %all-to-all-start.5 = ((bf16[4,4,6144]{2,1,0:T(4,128)(2,1)}), bf16[4,4,6144]{2,1,0:T(4,128)(2,1)S(1)}, u32[]{:S(2)}, u32[]{:S(2)}) async-start(bf16[4,4,6144]{2,1,0:T(4,128)(2,1)} %broadcast_in_dim.28), calls=%async_computation.5 | async-start | bytes 393216 | tf_op jit(solution)/shard_map/all_to_all | solution.py:22

commit v2 on v1

--- a/solution.py
+++ b/solution.py
@@ -1,12 +1,17 @@
+import functools
+
 import jax
 import jax.numpy as jnp
 from jax import lax
+from jax.experimental import pallas as pl
+from jax.experimental.pallas import tpu as pltpu
 from jax.sharding import Mesh, PartitionSpec as P
 
 BLOCKS = ("y", "zp")
 EXPERT = ("y", "zp", "zl", "core")
 BF16 = jnp.bfloat16
 F32 = jnp.float32
+LANES = 128
 EXACT = lax.Precision.HIGHEST
 
 
@@ -61,37 +66,124 @@
 
 
 def gather_block(own):
-    across = shift(own, "zl", 1)
-    left, right, far = shift(own, "head", 1), shift(own, "head", -1), shift(own, "head", 2)
-    across_left, across_right = shift(across, "head", 1), shift(across, "head", -1)
-    across_far = shift(far, "zl", 1)
-    return [own, left, right, far, across, across_left, across_right, across_far]
+    half = own.shape[0] // 2
+    left, right, across = shift(own, "head", 1), shift(own, "head", -1), shift(own, "zl", 1)
+
+    def halves(one, other):
+        return jnp.concatenate([one, other], axis=0)
+
+    by_left = shift(halves(left[:half], across[:half]), "head", 1)
+    by_right = shift(halves(right[half:], across[half:]), "head", -1)
+    by_across = shift(halves(left[half:], right[:half]), "zl", 1)
+    last_left = shift(by_left[half:], "head", 1)
+    last_right = shift(by_right[half:], "head", -1)
+    return [own, left, right, across, by_left, by_right, by_across, last_left, last_right]
 
 
 def scatter_block(parts):
-    own, left, right, far, across, across_left, across_right, across_far = parts
+    own, left, right, across, by_left, by_right, by_across, last_left, last_right = parts
+    half = own.shape[0] // 2
 
     def add(*terms):
-        return sum(t.astype(F32) for t in terms)
-
-    from_right = shift(across_left, "head", -1)
-    from_left = shift(across_right, "head", 1)
-    from_far = shift(across_far, "zl", 1)
-    got_left = shift(right, "head", 1)
-    got_right = shift(left, "head", -1)
-    got_far = shift(add(far, from_far).astype(BF16), "head", 2)
-    got_across = shift(add(across, from_right, from_left).astype(BF16), "zl", 1)
-    return add(own, got_left, got_right, got_far, got_across).astype(BF16)
-
-
-def expert_ffn(rows, weights):
-    total = 0.0
-    for gate, up, down in weights:
-        gated = jnp.dot(rows, gate, preferred_element_type=F32)
-        lifted = jnp.dot(rows, up, preferred_element_type=F32)
-        hidden = (jax.nn.silu(gated) * lifted).astype(BF16)
-        total = total + jnp.dot(hidden, down, preferred_element_type=F32)
-    return total.astype(BF16)
+        return sum(t.astype(F32) for t in terms).astype(BF16)
+
+    def halves(one, other):
+        return jnp.concatenate([one, other], axis=0)
+
+    from_right = shift(last_left, "head", -1)
+    from_left = shift(last_right, "head", 1)
+    by_left = halves(by_left[:half], add(by_left[half:], from_right))
+    by_right = halves(by_right[:half], add(by_right[half:], from_left))
+    from_right = shift(by_left, "head", -1)
+    from_left = shift(by_right, "head", 1)
+    from_across = shift(by_across, "zl", 1)
+    left = add(left, halves(from_right[:half], from_across[:half]))
+    right = add(right, halves(from_across[half:], from_left[:half]))
+    across = add(across, halves(from_right[half:], from_left[half:]))
+    return add(own, shift(left, "head", -1), shift(right, "head", 1), shift(across, "zl", 1))
+
+
+def ffn_kernel(count, inner, *refs):
+    rows, refs = refs[:count], refs[count:]
+    gate, up, down = refs[0:2], refs[2:4], refs[4:6]
+    outs, refs = refs[6 : 6 + count], refs[6 + count :]
+    gated, lifted, hidden = refs
+    step = pl.program_id(0)
+
+    @pl.when(step == 0)
+    def _():
+        gated[...] = jnp.zeros_like(gated)
+        lifted[...] = jnp.zeros_like(lifted)
+
+    @pl.when(step < inner)
+    def _():
+        block = jnp.concatenate([r[...] for r in rows], axis=0)
+        for i in range(2):
+            gated[i] += jnp.dot(block, gate[i][...], preferred_element_type=F32)
+            lifted[i] += jnp.dot(block, up[i][...], preferred_element_type=F32)
+
+    @pl.when(step == inner - 1)
+    def _():
+        value = gated[...]
+        hidden[...] = (value / (1.0 + jnp.exp(-value)) * lifted[...]).astype(BF16)
+
+    @pl.when(step >= inner)
+    def _():
+        total = jnp.dot(hidden[0], down[0][...], preferred_element_type=F32)
+        total += jnp.dot(hidden[1], down[1][...], preferred_element_type=F32)
+        total = total.astype(BF16)
+        start = 0
+        for out in outs:
+            out[...] = total[start : start + out.shape[0]]
+            start += out.shape[0]
+
+
+def expert_ffn(parts, gate, up, down):
+    features, width = gate[0].shape
+    total_rows = sum(p.shape[0] for p in parts)
+    tile = min(features, 1024)
+    inner = features // tile
+
+    def first(i):
+        return jnp.minimum(i, inner - 1)
+
+    def second(i):
+        return jnp.maximum(i - inner, 0)
+
+    return pl.pallas_call(
+        functools.partial(ffn_kernel, len(parts), inner),
+        grid=(2 * inner,),
+        in_specs=[pl.BlockSpec((p.shape[0], tile), lambda i: (0, first(i))) for p in parts]
+        + [pl.BlockSpec((tile, width), lambda i: (first(i), 0))] * 4
+        + [pl.BlockSpec((width, tile), lambda i: (0, second(i)))] * 2,
+        out_specs=[pl.BlockSpec((p.shape[0], tile), lambda i: (0, second(i))) for p in parts],
+        out_shape=[jax.ShapeDtypeStruct(p.shape, BF16) for p in parts],
+        scratch_shapes=[
+            pltpu.VMEM((2, total_rows, width), F32),
+            pltpu.VMEM((2, total_rows, width), F32),
+            pltpu.VMEM((2, total_rows, width), BF16),
+        ],
+        compiler_params=pltpu.CompilerParams(vmem_limit_bytes=32 * 1024 * 1024),
+        cost_estimate=pl.CostEstimate(
+            flops=12 * total_rows * features * width,
+            bytes_accessed=12 * features * width + 4 * total_rows * features,
+            transcendentals=2 * total_rows * width,
+        ),
+    )(*parts, *gate, *up, *down)
+
+
+def block_columns(out_weight):
+    width = out_weight.shape[1]
+
+    def ordered(own, other, axis):
+        first = lax.axis_index(axis) == 0
+        return jnp.where(first, own, other), jnp.where(first, other, own)
+
+    pair = jnp.concatenate(ordered(out_weight, shift(out_weight, "zl", 1), "zl"), axis=1)
+    low, high = ordered(pair, shift(pair, "core", 1), "core")
+    return jnp.concatenate(
+        [low[:, :width], high[:, :width], low[:, width:], high[:, width:]], axis=1
+    )
 
 
 def shards(
@@ -113,55 +205,57 @@
     capacity = rows // 2
     head = lax.axis_index("head")
 
-    own_weights = (gate_weight[0], up_weight[0], down_weight[0])
-    other_weights = tuple(shift(w, "core", 1) for w in own_weights)
-    columns = lax.all_gather(out_weight, ("zl", "core"), axis=1, tiled=True)
+    gate, up, down = (
+        (w[0], shift(w[0], "core", 1)) for w in (gate_weight, up_weight, down_weight)
+    )
+    columns = block_columns(out_weight)
     width = columns.shape[1]
     features = width * blocks
 
-    own_ids = lax.dynamic_index_in_dim(route_ids, head, 0, keepdims=False)
-    own_gate = lax.dynamic_index_in_dim(route_gate, head, 0, keepdims=False)
-    peer_ids = lax.all_gather(own_ids, BLOCKS, axis=0, tiled=False)
-
     attended, state_out = attention(query_rows, key_rows, value_rows, forget, head_state)
 
-    peers = spread(attended, BLOCKS).reshape(blocks, steps, rows, -1)
-    peers = jnp.transpose(peers, (1, 2, 0, 3)).reshape(steps * rows * blocks, -1)
+    depth = attended.shape[1]
+    ids = jnp.pad(route_ids.reshape(steps * rows, 2).astype(BF16), ((0, 0), (0, LANES - 2)))
+    peers = spread(jnp.concatenate([attended, ids], axis=1), BLOCKS)
+    peers = peers.reshape(blocks, steps, rows, depth + LANES)
+    peer_ids = peers[..., depth : depth + 2].astype(jnp.int32)
+    peers = jnp.transpose(peers[..., :depth], (1, 2, 0, 3)).reshape(steps * rows * blocks, depth)
     partial = jnp.dot(peers, columns, preferred_element_type=F32)
     partial = partial.reshape(steps, rows * blocks, width)
-    projected = lax.dynamic_index_in_dim(partial, head, 0, keepdims=False)
+
+    def of_step(array, axis, there=head):
+        return lax.dynamic_index_in_dim(array, there, axis, keepdims=False)
+
+    projected = of_step(partial, 0)
     for distance in range(1, steps):
         there = lax.rem(head + distance, steps)
-        projected = projected + shift(
-            lax.dynamic_index_in_dim(partial, there, 0, keepdims=False), "head", distance
-        )
+        projected = projected + shift(of_step(partial, 0, there), "head", distance)
     projected = projected.astype(BF16).reshape(rows, blocks, width)
 
-    returned = lax.all_to_all(
-        jnp.transpose(projected, (1, 0, 2)), BLOCKS, split_axis=0, concat_axis=0, tiled=True
-    )
-    mixed = spread(jnp.transpose(returned, (1, 0, 2)).reshape(rows, features), "head")
-
-    placed = jnp.sum(place(peer_ids, experts, capacity), axis=-1)
+    placed = jnp.sum(place(of_step(peer_ids, 1), experts, capacity), axis=-1)
     packed = sum(
         placed[:, :, :, r, None] * projected[r].astype(F32)[None, None] for r in range(rows)
     ).astype(BF16)
     packed = lax.all_to_all(packed, BLOCKS, split_axis=0, concat_axis=0, tiled=True)
     piece = jnp.transpose(packed, (1, 2, 0, 3)).reshape(capacity * blocks, features)
 
-    pieces = gather_block(piece)
-    count = len(pieces)
-    result = expert_ffn(jnp.concatenate(pieces, axis=0), (own_weights, other_weights))
-    result = scatter_block(list(result.reshape(count, capacity * blocks, features)))
+    result = scatter_block(expert_ffn(gather_block(piece), gate, up, down))
 
     result = jnp.transpose(result.reshape(capacity, blocks, features), (1, 0, 2))
-    result = lax.all_to_all(result, BLOCKS, split_axis=0, concat_axis=0, tiled=True)
-    weights = jnp.sum(place(own_ids, experts, capacity) * own_gate, axis=-1)
+    mixed = jnp.transpose(projected, (1, 0, 2)).reshape(blocks, capacity, 2 * width)
+    result = lax.all_to_all(
+        jnp.concatenate([result, mixed], axis=2), BLOCKS, split_axis=0, concat_axis=0, tiled=True
+    )
+    mixed = result[..., features:].reshape(blocks, rows, width)
+    mixed = jnp.transpose(mixed, (1, 0, 2)).reshape(rows, features)
+    weights = jnp.sum(
+        place(of_step(route_ids, 0), experts, capacity) * of_step(route_gate, 0), axis=-1
+    )
     combined = jnp.einsum(
-        "esr,esd->rd", weights, result.astype(F32), precision=EXACT
+        "esr,esd->rd", weights, result[..., :features].astype(F32), precision=EXACT
     ).astype(BF16)
-    moe_out = spread(combined, "head")
-    return mixed, moe_out, state_out
+    both = spread(jnp.concatenate([mixed, combined], axis=0), "head")
+    return both[:, :rows], both[:, rows:], state_out
 
 
 def solution(mesh):

time: 251 us -> 229 us (0.912)
  blocking collectives: 57.4 us -> 17.5 us
  local copies, waits for them, and re-layouts: 12.4 us -> 50 us
  matrix products: 31.7 us -> 5.72 us
  Pallas kernels: 0 us -> 16.4 us
  waiting for transfers between devices: 83.1 us -> 73.8 us
  starting transfers between devices: 59 us -> 54.1 us
    all_gather x2 -> x0, blocking collectives: 57.4 us -> none  [the longest x1 48 us: shards(): peer_ids = lax.all_gather(own_ids, BLOCKS, axis=0, tiled=False)]
    dot_general x5 -> x1, matrix products: 26.6 us -> 0.36 us  [shards(): jnp.einsum('esr,esd->rd', weights, result[..., :features].astype(F32), pr...]
    unnamed x23 -> x61, local copies, waits for them, and re-layouts: 1.66 us -> 25.9 us
    all_to_all x3 -> x1, waiting for transfers between devices: 34.2 us -> 12.9 us  [shards(): lax.all_to_all(jnp.concatenate([result, mixed], axis=2), BLOCKS, split_ax...]
    all_to_all x0 -> x1, blocking collectives: none -> 17.5 us  [shards(): lax.all_to_all(packed, BLOCKS, split_axis=0, concat_axis=0, tiled=True)]
    pallas_call x0 -> x1, Pallas kernels: none -> 16.4 us  [expert_ffn(): pl.pallas_call(functools.partial(ffn_kernel, len(parts), inner), grid=(2...]
    all_to_all x3 -> x2, waiting for transfers between devices: 7.51 us -> 20.2 us  [spread(): return lax.all_to_all(copies, axis, split_axis=0, concat_axis=0, tiled=True)]
    ppermute x0 -> x2, local copies, waits for them, and re-layouts: none -> 12.6 us  [shift(): return lax.ppermute(array, axis, pairs)]
  transfers between devices with their start and end apart: 26 -> 27, of which waited for: 18 -> 14; matrix products, arithmetic and copies ran while one was open for 10% -> 19% of each run, Pallas kernels for 0% -> 0%
where the time goes in v2:
time: 229 us; the launch traced here: 227 us
  waiting for transfers between devices  73.8 us (32%)
  starting transfers between devices  54.1 us (24%)
  local copies, waits for them, and re-layouts  50 us (22%)
  blocking collectives  17.5 us (8%)
  Pallas kernels  16.4 us (7%)
  other arithmetic  7.98 us (3%)
  matrix products  5.72 us (2%)
    ppermute x24, waiting for transfers between devices, shift(): return lax.ppermute(array, axis, pairs)  40.7 us
    ppermute x24, starting transfers between devices, shift(): return lax.ppermute(array, axis, pairs)  27.8 us
    unnamed x61, local copies, waits for them, and re-layouts  25.9 us
    all_to_all x2, starting transfers between devices, spread(): return lax.all_to_all(copies, axis, split_axis=0, concat_axis=0, tiled=True)  20.3 us
    all_to_all x2, waiting for transfers between devices, spread(): return lax.all_to_all(copies, axis, split_axis=0, concat_axis=0, tiled=True)  20.2 us
    all_to_all x1, blocking collectives, shards(): lax.all_to_all(packed, BLOCKS, split_axis=0, concat_axis=0, tiled=True)  17.5 us
    pallas_call x1, Pallas kernels, expert_ffn(): pl.pallas_call(functools.partial(ffn_kernel, len(parts), inner), grid=(2...  16.4 us
    all_to_all x1, waiting for transfers between devices, shards(): lax.all_to_all(jnp.concatenate([result, mixed], axis=2), BLOCKS, split_ax...  12.9 us
  transfers between devices with their start and end apart: 27, of which 14 were waited for; matrix products, arithmetic and copies ran while one was open for 19% of the time, Pallas kernels for 0%

profile of v2, /device:TPU:2, one launch (start us, length us, event | category | flops | bytes accessed | tf_op | source)
XLA Modules:
  0.0 226.8 jit_solution(5902194677134522401)
XLA Ops:
  0.7 1.1 copy.176
  1.8 2.0 collective-permute-start
  3.8 0.8 reshape.192
  4.6 0.8 reshape.193
  6.4 0.8 reshape.194
  7.9 1.6 fusion.4
  9.7 0.9 broadcast_in_dim.18
  10.5 10.3 %all-to-all-start = ((bf16[16,16,1152]{2,1,0:T(8,128)(2,1)}), bf16[16,16,1152]{2,1,0:T(8,128)(2,1)S(1)}, u32[]{:S(2)}, u32[]{:S(2)}) async-start(bf16[16,16,1152]{2,1,0:T(8,128)(2,1)} %broadcast_in_dim.18), calls=%async_computation | async-start | bytes 1179648 | tf_op jit(solution)/shard_map/all_to_all | solution.py:27
  21.3 1.9 collective-permute-done.1
  23.8 17.3 %all-to-all-done = bf16[16,16,1152]{2,1,0:T(8,128)(2,1)S(1)} async-done(((bf16[16,16,1152]{2,1,0:T(8,128)(2,1)}), bf16[16,16,1152]{2,1,0:T(8,128)(2,1)S(1)}, u32[]{:S(2)}, u32[]{:S(2)}) %all-to-all-start) | async-done | bytes 589856 | tf_op jit(solution)/shard_map/all_to_all | solution.py:27
  41.9 0.8 dynamic-slice_bitcast_fusion.2
  42.7 1.5 collective-permute-start.2
  44.2 1.1 collective-permute-start.3
  45.3 2.2 collective-permute-start.4
  48.1 1.0 copy.171
  49.8 0.9 copy.173
  50.6 0.9 convert_reduce_fusion
  51.6 1.1 fusion.15
  53.7 17.5 %all_to_all.20 = bf16[16,2,16,384]{3,2,1,0:T(8,128)(2,1)S(1)} all-to-all(bf16[16,2,16,384]{3,2,1,0:T(8,128)(2,1)S(1)} %add_convert_fusion.5), channel_id=1, replica_groups=mesh['head'=4,'y'=4,'zp'=4,'zl'=2,'core'=2] {'y','zp'}, dimensions={0} | all-to-all | bytes 786432 | tf_op jit(solution)/shard_map/all_to_all | solution.py:239
  71.4 1.5 collective-permute-start.6
  74.0 5.2 %collective-permute-done.6.refs_2_ = bf16[32,6144]{1,0:T(8,128)(2,1)S(1)} collective-permute-done((bf16[32,6144]{1,0:T(8,128)(2,1)S(1)}, bf16[32,6144]{1,0:T(8,128)(2,1)S(1)}, u32[]{:S(2)}, u32[]{:S(2)}) %collective-permute-start.6) | collective-permute-done | bytes 393248 | tf_op jit(solution)/shard_map/ppermute | solution.py:21
  79.2 1.4 collective-permute-start.7
  80.7 6.3 %collective-permute-done.7.refs_3_ = bf16[32,6144]{1,0:T(8,128)(2,1)S(1)} collective-permute-done((bf16[32,6144]{1,0:T(8,128)(2,1)S(1)}, bf16[32,6144]{1,0:T(8,128)(2,1)S(1)}, u32[]{:S(2)}, u32[]{:S(2)}) %collective-permute-start.7) | collective-permute-done | bytes 393248 | tf_op jit(solution)/shard_map/ppermute | solution.py:21
  87.1 1.5 collective-permute-start.9
  88.6 0.9 collective-permute-start.8
  89.5 0.8 pad_maximum_fusion.4
  90.3 4.6 %collective-permute-done.9.refs_5_ = bf16[32,6144]{1,0:T(8,128)(2,1)S(1)} collective-permute-done((bf16[32,6144]{1,0:T(8,128)(2,1)S(1)}, bf16[32,6144]{1,0:T(8,128)(2,1)S(1)}, u32[]{:S(2)}, u32[]{:S(2)}) %collective-permute-start.9) | collective-permute-done | bytes 393248 | tf_op jit(solution)/shard_map/ppermute | solution.py:21
  94.9 1.4 collective-permute-start.10
  96.3 0.7 slice.221
  97.0 1.1 collective-permute-done.8.refs_4_
  98.1 3.2 %collective-permute-start.12 = (bf16[16,6144]{1,0:T(8,128)(2,1)}, bf16[16,6144]{1,0:T(8,128)(2,1)}, u32[]{:S(2)}, u32[]{:S(2)}) collective-permute-start(bf16[16,6144]{1,0:T(8,128)(2,1)} %slice.221), channel_id=1, source_target_pairs={{0,192},{64,0},{128,64},{192,128},{1,193},{65,1},{129,65},{193,129... | collective-permute-start | bytes 589832 | tf_op jit(solution)/shard_map/ppermute | solution.py:21
  101.4 0.7 slice.220
  102.1 0.8 copy-done.14
  102.8 6.3 %copy.182 = bf16[1,6144,288]{2,1,0:T(8,128)(2,1)} copy(bf16[1,6144,288]{1,2,0:T(8,128)(2,1)} %param.19) | data formatting | bytes 7077888 | tf_op args[8]
  109.1 6.3 %copy.184 = bf16[1,6144,288]{2,1,0:T(8,128)(2,1)} copy(bf16[1,6144,288]{1,2,0:T(8,128)(2,1)} %param.20) | data formatting | bytes 7077888 | tf_op args[9]
  115.4 6.3 %copy.186.refs_10_ = bf16[6144,288]{1,0:T(8,128)(2,1)} copy(bf16[6144,288]{0,1:T(8,128)(2,1)} %collective-permute-done.13) | data formatting | bytes 7077888 | tf_op jit(solution)/shard_map/ppermute | solution.py:21
  121.7 6.3 %copy.187.refs_12_ = bf16[6144,288]{1,0:T(8,128)(2,1)} copy(bf16[6144,288]{0,1:T(8,128)(2,1)} %collective-permute-done.14) | data formatting | bytes 7077888 | tf_op jit(solution)/shard_map/ppermute | solution.py:21
  128.0 2.3 %copy-done.1 = bf16[1,6144,288]{2,1,0:T(8,128)(2,1)S(1)} copy-done((bf16[1,6144,288]{2,1,0:T(8,128)(2,1)S(1)}, bf16[1,6144,288]{2,1,0:T(8,128)(2,1)}, u32[]{:S(2)}) %copy-start.1) | copy-done | bytes 3538968
  130.3 2.3 %copy-done.2 = bf16[6144,288]{1,0:T(8,128)(2,1)S(1)} copy-done((bf16[6144,288]{1,0:T(8,128)(2,1)S(1)}, bf16[6144,288]{1,0:T(8,128)(2,1)}, u32[]{:S(2)}) %copy-start.2) | copy-done | bytes 3538968
  132.7 1.0 copy-done.5
  133.7 1.0 copy-done.7
  134.7 1.0 copy-done.9
  135.7 1.0 copy-done.11
  136.7 1.0 copy-done.13
  137.7 1.0 copy-done.15
  138.6 16.4 %shard_map.130 = (bf16[32,6144]{1,0:T(8,128)(2,1)S(1)}, bf16[32,6144]{1,0:T(8,128)(2,1)S(1)}, bf16[32,6144]{1,0:T(8,128)(2,1)S(1)}, bf16[32,6144]{1,0:T(8,128)(2...) custom-call(bf16[32,6144]{1,0:T(8,128)(2,1)S(1)} %bitcast.106, ...), custom_call_target="tpu_custom_call" | custom-call | flops 5435817984 | bytes 27525120 | tf_op jit(solution)/shard_map/pallas_call | solution.py:153
  155.1 2.1 collective-permute-start.16
  157.2 1.2 collective-permute-start.18
  158.5 4.3 %collective-permute-done.16 = bf16[16,6144]{1,0:T(8,128)(2,1)S(1)} collective-permute-done((bf16[16,6144]{1,0:T(8,128)(2,1)S(1)}, bf16[16,6144]{1,0:T(8,128)(2,1)S(1)}, u32[]{:S(2)}, u32[]{:S(2)}) %collective-permute-start.16) | collective-permute-done | bytes 196640 | tf_op jit(solution)/shard_map/ppermute | solution.py:21
  162.9 2.2 collective-permute-start.17
  165.2 1.7 collective-permute-done.20
  167.0 7.8 %collective-permute-done.17 = bf16[32,6144]{1,0:T(8,128)(2,1)S(1)} collective-permute-done((bf16[32,6144]{1,0:T(8,128)(2,1)S(1)}, bf16[32,6144]{1,0:T(8,128)(2,1)S(1)}, u32[]{:S(2)}, u32[]{:S(2)}) %collective-permute-start.17) | collective-permute-done | bytes 393248 | tf_op jit(solution)/shard_map/ppermute | solution.py:21
  175.0 2.8 %collective-permute-start.19 = (bf16[32,6144]{1,0:T(8,128)(2,1)S(1)}, bf16[32,6144]{1,0:T(8,128)(2,1)S(1)}, u32[]{:S(2)}, u32[]{:S(2)}) collective-permute-start(bf16[32,6144]{1,0:T(8,128)(2,1)S(1)} %add_convert_fusion.4), channel_id=1, source_target_pairs={{0,192},{64,0},{128,64},{192,128},{1,193},{65,1},{129,65},{193,129... | collective-permute-start | bytes 1179656 | tf_op jit(solution)/shard_map/ppermute | solution.py:21
  178.7 1.4 collective-permute-start.23
  180.3 3.3 %collective-permute-done.19 = bf16[32,6144]{1,0:T(8,128)(2,1)S(1)} collective-permute-done((bf16[32,6144]{1,0:T(8,128)(2,1)S(1)}, bf16[32,6144]{1,0:T(8,128)(2,1)S(1)}, u32[]{:S(2)}, u32[]{:S(2)}) %collective-permute-start.19) | collective-permute-done | bytes 393248 | tf_op jit(solution)/shard_map/ppermute | solution.py:21
  183.7 3.8 %collective-permute-done.22 = bf16[32,6144]{1,0:T(8,128)(2,1)S(1)} collective-permute-done((bf16[32,6144]{1,0:T(8,128)(2,1)S(1)}, bf16[32,6144]{1,0:T(8,128)(2,1)S(1)}, u32[]{:S(2)}, u32[]{:S(2)}) %collective-permute-start.22) | collective-permute-done | bytes 393248 | tf_op jit(solution)/shard_map/ppermute | solution.py:21
  188.1 1.2 pad_maximum_fusion.1
  189.2 6.0 %all-to-all-start.2 = ((bf16[16,2,6912]{2,1,0:T(2,128)(2,1)}), bf16[16,2,6912]{2,1,0:T(2,128)(2,1)S(1)}, u32[]{:S(2)}, u32[]{:S(2)}) async-start(bf16[16,2,6912]{2,1,0:T(2,128)(2,1)} %pad_maximum_fusion.1), calls=%async_computation.2 | async-start | bytes 884736 | tf_op jit(solution)/shard_map/all_to_all | solution.py:246
  195.6 12.9 %all-to-all-done.2 = bf16[16,2,6912]{2,1,0:T(2,128)(2,1)S(1)} async-done(((bf16[16,2,6912]{2,1,0:T(2,128)(2,1)}), bf16[16,2,6912]{2,1,0:T(2,128)(2,1)S(1)}, u32[]{:S(2)}, u32[]{:S(2)}) %all-to-all-start.2) | async-done | bytes 442400 | tf_op jit(solution)/shard_map/all_to_all | solution.py:246
  209.3 0.8 broadcast_in_dim.19
  210.1 9.9 %all-to-all-start.3 = ((bf16[4,8,6144]{2,1,0:T(8,128)(2,1)}), bf16[4,8,6144]{2,1,0:T(8,128)(2,1)S(1)}, u32[]{:S(2)}, u32[]{:S(2)}) async-start(bf16[4,8,6144]{2,1,0:T(8,128)(2,1)} %broadcast_in_dim.19), calls=%async_computation.3 | async-start | bytes 786432 | tf_op jit(solution)/shard_map/all_to_all | solution.py:27
  220.2 2.9 %add_convert_fusion = bf16[4,8,128,128]{3,2,1,0:T(8,128)(2,1)} fusion(bf16[4,8,128,128]{3,2,1,0:T(8,128)(2,1)S(1)} %copy-done.18, f32[8]{0:T(128)S(1)} %slice_bitcast_fusion.8, bf16[4,4,8,128]{3,2,1,0:T(8,128)(2,1)S(1)} %copy-done.23, f32[4,8]{0,1:T(8,128)S(1)} %copy.194, bf16[4,4,8,128]{3,2,1,0:T(8,128)(2,1)S(1)} %copy-done.25), kind=kOutput, calls=%fused_computation.2 | convolution fusion | flops 27295744 | bytes 2162848 | tf_op jit(solution)/shard_map/trhi,trhj->rhij/dot_general | solution.py:50
  223.1 2.9 %all-to-all-done.3 = bf16[4,8,6144]{2,1,0:T(8,128)(2,1)S(1)} async-done(((bf16[4,8,6144]{2,1,0:T(8,128)(2,1)}), bf16[4,8,6144]{2,1,0:T(8,128)(2,1)S(1)}, u32[]{:S(2)}, u32[]{:S(2)}) %all-to-all-start.3) | async-done | bytes 393248 | tf_op jit(solution)/shard_map/all_to_all | solution.py:27
  226.0 0.9 fusion.38
  (146 shorter events, 10.8 us)
Async XLA Ops:
  0.6 194.8 %copy-start = (f32[4,4,2]{1,2,0:T(2,128)S(1)}, f32[4,4,2]{1,2,0:T(2,128)}, u32[]{:S(2)}) copy-start(f32[4,4,2]{1,2,0:T(2,128)} %param.18) | copy-start | bytes 388
  0.6 8.9 %copy-start.26 = (s32[4,4,2]{1,2,0:T(2,128)S(1)}, s32[4,4,2]{1,2,0:T(2,128)}, u32[]{:S(2)}) copy-start(s32[4,4,2]{1,2,0:T(2,128)} %param.17) | copy-start | bytes 388
  1.8 19.1 %collective-permute-start = (bf16[1024,96]{1,0:T(8,128)(2,1)S(1)}, bf16[1024,96]{1,0:T(8,128)(2,1)S(1)}, u32[]{:S(2)}, u32[]{:S(2)}) collective-permute-start(bf16[1024,96]{1,0:T(8,128)(2,1)S(1)} %copy.176), channel_id=1, source_target_pairs={{0,2},{2,0},{1,3},{3,1},{4,6},{6,4},{5,7},{7,5},{8,10},{10,8},{9,1... | collective-permute-start | bytes 589832 | tf_op jit(solution)/shard_map/ppermute | solution.py:21
  5.4 4.3 %copy-start.24 = (bf16[4,4,8,128]{3,2,1,0:T(8,128)(2,1)}, bf16[4,4,8,128]{3,2,1,0:T(8,128)(2,1)S(1)}, u32[]{:S(2)}) copy-start(bf16[4,4,8,128]{3,2,1,0:T(8,128)(2,1)S(1)} %reshape.193) | copy-start | bytes 98308
  7.1 3.4 %copy-start.22 = (bf16[4,4,8,128]{3,2,1,0:T(8,128)(2,1)}, bf16[4,4,8,128]{3,2,1,0:T(8,128)(2,1)S(1)}, u32[]{:S(2)}) copy-start(bf16[4,4,8,128]{3,2,1,0:T(8,128)(2,1)S(1)} %reshape.194) | copy-start | bytes 98308
  10.5 30.5 %all-to-all-start = ((bf16[16,16,1152]{2,1,0:T(8,128)(2,1)}), bf16[16,16,1152]{2,1,0:T(8,128)(2,1)S(1)}, u32[]{:S(2)}, u32[]{:S(2)}) async-start(bf16[16,16,1152]{2,1,0:T(8,128)(2,1)} %broadcast_in_dim.18), calls=%async_computation | async-start | bytes 1179648 | tf_op jit(solution)/shard_map/all_to_all | solution.py:27
  21.2 2.0 collective-permute-start.1
  41.9 6.2 %copy-start.21 = (f32[4,64,384]{2,1,0:T(8,128)}, f32[4,64,384]{2,1,0:T(8,128)S(1)}, u32[]{:S(2)}) copy-start(f32[4,64,384]{2,1,0:T(8,128)S(1)} %fusion.5) | copy-start | bytes 1179652
  42.7 8.9 %collective-permute-start.2 = (f32[64,384]{1,0:T(8,128)}, f32[64,384]{1,0:T(8,128)}, u32[]{:S(2)}, u32[]{:S(2)}) collective-permute-start(f32[64,384]{1,0:T(8,128)} %get-tuple-element.43), channel_id=1, source_target_pairs={{0,64},{64,128},{128,192},{192,0},{1,65},{65,129},{129,193},{193,1... | collective-permute-start | bytes 294920 | tf_op jit(solution)/shard_map/ppermute | solution.py:21
  44.2 7.4 %collective-permute-start.3 = (f32[64,384]{1,0:T(8,128)}, f32[64,384]{1,0:T(8,128)}, u32[]{:S(2)}, u32[]{:S(2)}) collective-permute-start(f32[64,384]{1,0:T(8,128)} %get-tuple-element.45), channel_id=1, source_target_pairs={{0,128},{64,192},{128,0},{192,64},{1,129},{65,193},{129,1},{193,65... | collective-permute-start | bytes 294920 | tf_op jit(solution)/shard_map/ppermute | solution.py:21
  45.3 6.3 %collective-permute-start.4 = (f32[64,384]{1,0:T(8,128)}, f32[64,384]{1,0:T(8,128)}, u32[]{:S(2)}, u32[]{:S(2)}) collective-permute-start(f32[64,384]{1,0:T(8,128)} %get-tuple-element.44), channel_id=1, source_target_pairs={{0,192},{64,0},{128,64},{192,128},{1,193},{65,1},{129,65},{193,129... | collective-permute-start | bytes 294920 | tf_op jit(solution)/shard_map/ppermute | solution.py:21
  48.1 24.8 %copy-start.3 = (bf16[1,288,6144]{2,1,0:T(8,128)(2,1)S(1)}, bf16[1,288,6144]{2,1,0:T(8,128)(2,1)}, u32[]{:S(2)}) copy-start(bf16[1,288,6144]{2,1,0:T(8,128)(2,1)} %param.21) | copy-start | bytes 10616836
  52.7 0.6 copy-start.19
  71.4 18.9 %copy-start.4 = (bf16[4,8,16,384]{3,1,2,0:T(8,128)(2,1)}, bf16[4,8,16,384]{3,1,2,0:T(8,128)(2,1)S(1)}, u32[]{:S(2)}) copy-start(bf16[4,8,16,384]{3,1,2,0:T(8,128)(2,1)S(1)} %copy.208) | copy-start | bytes 1179652
  71.4 7.9 %collective-permute-start.6 = (bf16[32,6144]{1,0:T(8,128)(2,1)S(1)}, bf16[32,6144]{1,0:T(8,128)(2,1)S(1)}, u32[]{:S(2)}, u32[]{:S(2)}) collective-permute-start(bf16[32,6144]{1,0:T(8,128)(2,1)S(1)} %bitcast.103), channel_id=1, source_target_pairs={{0,192},{64,0},{128,64},{192,128},{1,193},{65,1},{129,65},{193,129... | collective-permute-start | bytes 1179656 | tf_op jit(solution)/shard_map/ppermute | solution.py:21
  72.9 55.1 %collective-permute-start.15 = (bf16[288,6144]{1,0:T(8,128)(2,1)S(1)}, bf16[288,6144]{1,0:T(8,128)(2,1)}, u32[]{:S(2)}, u32[]{:S(2)}) collective-permute-start(bf16[288,6144]{1,0:T(8,128)(2,1)S(1)} %bitcast.101), channel_id=1, source_target_pairs={{0,1},{1,0},{2,3},{3,2},{4,5},{5,4},{6,7},{7,6},{8,9},{9,8},{10,11... | collective-permute-start | bytes 10616840 | tf_op jit(solution)/shard_map/ppermute | solution.py:21
  72.9 29.9 %collective-permute-start.13 = (bf16[6144,288]{0,1:T(8,128)(2,1)}, bf16[6144,288]{0,1:T(8,128)(2,1)}, u32[]{:S(2)}, u32[]{:S(2)}) collective-permute-start(bf16[6144,288]{0,1:T(8,128)(2,1)} %bitcast.108), channel_id=1, source_target_pairs={{0,1},{1,0},{2,3},{3,2},{4,5},{5,4},{6,7},{7,6},{8,9},{9,8},{10,11... | collective-permute-start | bytes 10616840 | tf_op jit(solution)/shard_map/ppermute | solution.py:21
  73.4 48.3 %collective-permute-start.14 = (bf16[6144,288]{0,1:T(8,128)(2,1)}, bf16[6144,288]{0,1:T(8,128)(2,1)}, u32[]{:S(2)}, u32[]{:S(2)}) collective-permute-start(bf16[6144,288]{0,1:T(8,128)(2,1)} %bitcast.109), channel_id=1, source_target_pairs={{0,1},{1,0},{2,3},{3,2},{4,5},{5,4},{6,7},{7,6},{8,9},{9,8},{10,11... | collective-permute-start | bytes 10616840 | tf_op jit(solution)/shard_map/ppermute | solution.py:21
  73.4 15.2 %collective-permute-start.5 = (bf16[32,6144]{1,0:T(8,128)(2,1)S(1)}, bf16[32,6144]{1,0:T(8,128)(2,1)S(1)}, u32[]{:S(2)}, u32[]{:S(2)}) collective-permute-start(bf16[32,6144]{1,0:T(8,128)(2,1)S(1)} %bitcast.104), channel_id=1, source_target_pairs={{0,64},{64,128},{128,192},{192,0},{1,65},{65,129},{129,193},{193,1... | collective-permute-start | bytes 1179656 | tf_op jit(solution)/shard_map/ppermute | solution.py:21
  79.2 11.1 %copy-start.6 = (bf16[32,6144]{1,0:T(8,128)(2,1)}, bf16[32,6144]{1,0:T(8,128)(2,1)S(1)}, u32[]{:S(2)}) copy-start(bf16[32,6144]{1,0:T(8,128)(2,1)S(1)} %collective-permute-done.6.refs_2_) | copy-start | bytes 1179652
  79.2 7.8 %collective-permute-start.7 = (bf16[32,6144]{1,0:T(8,128)(2,1)S(1)}, bf16[32,6144]{1,0:T(8,128)(2,1)S(1)}, u32[]{:S(2)}, u32[]{:S(2)}) collective-permute-start(bf16[32,6144]{1,0:T(8,128)(2,1)S(1)} %bitcast.105), channel_id=1, source_target_pairs={{0,2},{2,0},{1,3},{3,1},{4,6},{6,4},{5,7},{7,5},{8,10},{10,8},{9,1... | collective-permute-start | bytes 1179656 | tf_op jit(solution)/shard_map/ppermute | solution.py:21
  87.0 10.0 %copy-start.10 = (bf16[32,6144]{1,0:T(8,128)(2,1)}, bf16[32,6144]{1,0:T(8,128)(2,1)S(1)}, u32[]{:S(2)}) copy-start(bf16[32,6144]{1,0:T(8,128)(2,1)S(1)} %collective-permute-done.7.refs_3_) | copy-start | bytes 1179652
  87.1 7.9 %collective-permute-start.9 = (bf16[32,6144]{1,0:T(8,128)(2,1)S(1)}, bf16[32,6144]{1,0:T(8,128)(2,1)S(1)}, u32[]{:S(2)}, u32[]{:S(2)}) collective-permute-start(bf16[32,6144]{1,0:T(8,128)(2,1)S(1)} %pad_maximum_fusion.3), channel_id=1, source_target_pairs={{0,192},{64,0},{128,64},{192,128},{1,193},{65,1},{129,65},{193,129... | collective-permute-start | bytes 1179656 | tf_op jit(solution)/shard_map/ppermute | solution.py:21
  88.6 6.3 %copy-start.8 = (bf16[32,6144]{1,0:T(8,128)(2,1)}, bf16[32,6144]{1,0:T(8,128)(2,1)S(1)}, u32[]{:S(2)}) copy-start(bf16[32,6144]{1,0:T(8,128)(2,1)S(1)} %collective-permute-done.5.refs_1_) | copy-start | bytes 1179652
  88.6 9.5 %collective-permute-start.8 = (bf16[32,6144]{1,0:T(8,128)(2,1)S(1)}, bf16[32,6144]{1,0:T(8,128)(2,1)S(1)}, u32[]{:S(2)}, u32[]{:S(2)}) collective-permute-start(bf16[32,6144]{1,0:T(8,128)(2,1)S(1)} %pad_maximum_fusion.2), channel_id=1, source_target_pairs={{0,64},{64,128},{128,192},{192,0},{1,65},{65,129},{129,193},{193,1... | collective-permute-start | bytes 1179656 | tf_op jit(solution)/shard_map/ppermute | solution.py:21
  94.9 3.2 %copy-start.12 = (bf16[32,6144]{1,0:T(8,128)(2,1)}, bf16[32,6144]{1,0:T(8,128)(2,1)S(1)}, u32[]{:S(2)}) copy-start(bf16[32,6144]{1,0:T(8,128)(2,1)S(1)} %collective-permute-done.9.refs_5_) | copy-start | bytes 1179652
  94.9 33.0 %collective-permute-start.10 = (bf16[32,6144]{1,0:T(8,128)(2,1)}, bf16[32,6144]{1,0:T(8,128)(2,1)}, u32[]{:S(2)}, u32[]{:S(2)}) collective-permute-start(bf16[32,6144]{1,0:T(8,128)(2,1)} %pad_maximum_fusion.4), channel_id=1, source_target_pairs={{0,2},{2,0},{1,3},{3,1},{4,6},{6,4},{5,7},{7,5},{8,10},{10,8},{9,1... | collective-permute-start | bytes 1179656 | tf_op jit(solution)/shard_map/ppermute | solution.py:21
  98.1 29.8 %collective-permute-start.12 = (bf16[16,6144]{1,0:T(8,128)(2,1)}, bf16[16,6144]{1,0:T(8,128)(2,1)}, u32[]{:S(2)}, u32[]{:S(2)}) collective-permute-start(bf16[16,6144]{1,0:T(8,128)(2,1)} %slice.221), channel_id=1, source_target_pairs={{0,192},{64,0},{128,64},{192,128},{1,193},{65,1},{129,65},{193,129... | collective-permute-start | bytes 589832 | tf_op jit(solution)/shard_map/ppermute | solution.py:21
  102.1 0.8 copy-start.14
  102.8 25.2 %collective-permute-start.11 = (bf16[16,6144]{1,0:T(8,128)(2,1)}, bf16[16,6144]{1,0:T(8,128)(2,1)}, u32[]{:S(2)}, u32[]{:S(2)}) collective-permute-start(bf16[16,6144]{1,0:T(8,128)(2,1)} %slice.220), channel_id=1, source_target_pairs={{0,64},{64,128},{128,192},{192,0},{1,65},{65,129},{129,193},{193,1... | collective-permute-start | bytes 589832 | tf_op jit(solution)/shard_map/ppermute | solution.py:21
  128.0 2.3 %copy-start.1 = (bf16[1,6144,288]{2,1,0:T(8,128)(2,1)S(1)}, bf16[1,6144,288]{2,1,0:T(8,128)(2,1)}, u32[]{:S(2)}) copy-start(bf16[1,6144,288]{2,1,0:T(8,128)(2,1)} %copy.182) | copy-start | bytes 10616836
  130.3 2.3 %copy-start.2 = (bf16[6144,288]{1,0:T(8,128)(2,1)S(1)}, bf16[6144,288]{1,0:T(8,128)(2,1)}, u32[]{:S(2)}) copy-start(bf16[6144,288]{1,0:T(8,128)(2,1)} %copy.186.refs_10_) | copy-start | bytes 10616836
  132.7 1.0 copy-start.5
  133.7 1.0 copy-start.7
  134.7 1.0 copy-start.9
  135.7 1.0 copy-start.11
  136.7 1.0 copy-start.13
  137.7 1.0 copy-start.15
  155.1 12.0 %copy-start.16 = (bf16[32,6144]{1,0:T(8,128)(2,1)}, bf16[32,6144]{1,0:T(8,128)(2,1)S(1)}, u32[]{:S(2)}) copy-start(bf16[32,6144]{1,0:T(8,128)(2,1)S(1)} %get-tuple-element.12) | copy-start | bytes 1179652
  155.1 7.7 %collective-permute-start.16 = (bf16[16,6144]{1,0:T(8,128)(2,1)S(1)}, bf16[16,6144]{1,0:T(8,128)(2,1)S(1)}, u32[]{:S(2)}, u32[]{:S(2)}) collective-permute-start(bf16[16,6144]{1,0:T(8,128)(2,1)S(1)} %get-tuple-element.15), channel_id=1, source_target_pairs={{0,192},{64,0},{128,64},{192,128},{1,193},{65,1},{129,65},{193,129... | collective-permute-start | bytes 589832 | tf_op jit(solution)/shard_map/ppermute | solution.py:21
  157.2 9.8 %collective-permute-start.18 = (bf16[32,6144]{1,0:T(8,128)(2,1)S(1)}, bf16[32,6144]{1,0:T(8,128)(2,1)S(1)}, u32[]{:S(2)}, u32[]{:S(2)}) collective-permute-start(bf16[32,6144]{1,0:T(8,128)(2,1)S(1)} %get-tuple-element.16), channel_id=1, source_target_pairs={{0,2},{2,0},{1,3},{3,1},{4,6},{6,4},{5,7},{7,5},{8,10},{10,8},{9,1... | collective-permute-start | bytes 1179656 | tf_op jit(solution)/shard_map/ppermute | solution.py:21
  158.5 8.3 %collective-permute-start.20 = (bf16[16,6144]{1,0:T(8,128)(2,1)S(1)}, bf16[16,6144]{1,0:T(8,128)(2,1)S(1)}, u32[]{:S(2)}, u32[]{:S(2)}) collective-permute-start(bf16[16,6144]{1,0:T(8,128)(2,1)S(1)} %get-tuple-element.19), channel_id=1, source_target_pairs={{0,64},{64,128},{128,192},{192,0},{1,65},{65,129},{129,193},{193,1... | collective-permute-start | bytes 589832 | tf_op jit(solution)/shard_map/ppermute | solution.py:21
  162.9 11.9 %collective-permute-start.17 = (bf16[32,6144]{1,0:T(8,128)(2,1)S(1)}, bf16[32,6144]{1,0:T(8,128)(2,1)S(1)}, u32[]{:S(2)}, u32[]{:S(2)}) collective-permute-start(bf16[32,6144]{1,0:T(8,128)(2,1)S(1)} %pad_maximum_fusion.5), channel_id=1, source_target_pairs={{0,192},{64,0},{128,64},{192,128},{1,193},{65,1},{129,65},{193,129... | collective-permute-start | bytes 1179656 | tf_op jit(solution)/shard_map/ppermute | solution.py:21
  166.9 11.5 %collective-permute-start.21 = (bf16[32,6144]{1,0:T(8,128)(2,1)S(1)}, bf16[32,6144]{1,0:T(8,128)(2,1)S(1)}, u32[]{:S(2)}, u32[]{:S(2)}) collective-permute-start(bf16[32,6144]{1,0:T(8,128)(2,1)S(1)} %pad_maximum_fusion.6), channel_id=1, source_target_pairs={{0,64},{64,128},{128,192},{192,0},{1,65},{65,129},{129,193},{193,1... | collective-permute-start | bytes 1179656 | tf_op jit(solution)/shard_map/ppermute | solution.py:21
  174.9 5.4 %copy-start.20 = (bf16[64,384]{1,0:T(8,128)(2,1)S(1)}, bf16[64,384]{1,0:T(8,128)(2,1)}, u32[]{:S(2)}) copy-start(bf16[64,384]{1,0:T(8,128)(2,1)} %copy-done.19) | copy-start | bytes 147460
  174.9 12.6 %copy-start.17 = (bf16[32,6144]{1,0:T(8,128)(2,1)S(1)}, bf16[32,6144]{1,0:T(8,128)(2,1)}, u32[]{:S(2)}) copy-start(bf16[32,6144]{1,0:T(8,128)(2,1)} %copy-done.16) | copy-start | bytes 1179652
  175.0 8.7 %collective-permute-start.19 = (bf16[32,6144]{1,0:T(8,128)(2,1)S(1)}, bf16[32,6144]{1,0:T(8,128)(2,1)S(1)}, u32[]{:S(2)}, u32[]{:S(2)}) collective-permute-start(bf16[32,6144]{1,0:T(8,128)(2,1)S(1)} %add_convert_fusion.4), channel_id=1, source_target_pairs={{0,192},{64,0},{128,64},{192,128},{1,193},{65,1},{129,65},{193,129... | collective-permute-start | bytes 1179656 | tf_op jit(solution)/shard_map/ppermute | solution.py:21
  178.5 8.9 %collective-permute-start.22 = (bf16[32,6144]{1,0:T(8,128)(2,1)S(1)}, bf16[32,6144]{1,0:T(8,128)(2,1)S(1)}, u32[]{:S(2)}, u32[]{:S(2)}) collective-permute-start(bf16[32,6144]{1,0:T(8,128)(2,1)S(1)} %add_convert_fusion.3), channel_id=1, source_target_pairs={{0,64},{64,128},{128,192},{192,0},{1,65},{65,129},{129,193},{193,1... | collective-permute-start | bytes 1179656 | tf_op jit(solution)/shard_map/ppermute | solution.py:21
  178.7 8.7 %collective-permute-start.23 = (bf16[32,6144]{1,0:T(8,128)(2,1)S(1)}, bf16[32,6144]{1,0:T(8,128)(2,1)S(1)}, u32[]{:S(2)}, u32[]{:S(2)}) collective-permute-start(bf16[32,6144]{1,0:T(8,128)(2,1)S(1)} %add_convert_fusion.2), channel_id=1, source_target_pairs={{0,2},{2,0},{1,3},{3,1},{4,6},{6,4},{5,7},{7,5},{8,10},{10,8},{9,1... | collective-permute-start | bytes 1179656 | tf_op jit(solution)/shard_map/ppermute | solution.py:21
  189.2 30.8 %copy-start.27 = (f32[4,8]{1,0:T(4,128)S(1)}, f32[4,8]{1,0:T(4,128)}, u32[]{:S(2)}) copy-start(f32[4,8]{1,0:T(4,128)} %get-tuple-element.64) | copy-start | bytes 388
  189.2 30.9 %copy-start.18 = (bf16[4,8,128,128]{3,2,1,0:T(8,128)(2,1)S(1)}, bf16[4,8,128,128]{3,2,1,0:T(8,128)(2,1)}, u32[]{:S(2)}) copy-start(bf16[4,8,128,128]{3,2,1,0:T(8,128)(2,1)} %param.15) | copy-start | bytes 3145732
  189.2 30.9 %copy-start.23 = (bf16[4,4,8,128]{3,2,1,0:T(8,128)(2,1)S(1)}, bf16[4,4,8,128]{3,2,1,0:T(8,128)(2,1)}, u32[]{:S(2)}) copy-start(bf16[4,4,8,128]{3,2,1,0:T(8,128)(2,1)} %copy-done.22) | copy-start | bytes 98308
  189.2 30.9 %copy-start.25 = (bf16[4,4,8,128]{3,2,1,0:T(8,128)(2,1)S(1)}, bf16[4,4,8,128]{3,2,1,0:T(8,128)(2,1)}, u32[]{:S(2)}) copy-start(bf16[4,4,8,128]{3,2,1,0:T(8,128)(2,1)} %copy-done.24) | copy-start | bytes 98308
  189.2 19.3 %all-to-all-start.2 = ((bf16[16,2,6912]{2,1,0:T(2,128)(2,1)}), bf16[16,2,6912]{2,1,0:T(2,128)(2,1)S(1)}, u32[]{:S(2)}, u32[]{:S(2)}) async-start(bf16[16,2,6912]{2,1,0:T(2,128)(2,1)} %pad_maximum_fusion.1), calls=%async_computation.2 | async-start | bytes 884736 | tf_op jit(solution)/shard_map/all_to_all | solution.py:246
  210.1 15.9 %all-to-all-start.3 = ((bf16[4,8,6144]{2,1,0:T(8,128)(2,1)}), bf16[4,8,6144]{2,1,0:T(8,128)(2,1)S(1)}, u32[]{:S(2)}, u32[]{:S(2)}) async-start(bf16[4,8,6144]{2,1,0:T(8,128)(2,1)} %broadcast_in_dim.19), calls=%async_computation.3 | async-start | bytes 786432 | tf_op jit(solution)/shard_map/all_to_all | solution.py:27

commit v3 on v2

--- a/solution.py
+++ b/solution.py
@@ -27,30 +27,63 @@
     return lax.all_to_all(copies, axis, split_axis=0, concat_axis=0, tiled=True)
 
 
-def attention(query_rows, key_rows, value_rows, forget, head_state):
+def split(array):
+    high = array.astype(BF16)
+    return high, (array - high.astype(F32)).astype(BF16)
+
+
+def attend_kernel(steps, rows, forget_ref, query_ref, key_ref, value_ref, state_ref, out_ref):
+    rate = forget_ref[pl.program_id(0)]
+    query, key, value = query_ref[...], key_ref[...], value_ref[...]
+    count = steps * rows
+    row_of = lax.broadcasted_iota(jnp.int32, (count, 1), 0)
+    step_of = (row_of // rows).astype(F32)
+    member = row_of % rows
+    from_state = jnp.zeros(out_ref.shape, F32)
+    for r in range(rows):
+        product = jnp.dot(query, state_ref[r, 0], preferred_element_type=F32)
+        from_state += jnp.where(member == r, product, 0.0)
+    one = lax.broadcasted_iota(jnp.int32, (count, count), 0)
+    other = lax.broadcasted_iota(jnp.int32, (count, count), 1)
+    lag = one // rows - other // rows
+    seen = (lag >= 0) & (one % rows == other % rows)
+    scale = jnp.where(seen, jnp.exp(-rate * jnp.maximum(lag, 0).astype(F32)), 0.0)
+    scores = across_lanes(query, key) * scale
+    from_steps = sum(jnp.dot(s, value, preferred_element_type=F32) for s in split(scores))
+    out_ref[...] = (jnp.exp(-rate * (step_of + 1.0)) * from_state + from_steps).astype(BF16)
+
+
+def attend(query_rows, key_rows, value_rows, forget, head_state):
     steps, rows, width = query_rows.shape
     heads = forget.shape[0]
     size = width // heads
-    shape = (steps, rows, heads, size)
-    query, key, value = (a.reshape(shape) for a in (query_rows, key_rows, value_rows))
-    times = jnp.arange(steps, dtype=F32)
+    count = steps * rows
+    lane_block = pl.BlockSpec((count, size), lambda i: (0, i))
+    return pl.pallas_call(
+        functools.partial(attend_kernel, steps, rows),
+        grid=(heads,),
+        in_specs=[
+            pl.BlockSpec(memory_space=pltpu.SMEM),
+            lane_block,
+            lane_block,
+            lane_block,
+            pl.BlockSpec((rows, 1, size, size), lambda i: (0, i, 0, 0)),
+        ],
+        out_specs=lane_block,
+        out_shape=jax.ShapeDtypeStruct((count, width), BF16),
+    )(forget, *(a.reshape(count, width) for a in (query_rows, key_rows, value_rows)), head_state)
+
+
+def last_state(key_rows, value_rows, forget, head_state):
+    steps, rows, width = key_rows.shape
+    heads = forget.shape[0]
+    shape = (steps, rows, heads, width // heads)
     power = jnp.exp(-forget[None, :] * jnp.arange(steps + 1, dtype=F32)[:, None])
-    lag = times[:, None] - times[None, :]
-    causal = jnp.where(
-        lag[..., None] >= 0, jnp.exp(-forget * jnp.maximum(lag, 0.0)[..., None]), 0.0
-    )
-    from_state = jnp.einsum("trhi,rhij->trhj", query, head_state, preferred_element_type=F32)
-    scores = jnp.einsum("trhi,srhi->tsrh", query, key, preferred_element_type=F32)
-    scores = scores * causal[:, :, None, :]
-    value_float = value.astype(F32)
-    from_steps = sum(scores[:, s, :, :, None] * value_float[s][None] for s in range(steps))
-    attended = power[1:, None, :, None] * from_state + from_steps
-    attended = attended.astype(BF16).reshape(steps * rows, width)
-    scaled_key = key.astype(F32) * power[steps - 1 :: -1][:steps, None, :, None]
+    scaled = key_rows.reshape(shape).astype(F32) * power[steps - 1 :: -1][:steps, None, :, None]
     state = power[steps][None, :, None, None] * head_state.astype(F32) + jnp.einsum(
-        "trhi,trhj->rhij", scaled_key, value_float, precision=EXACT
-    )
-    return attended, state.astype(BF16)
+        "trhi,trhj->rhij", scaled, value_rows.reshape(shape).astype(F32), precision=EXACT
+    )
+    return state.astype(BF16)
 
 
 def place(ids, experts, capacity):
@@ -103,35 +136,41 @@
     return add(own, shift(left, "head", -1), shift(right, "head", 1), shift(across, "zl", 1))
 
 
+def across_lanes(one, other):
+    return lax.dot_general(one, other, (((1,), (1,)), ((), ())), preferred_element_type=F32)
+
+
 def ffn_kernel(count, inner, *refs):
     rows, refs = refs[:count], refs[count:]
-    gate, up, down = refs[0:2], refs[2:4], refs[4:6]
-    outs, refs = refs[6 : 6 + count], refs[6 + count :]
-    gated, lifted, hidden = refs
+    wide, down, refs = refs[:4], refs[4:6], refs[6:]
+    outs, (sums, hidden) = refs[:count], refs[count:]
     step = pl.program_id(0)
-
-    @pl.when(step == 0)
-    def _():
-        gated[...] = jnp.zeros_like(gated)
-        lifted[...] = jnp.zeros_like(lifted)
 
     @pl.when(step < inner)
     def _():
         block = jnp.concatenate([r[...] for r in rows], axis=0)
-        for i in range(2):
-            gated[i] += jnp.dot(block, gate[i][...], preferred_element_type=F32)
-            lifted[i] += jnp.dot(block, up[i][...], preferred_element_type=F32)
+        weights = jnp.concatenate([w[...] for w in wide], axis=0)
+        product = across_lanes(block, weights)
+
+        @pl.when(step == 0)
+        def _():
+            sums[...] = product
+
+        @pl.when(step > 0)
+        def _():
+            sums[...] += product
 
     @pl.when(step == inner - 1)
     def _():
-        value = gated[...]
-        hidden[...] = (value / (1.0 + jnp.exp(-value)) * lifted[...]).astype(BF16)
+        value = sums[...]
+        width = value.shape[1] // 2
+        gated, lifted = value[:, :width], value[:, width:]
+        hidden[...] = (gated / (1.0 + jnp.exp(-gated)) * lifted).astype(BF16)
 
     @pl.when(step >= inner)
     def _():
-        total = jnp.dot(hidden[0], down[0][...], preferred_element_type=F32)
-        total += jnp.dot(hidden[1], down[1][...], preferred_element_type=F32)
-        total = total.astype(BF16)
+        weights = jnp.concatenate([w[...] for w in down], axis=0)
+        total = jnp.dot(hidden[...], weights, preferred_element_type=F32).astype(BF16)
         start = 0
         for out in outs:
             out[...] = total[start : start + out.shape[0]]
@@ -139,29 +178,28 @@
 
 
 def expert_ffn(parts, gate, up, down):
-    features, width = gate[0].shape
+    width, features = gate[0].shape
     total_rows = sum(p.shape[0] for p in parts)
     tile = min(features, 1024)
     inner = features // tile
 
     def first(i):
-        return jnp.minimum(i, inner - 1)
+        return (0, jnp.minimum(i, inner - 1))
 
     def second(i):
-        return jnp.maximum(i - inner, 0)
+        return (0, jnp.maximum(i - inner, 0))
 
     return pl.pallas_call(
         functools.partial(ffn_kernel, len(parts), inner),
         grid=(2 * inner,),
-        in_specs=[pl.BlockSpec((p.shape[0], tile), lambda i: (0, first(i))) for p in parts]
-        + [pl.BlockSpec((tile, width), lambda i: (first(i), 0))] * 4
-        + [pl.BlockSpec((width, tile), lambda i: (0, second(i)))] * 2,
-        out_specs=[pl.BlockSpec((p.shape[0], tile), lambda i: (0, second(i))) for p in parts],
+        in_specs=[pl.BlockSpec((p.shape[0], tile), first) for p in parts]
+        + [pl.BlockSpec((width, tile), first)] * 4
+        + [pl.BlockSpec((width, tile), second)] * 2,
+        out_specs=[pl.BlockSpec((p.shape[0], tile), second) for p in parts],
         out_shape=[jax.ShapeDtypeStruct(p.shape, BF16) for p in parts],
         scratch_shapes=[
-            pltpu.VMEM((2, total_rows, width), F32),
-            pltpu.VMEM((2, total_rows, width), F32),
-            pltpu.VMEM((2, total_rows, width), BF16),
+            pltpu.VMEM((total_rows, 4 * width), F32),
+            pltpu.VMEM((total_rows, 2 * width), BF16),
         ],
         compiler_params=pltpu.CompilerParams(vmem_limit_bytes=32 * 1024 * 1024),
         cost_estimate=pl.CostEstimate(
@@ -206,17 +244,19 @@
     head = lax.axis_index("head")
 
     gate, up, down = (
-        (w[0], shift(w[0], "core", 1)) for w in (gate_weight, up_weight, down_weight)
+        (w, shift(w, "core", 1)) for w in (gate_weight[0].T, up_weight[0].T, down_weight[0])
     )
     columns = block_columns(out_weight)
     width = columns.shape[1]
     features = width * blocks
 
-    attended, state_out = attention(query_rows, key_rows, value_rows, forget, head_state)
+    attended = attend(query_rows, key_rows, value_rows, forget, head_state)
+    state_out = last_state(key_rows, value_rows, forget, head_state)
 
     depth = attended.shape[1]
     ids = jnp.pad(route_ids.reshape(steps * rows, 2).astype(BF16), ((0, 0), (0, LANES - 2)))
     peers = spread(jnp.concatenate([attended, ids], axis=1), BLOCKS)
+    peers, gate, up, down = lax.optimization_barrier((peers, gate, up, down))
     peers = peers.reshape(blocks, steps, rows, depth + LANES)
     peer_ids = peers[..., depth : depth + 2].astype(jnp.int32)
     peers = jnp.transpose(peers[..., :depth], (1, 2, 0, 3)).reshape(steps * rows * blocks, depth)

time: 229 us -> 197 us (0.86)
  local copies, waits for them, and re-layouts: 50 us -> 17.3 us
  Pallas kernels: 16.4 us -> 21.3 us
  waiting for transfers between devices: 73.8 us -> 70.6 us
  other arithmetic: 7.98 us -> 10.9 us
    unnamed x61 -> x40, local copies, waits for them, and re-layouts: 25.9 us -> 3.97 us
    ppermute x2 -> x0, local copies, waits for them, and re-layouts: 12.6 us -> none  [shift(): return lax.ppermute(array, axis, pairs)]
    pallas_call x0 -> x1, Pallas kernels: none -> 6.2 us  [attend(): pl.pallas_call(functools.partial(attend_kernel, steps, rows), grid=(heads...]
    all_to_all x2, waiting for transfers between devices: 20.2 us -> 15.7 us  [spread(): return lax.all_to_all(copies, axis, split_axis=0, concat_axis=0, tiled=True)]
    dot_general x3 -> x1, matrix products: 4.69 us -> 2.92 us  [last_state(): jnp.einsum('trhi,trhj->rhij', scaled, value_rows.reshape(shape).astype(F3...]
  transfers between devices with their start and end apart: 27 -> 27, of which waited for: 14 -> 16; matrix products, arithmetic and copies ran while one was open for 19% -> 11% of each run, Pallas kernels for 0% -> 3%
where the time goes in v3:
time: 197 us; the launch traced here: 195 us
  waiting for transfers between devices  70.6 us (36%)
  starting transfers between devices  51.9 us (26%)
  Pallas kernels  21.3 us (11%)
  blocking collectives  17.7 us (9%)
  local copies, waits for them, and re-layouts  17.3 us (9%)
  other arithmetic  10.9 us (6%)
  matrix products  3.95 us (2%)
    ppermute x24, waiting for transfers between devices, shift(): return lax.ppermute(array, axis, pairs)  41.4 us
    ppermute x24, starting transfers between devices, shift(): return lax.ppermute(array, axis, pairs)  27.4 us
    all_to_all x2, starting transfers between devices, spread(): return lax.all_to_all(copies, axis, split_axis=0, concat_axis=0, tiled=True)  19.3 us
    all_to_all x1, blocking collectives, shards(): lax.all_to_all(packed, BLOCKS, split_axis=0, concat_axis=0, tiled=True)  17.7 us
    all_to_all x2, waiting for transfers between devices, spread(): return lax.all_to_all(copies, axis, split_axis=0, concat_axis=0, tiled=True)  15.7 us
    pallas_call x1, Pallas kernels, expert_ffn(): pl.pallas_call(functools.partial(ffn_kernel, len(parts), inner), grid=(2...  15.1 us
    all_to_all x1, waiting for transfers between devices, shards(): lax.all_to_all(jnp.concatenate([result, mixed], axis=2), BLOCKS, split_ax...  13.5 us
    pallas_call x1, Pallas kernels, attend(): pl.pallas_call(functools.partial(attend_kernel, steps, rows), grid=(heads...  6.2 us
  transfers between devices with their start and end apart: 27, of which 16 were waited for; matrix products, arithmetic and copies ran while one was open for 11% of the time, Pallas kernels for 3%

profile of v3, /device:TPU:2, one launch (start us, length us, event | category | flops | bytes accessed | tf_op | source)
XLA Modules:
  0.0 194.9 jit_solution(13381604608634910052)
XLA Ops:
  0.7 0.5 collective-permute-start.1
  1.3 1.8 copy.100
  3.1 1.9 collective-permute-start.3
  5.0 1.4 reshape.162.query_ref
  6.4 1.4 reshape.163.key_ref
  7.8 1.4 reshape.164.value_ref
  9.2 0.7 convert_element_type.154
  10.0 6.2 %shard_map.130 = bf16[16,1024]{1,0:T(8,128)(2,1)} custom-call(f32[8]{0:T(128)} %forget_ref.1, bf16[16,1024]{1,0:T(8,128)(2,1)} %reshape.162.query_ref, bf16[16,1024]{1,0:T(8,128)(2,1)} %reshape.163.key_ref, bf16[16,1024]{1,0:T(8,128)(2,1)} %reshape.164.value_ref, bf16[4,8,128,128]{3,2,1,0:T(8,128)(2,1)} %state_ref.1), custom_call_target="tpu_custom_call" | custom-call | tf_op jit(solution)/shard_map/pallas_call | solution.py:62
  16.2 0.8 fusion.15
  17.0 0.9 broadcast_in_dim.4
  17.8 10.3 %all-to-all-start = ((bf16[16,16,1152]{2,1,0:T(8,128)(2,1)}), bf16[16,16,1152]{2,1,0:T(8,128)(2,1)}, u32[]{:S(2)}, u32[]{:S(2)}) async-start(bf16[16,16,1152]{2,1,0:T(8,128)(2,1)} %broadcast_in_dim.4), calls=%async_computation | async-start | bytes 1179648 | tf_op jit(solution)/shard_map/all_to_all | solution.py:27
  28.2 1.1 broadcast_select_fusion.3
  29.3 0.7 copy-done.6
  30.0 1.1 pad_maximum_fusion
  31.1 2.2 %collective-permute-done.4 = bf16[1024,192]{1,0:T(8,128)(2,1)} collective-permute-done((bf16[1024,192]{1,0:T(8,128)(2,1)}, bf16[1024,192]{1,0:T(8,128)(2,1)}, u32[]{:S(2)}, u32[]{:S(2)}) %collective-permute-start.4) | collective-permute-done | bytes 393248 | tf_op jit(solution)/shard_map/ppermute | solution.py:21
  33.3 1.5 broadcast_select_fusion.1
  34.8 1.3 fusion.24
  36.2 12.9 %all-to-all-done = bf16[16,16,1152]{2,1,0:T(8,128)(2,1)} async-done(((bf16[16,16,1152]{2,1,0:T(8,128)(2,1)}), bf16[16,16,1152]{2,1,0:T(8,128)(2,1)}, u32[]{:S(2)}, u32[]{:S(2)}) %all-to-all-start) | async-done | bytes 589856 | tf_op jit(solution)/shard_map/all_to_all | solution.py:27
  49.1 1.2 copy.94
  50.5 0.7 fusion.1
  51.2 0.7 copy-done.10
  51.9 0.7 dynamic-slice_bitcast_fusion.2
  52.6 1.5 collective-permute-start.5
  54.1 1.1 collective-permute-start.6
  55.2 2.2 %collective-permute-start.7 = (f32[64,384]{1,0:T(8,128)}, f32[64,384]{1,0:T(8,128)}, u32[]{:S(2)}, u32[]{:S(2)}) collective-permute-start(f32[64,384]{1,0:T(8,128)} %get-tuple-element.58), channel_id=1, source_target_pairs={{0,192},{64,0},{128,64},{192,128},{1,193},{65,1},{129,65},{193,129... | collective-permute-start | bytes 294920 | tf_op jit(solution)/shard_map/ppermute | solution.py:21
  57.4 0.7 dynamic-slice_convert_fusion
  58.0 0.9 copy.95
  58.9 0.7 reduce-window_add_fusion
  59.6 0.9 copy.97
  60.4 0.9 convert_reduce_fusion
  61.4 1.1 fusion.11
  62.5 0.6 copy-done.8
  63.4 17.7 %all_to_all.20 = bf16[16,2,16,384]{3,2,1,0:T(8,128)(2,1)S(1)} all-to-all(bf16[16,2,16,384]{3,2,1,0:T(8,128)(2,1)S(1)} %add_convert_fusion.5), channel_id=1, replica_groups=mesh['head'=4,'y'=4,'zp'=4,'zl'=2,'core'=2] {'y','zp'}, dimensions={0} | all-to-all | bytes 786432 | tf_op jit(solution)/shard_map/all_to_all | solution.py:279
  81.4 1.5 collective-permute-start.9
  82.9 0.6 collective-permute-start.8
  83.5 0.9 collective-permute-start.10
  84.4 5.0 %collective-permute-done.9.refs_2_ = bf16[32,6144]{1,0:T(8,128)(2,1)S(1)} collective-permute-done((bf16[32,6144]{1,0:T(8,128)(2,1)S(1)}, bf16[32,6144]{1,0:T(8,128)(2,1)S(1)}, u32[]{:S(2)}, u32[]{:S(2)}) %collective-permute-start.9) | collective-permute-done | bytes 393248 | tf_op jit(solution)/shard_map/ppermute | solution.py:21
  89.4 1.9 collective-permute-done.10.refs_3_
  91.3 1.6 collective-permute-start.12
  93.0 0.8 collective-permute-start.11
  93.8 1.7 collective-permute-start.13
  95.5 5.2 %collective-permute-done.12.refs_5_ = bf16[32,6144]{1,0:T(8,128)(2,1)S(1)} collective-permute-done((bf16[32,6144]{1,0:T(8,128)(2,1)S(1)}, bf16[32,6144]{1,0:T(8,128)(2,1)S(1)}, u32[]{:S(2)}, u32[]{:S(2)}) %collective-permute-start.12) | collective-permute-done | bytes 393248 | tf_op jit(solution)/shard_map/ppermute | solution.py:21
  100.6 2.1 %collective-permute-start.15 = (bf16[16,6144]{1,0:T(8,128)(2,1)S(1)}, bf16[16,6144]{1,0:T(8,128)(2,1)S(1)}, u32[]{:S(2)}, u32[]{:S(2)}) collective-permute-start(bf16[16,6144]{1,0:T(8,128)(2,1)S(1)} %slice.177), channel_id=1, source_target_pairs={{0,192},{64,0},{128,64},{192,128},{1,193},{65,1},{129,65},{193,129... | collective-permute-start | bytes 589832 | tf_op jit(solution)/shard_map/ppermute | solution.py:21
  102.9 0.4 collective-permute-start.14
  103.3 3.0 %collective-permute-done.15.refs_8_ = bf16[16,6144]{1,0:T(8,128)(2,1)S(1)} collective-permute-done((bf16[16,6144]{1,0:T(8,128)(2,1)S(1)}, bf16[16,6144]{1,0:T(8,128)(2,1)S(1)}, u32[]{:S(2)}, u32[]{:S(2)}) %collective-permute-start.15) | collective-permute-done | bytes 196640 | tf_op jit(solution)/shard_map/ppermute | solution.py:21
  106.4 3.8 %collective-permute-done.14.refs_7_ = bf16[16,6144]{1,0:T(8,128)(2,1)S(1)} collective-permute-done((bf16[16,6144]{1,0:T(8,128)(2,1)S(1)}, bf16[16,6144]{1,0:T(8,128)(2,1)S(1)}, u32[]{:S(2)}, u32[]{:S(2)}) %collective-permute-start.14) | collective-permute-done | bytes 196640 | tf_op jit(solution)/shard_map/ppermute | solution.py:21
  110.1 15.1 %shard_map.131 = (bf16[32,6144]{1,0:T(8,128)(2,1)S(1)}, bf16[32,6144]{1,0:T(8,128)(2,1)S(1)}, bf16[32,6144]{1,0:T(8,128)(2,1)S(1)}, bf16[32,6144]{1,0:T(8,128)(2...) custom-call(bf16[32,6144]{1,0:T(8,128)(2,1)S(1)} %bitcast.79, ...), custom_call_target="tpu_custom_call" | custom-call | flops 5435817984 | bytes 27525120 | tf_op jit(solution)/shard_map/pallas_call | solution.py:192
  125.3 3.3 %collective-permute-start.16 = (bf16[16,6144]{1,0:T(8,128)(2,1)S(1)}, bf16[16,6144]{1,0:T(8,128)(2,1)S(1)}, u32[]{:S(2)}, u32[]{:S(2)}) collective-permute-start(bf16[16,6144]{1,0:T(8,128)(2,1)S(1)} %get-tuple-element.29), channel_id=1, source_target_pairs={{0,192},{64,0},{128,64},{192,128},{1,193},{65,1},{129,65},{193,129... | collective-permute-start | bytes 589832 | tf_op jit(solution)/shard_map/ppermute | solution.py:21
  128.9 4.2 %collective-permute-done.16 = bf16[16,6144]{1,0:T(8,128)(2,1)S(1)} collective-permute-done((bf16[16,6144]{1,0:T(8,128)(2,1)S(1)}, bf16[16,6144]{1,0:T(8,128)(2,1)S(1)}, u32[]{:S(2)}, u32[]{:S(2)}) %collective-permute-start.16) | collective-permute-done | bytes 196640 | tf_op jit(solution)/shard_map/ppermute | solution.py:21
  133.3 2.5 %collective-permute-start.17 = (bf16[32,6144]{1,0:T(8,128)(2,1)S(1)}, bf16[32,6144]{1,0:T(8,128)(2,1)S(1)}, u32[]{:S(2)}, u32[]{:S(2)}) collective-permute-start(bf16[32,6144]{1,0:T(8,128)(2,1)S(1)} %pad_maximum_fusion.5), channel_id=1, source_target_pairs={{0,192},{64,0},{128,64},{192,128},{1,193},{65,1},{129,65},{193,129... | collective-permute-start | bytes 1179656 | tf_op jit(solution)/shard_map/ppermute | solution.py:21
  136.5 8.3 %collective-permute-done.17 = bf16[32,6144]{1,0:T(8,128)(2,1)S(1)} collective-permute-done((bf16[32,6144]{1,0:T(8,128)(2,1)S(1)}, bf16[32,6144]{1,0:T(8,128)(2,1)S(1)}, u32[]{:S(2)}, u32[]{:S(2)}) %collective-permute-start.17) | collective-permute-done | bytes 393248 | tf_op jit(solution)/shard_map/ppermute | solution.py:21
  145.0 2.2 %collective-permute-start.19 = (bf16[32,6144]{1,0:T(8,128)(2,1)S(1)}, bf16[32,6144]{1,0:T(8,128)(2,1)S(1)}, u32[]{:S(2)}, u32[]{:S(2)}) collective-permute-start(bf16[32,6144]{1,0:T(8,128)(2,1)S(1)} %add_convert_fusion.4), channel_id=1, source_target_pairs={{0,192},{64,0},{128,64},{192,128},{1,193},{65,1},{129,65},{193,129... | collective-permute-start | bytes 1179656 | tf_op jit(solution)/shard_map/ppermute | solution.py:21
  147.1 0.7 collective-permute-done.21
  148.1 1.6 collective-permute-start.23
  150.1 2.9 %collective-permute-done.19 = bf16[32,6144]{1,0:T(8,128)(2,1)S(1)} collective-permute-done((bf16[32,6144]{1,0:T(8,128)(2,1)S(1)}, bf16[32,6144]{1,0:T(8,128)(2,1)S(1)}, u32[]{:S(2)}, u32[]{:S(2)}) %collective-permute-start.19) | collective-permute-done | bytes 393248 | tf_op jit(solution)/shard_map/ppermute | solution.py:21
  153.0 3.8 %collective-permute-done.22 = bf16[32,6144]{1,0:T(8,128)(2,1)S(1)} collective-permute-done((bf16[32,6144]{1,0:T(8,128)(2,1)S(1)}, bf16[32,6144]{1,0:T(8,128)(2,1)S(1)}, u32[]{:S(2)}, u32[]{:S(2)}) %collective-permute-start.22) | collective-permute-done | bytes 393248 | tf_op jit(solution)/shard_map/ppermute | solution.py:21
  157.4 1.2 pad_maximum_fusion.1
  158.6 5.2 %all-to-all-start.2 = ((bf16[16,2,6912]{2,1,0:T(2,128)(2,1)}), bf16[16,2,6912]{2,1,0:T(2,128)(2,1)S(1)}, u32[]{:S(2)}, u32[]{:S(2)}) async-start(bf16[16,2,6912]{2,1,0:T(2,128)(2,1)} %pad_maximum_fusion.1), calls=%async_computation.2 | async-start | bytes 884736 | tf_op jit(solution)/shard_map/all_to_all | solution.py:286
  164.1 13.5 %all-to-all-done.2 = bf16[16,2,6912]{2,1,0:T(2,128)(2,1)S(1)} async-done(((bf16[16,2,6912]{2,1,0:T(2,128)(2,1)}), bf16[16,2,6912]{2,1,0:T(2,128)(2,1)S(1)}, u32[]{:S(2)}, u32[]{:S(2)}) %all-to-all-start.2) | async-done | bytes 442400 | tf_op jit(solution)/shard_map/all_to_all | solution.py:286
  178.4 0.8 broadcast_in_dim.5
  179.2 8.9 %all-to-all-start.3 = ((bf16[4,8,6144]{2,1,0:T(8,128)(2,1)}), bf16[4,8,6144]{2,1,0:T(8,128)(2,1)S(1)}, u32[]{:S(2)}, u32[]{:S(2)}) async-start(bf16[4,8,6144]{2,1,0:T(8,128)(2,1)} %broadcast_in_dim.5), calls=%async_computation.3 | async-start | bytes 786432 | tf_op jit(solution)/shard_map/all_to_all | solution.py:27
  188.3 2.9 %add_convert_fusion = bf16[4,8,128,128]{3,2,1,0:T(8,128)(2,1)} fusion(bf16[4,8,128,128]{3,2,1,0:T(8,128)(2,1)S(1)} %copy-done.5, f32[8]{0:T(128)S(1)} %slice_bitcast_fusion.4, f32[4,4,8,128]{3,2,1,0:T(8,128)S(1)} %reshape.173, bf16[4,4,8,128]{3,2,1,0:T(8,128)(2,1)S(1)} %reshape.172, f32[4,8]{0,1:T(8,128)S(1)} %copy.111), kind=kOutput, calls=%fused_computation.2 | convolution fusion | flops 27279360 | bytes 2195616 | tf_op jit(solution)/shard_map/trhi,trhj->rhij/dot_general | solution.py:83
  191.2 2.8 %all-to-all-done.3 = bf16[4,8,6144]{2,1,0:T(8,128)(2,1)S(1)} async-done(((bf16[4,8,6144]{2,1,0:T(8,128)(2,1)}), bf16[4,8,6144]{2,1,0:T(8,128)(2,1)S(1)}, u32[]{:S(2)}, u32[]{:S(2)}) %all-to-all-start.3) | async-done | bytes 393248 | tf_op jit(solution)/shard_map/all_to_all | solution.py:27
  194.1 0.9 fusion.26
  (116 shorter events, 5.1 us)
Async XLA Ops:
  0.6 163.3 %copy-start = (f32[4,4,2]{1,2,0:T(2,128)S(1)}, f32[4,4,2]{1,2,0:T(2,128)}, u32[]{:S(2)}) copy-start(f32[4,4,2]{1,2,0:T(2,128)} %param.18) | copy-start | bytes 388
  0.6 48.4 %collective-permute-start = (bf16[288,6144]{1,0:T(8,128)(2,1)}, bf16[288,6144]{1,0:T(8,128)(2,1)S(1)}, u32[]{:S(2)}, u32[]{:S(2)}) collective-permute-start(bf16[288,6144]{1,0:T(8,128)(2,1)} %bitcast.72), channel_id=1, source_target_pairs={{0,1},{1,0},{2,3},{3,2},{4,5},{5,4},{6,7},{7,6},{8,9},{9,8},{10,11... | collective-permute-start | bytes 10616840 | tf_op jit(solution)/shard_map/ppermute | solution.py:21
  0.7 48.4 %collective-permute-start.1 = (bf16[288,6144]{1,0:T(8,128)(2,1)}, bf16[288,6144]{1,0:T(8,128)(2,1)}, u32[]{:S(2)}, u32[]{:S(2)}) collective-permute-start(bf16[288,6144]{1,0:T(8,128)(2,1)} %bitcast.74), channel_id=1, source_target_pairs={{0,1},{1,0},{2,3},{3,2},{4,5},{5,4},{6,7},{7,6},{8,9},{9,8},{10,11... | collective-permute-start | bytes 10616840 | tf_op jit(solution)/shard_map/ppermute | solution.py:21
  1.2 47.9 %collective-permute-start.2 = (bf16[288,6144]{1,0:T(8,128)(2,1)}, bf16[288,6144]{1,0:T(8,128)(2,1)}, u32[]{:S(2)}, u32[]{:S(2)}) collective-permute-start(bf16[288,6144]{1,0:T(8,128)(2,1)} %bitcast.80), channel_id=1, source_target_pairs={{0,1},{1,0},{2,3},{3,2},{4,5},{5,4},{6,7},{7,6},{8,9},{9,8},{10,11... | collective-permute-start | bytes 10616840 | tf_op jit(solution)/shard_map/ppermute | solution.py:21
  3.1 25.1 %collective-permute-start.3 = (bf16[1024,96]{1,0:T(8,128)(2,1)}, bf16[1024,96]{1,0:T(8,128)(2,1)}, u32[]{:S(2)}, u32[]{:S(2)}) collective-permute-start(bf16[1024,96]{1,0:T(8,128)(2,1)} %copy.100), channel_id=1, source_target_pairs={{0,2},{2,0},{1,3},{3,1},{4,6},{6,4},{5,7},{7,5},{8,10},{10,8},{9,1... | collective-permute-start | bytes 589832 | tf_op jit(solution)/shard_map/ppermute | solution.py:21
  17.8 31.2 %all-to-all-start = ((bf16[16,16,1152]{2,1,0:T(8,128)(2,1)}), bf16[16,16,1152]{2,1,0:T(8,128)(2,1)}, u32[]{:S(2)}, u32[]{:S(2)}) async-start(bf16[16,16,1152]{2,1,0:T(8,128)(2,1)} %broadcast_in_dim.4), calls=%async_computation | async-start | bytes 1179648 | tf_op jit(solution)/shard_map/all_to_all | solution.py:27
  29.3 0.7 copy-start.6
  29.3 1.8 copy-start.7
  31.1 2.3 %collective-permute-start.4 = (bf16[1024,192]{1,0:T(8,128)(2,1)}, bf16[1024,192]{1,0:T(8,128)(2,1)}, u32[]{:S(2)}, u32[]{:S(2)}) collective-permute-start(bf16[1024,192]{1,0:T(8,128)(2,1)} %pad_maximum_fusion), channel_id=1, source_target_pairs={{0,1},{1,0},{2,3},{3,2},{4,5},{5,4},{6,7},{7,6},{8,9},{9,8},{10,11... | collective-permute-start | bytes 1179656 | tf_op jit(solution)/shard_map/ppermute | solution.py:21
  49.1 1.4 copy-start.11
  49.1 1.4 copy-start.12
  49.1 1.4 copy-start.13
  49.1 1.4 copy-start.14
  51.2 0.7 copy-start.10
  52.6 8.8 %collective-permute-start.5 = (f32[64,384]{1,0:T(8,128)}, f32[64,384]{1,0:T(8,128)}, u32[]{:S(2)}, u32[]{:S(2)}) collective-permute-start(f32[64,384]{1,0:T(8,128)} %get-tuple-element.57), channel_id=1, source_target_pairs={{0,64},{64,128},{128,192},{192,0},{1,65},{65,129},{129,193},{193,1... | collective-permute-start | bytes 294920 | tf_op jit(solution)/shard_map/ppermute | solution.py:21
  54.1 7.3 %collective-permute-start.6 = (f32[64,384]{1,0:T(8,128)}, f32[64,384]{1,0:T(8,128)}, u32[]{:S(2)}, u32[]{:S(2)}) collective-permute-start(f32[64,384]{1,0:T(8,128)} %get-tuple-element.59), channel_id=1, source_target_pairs={{0,128},{64,192},{128,0},{192,64},{1,129},{65,193},{129,1},{193,65... | collective-permute-start | bytes 294920 | tf_op jit(solution)/shard_map/ppermute | solution.py:21
  55.2 6.2 %collective-permute-start.7 = (f32[64,384]{1,0:T(8,128)}, f32[64,384]{1,0:T(8,128)}, u32[]{:S(2)}, u32[]{:S(2)}) collective-permute-start(f32[64,384]{1,0:T(8,128)} %get-tuple-element.58), channel_id=1, source_target_pairs={{0,192},{64,0},{128,64},{192,128},{1,193},{65,1},{129,65},{193,129... | collective-permute-start | bytes 294920 | tf_op jit(solution)/shard_map/ppermute | solution.py:21
  62.5 0.6 copy-start.8
  81.1 29.0 %copy-start.2 = (bf16[1,6144,288]{1,2,0:T(8,128)(2,1)S(1)}, bf16[1,6144,288]{1,2,0:T(8,128)(2,1)}, u32[]{:S(2)}) copy-start(bf16[1,6144,288]{1,2,0:T(8,128)(2,1)} %param.20) | copy-start | bytes 10616836
  81.4 8.0 %collective-permute-start.9 = (bf16[32,6144]{1,0:T(8,128)(2,1)S(1)}, bf16[32,6144]{1,0:T(8,128)(2,1)S(1)}, u32[]{:S(2)}, u32[]{:S(2)}) collective-permute-start(bf16[32,6144]{1,0:T(8,128)(2,1)S(1)} %bitcast.76), channel_id=1, source_target_pairs={{0,192},{64,0},{128,64},{192,128},{1,193},{65,1},{129,65},{193,129... | collective-permute-start | bytes 1179656 | tf_op jit(solution)/shard_map/ppermute | solution.py:21
  82.9 10.0 %collective-permute-start.8 = (bf16[32,6144]{1,0:T(8,128)(2,1)S(1)}, bf16[32,6144]{1,0:T(8,128)(2,1)S(1)}, u32[]{:S(2)}, u32[]{:S(2)}) collective-permute-start(bf16[32,6144]{1,0:T(8,128)(2,1)S(1)} %bitcast.77), channel_id=1, source_target_pairs={{0,64},{64,128},{128,192},{192,0},{1,65},{65,129},{129,193},{193,1... | collective-permute-start | bytes 1179656 | tf_op jit(solution)/shard_map/ppermute | solution.py:21
  83.5 7.8 %collective-permute-start.10 = (bf16[32,6144]{1,0:T(8,128)(2,1)S(1)}, bf16[32,6144]{1,0:T(8,128)(2,1)S(1)}, u32[]{:S(2)}, u32[]{:S(2)}) collective-permute-start(bf16[32,6144]{1,0:T(8,128)(2,1)S(1)} %bitcast.78), channel_id=1, source_target_pairs={{0,2},{2,0},{1,3},{3,1},{4,6},{6,4},{5,7},{7,5},{8,10},{10,8},{9,1... | collective-permute-start | bytes 1179656 | tf_op jit(solution)/shard_map/ppermute | solution.py:21
  91.3 18.9 %copy-start.1 = (bf16[1,6144,288]{1,2,0:T(8,128)(2,1)S(1)}, bf16[1,6144,288]{1,2,0:T(8,128)(2,1)}, u32[]{:S(2)}) copy-start(bf16[1,6144,288]{1,2,0:T(8,128)(2,1)} %param.19) | copy-start | bytes 10616836
  91.3 9.3 %collective-permute-start.12 = (bf16[32,6144]{1,0:T(8,128)(2,1)S(1)}, bf16[32,6144]{1,0:T(8,128)(2,1)S(1)}, u32[]{:S(2)}, u32[]{:S(2)}) collective-permute-start(bf16[32,6144]{1,0:T(8,128)(2,1)S(1)} %pad_maximum_fusion.3), channel_id=1, source_target_pairs={{0,192},{64,0},{128,64},{192,128},{1,193},{65,1},{129,65},{193,129... | collective-permute-start | bytes 1179656 | tf_op jit(solution)/shard_map/ppermute | solution.py:21
  93.0 9.9 %collective-permute-start.11 = (bf16[32,6144]{1,0:T(8,128)(2,1)S(1)}, bf16[32,6144]{1,0:T(8,128)(2,1)S(1)}, u32[]{:S(2)}, u32[]{:S(2)}) collective-permute-start(bf16[32,6144]{1,0:T(8,128)(2,1)S(1)} %pad_maximum_fusion.2), channel_id=1, source_target_pairs={{0,64},{64,128},{128,192},{192,0},{1,65},{65,129},{129,193},{193,1... | collective-permute-start | bytes 1179656 | tf_op jit(solution)/shard_map/ppermute | solution.py:21
  93.8 9.6 %collective-permute-start.13 = (bf16[32,6144]{1,0:T(8,128)(2,1)S(1)}, bf16[32,6144]{1,0:T(8,128)(2,1)S(1)}, u32[]{:S(2)}, u32[]{:S(2)}) collective-permute-start(bf16[32,6144]{1,0:T(8,128)(2,1)S(1)} %pad_maximum_fusion.4), channel_id=1, source_target_pairs={{0,2},{2,0},{1,3},{3,1},{4,6},{6,4},{5,7},{7,5},{8,10},{10,8},{9,1... | collective-permute-start | bytes 1179656 | tf_op jit(solution)/shard_map/ppermute | solution.py:21
  100.6 5.7 %collective-permute-start.15 = (bf16[16,6144]{1,0:T(8,128)(2,1)S(1)}, bf16[16,6144]{1,0:T(8,128)(2,1)S(1)}, u32[]{:S(2)}, u32[]{:S(2)}) collective-permute-start(bf16[16,6144]{1,0:T(8,128)(2,1)S(1)} %slice.177), channel_id=1, source_target_pairs={{0,192},{64,0},{128,64},{192,128},{1,193},{65,1},{129,65},{193,129... | collective-permute-start | bytes 589832 | tf_op jit(solution)/shard_map/ppermute | solution.py:21
  102.9 7.2 %collective-permute-start.14 = (bf16[16,6144]{1,0:T(8,128)(2,1)S(1)}, bf16[16,6144]{1,0:T(8,128)(2,1)S(1)}, u32[]{:S(2)}, u32[]{:S(2)}) collective-permute-start(bf16[16,6144]{1,0:T(8,128)(2,1)S(1)} %slice.176), channel_id=1, source_target_pairs={{0,64},{64,128},{128,192},{192,0},{1,65},{65,129},{129,193},{193,1... | collective-permute-start | bytes 589832 | tf_op jit(solution)/shard_map/ppermute | solution.py:21
  125.2 11.2 %copy-start.3 = (bf16[32,6144]{1,0:T(8,128)(2,1)}, bf16[32,6144]{1,0:T(8,128)(2,1)S(1)}, u32[]{:S(2)}) copy-start(bf16[32,6144]{1,0:T(8,128)(2,1)S(1)} %get-tuple-element.26) | copy-start | bytes 1179652
  125.3 7.9 %collective-permute-start.16 = (bf16[16,6144]{1,0:T(8,128)(2,1)S(1)}, bf16[16,6144]{1,0:T(8,128)(2,1)S(1)}, u32[]{:S(2)}, u32[]{:S(2)}) collective-permute-start(bf16[16,6144]{1,0:T(8,128)(2,1)S(1)} %get-tuple-element.29), channel_id=1, source_target_pairs={{0,192},{64,0},{128,64},{192,128},{1,193},{65,1},{129,65},{193,129... | collective-permute-start | bytes 589832 | tf_op jit(solution)/shard_map/ppermute | solution.py:21
  128.6 7.9 %collective-permute-start.18 = (bf16[32,6144]{1,0:T(8,128)(2,1)S(1)}, bf16[32,6144]{1,0:T(8,128)(2,1)S(1)}, u32[]{:S(2)}, u32[]{:S(2)}) collective-permute-start(bf16[32,6144]{1,0:T(8,128)(2,1)S(1)} %get-tuple-element.30), channel_id=1, source_target_pairs={{0,2},{2,0},{1,3},{3,1},{4,6},{6,4},{5,7},{7,5},{8,10},{10,8},{9,1... | collective-permute-start | bytes 1179656 | tf_op jit(solution)/shard_map/ppermute | solution.py:21
  128.9 6.9 %collective-permute-start.20 = (bf16[16,6144]{1,0:T(8,128)(2,1)S(1)}, bf16[16,6144]{1,0:T(8,128)(2,1)S(1)}, u32[]{:S(2)}, u32[]{:S(2)}) collective-permute-start(bf16[16,6144]{1,0:T(8,128)(2,1)S(1)} %get-tuple-element.33), channel_id=1, source_target_pairs={{0,64},{64,128},{128,192},{192,0},{1,65},{65,129},{129,193},{193,1... | collective-permute-start | bytes 589832 | tf_op jit(solution)/shard_map/ppermute | solution.py:21
  133.3 11.5 %collective-permute-start.17 = (bf16[32,6144]{1,0:T(8,128)(2,1)S(1)}, bf16[32,6144]{1,0:T(8,128)(2,1)S(1)}, u32[]{:S(2)}, u32[]{:S(2)}) collective-permute-start(bf16[32,6144]{1,0:T(8,128)(2,1)S(1)} %pad_maximum_fusion.5), channel_id=1, source_target_pairs={{0,192},{64,0},{128,64},{192,128},{1,193},{65,1},{129,65},{193,129... | collective-permute-start | bytes 1179656 | tf_op jit(solution)/shard_map/ppermute | solution.py:21
  135.9 11.9 %collective-permute-start.21 = (bf16[32,6144]{1,0:T(8,128)(2,1)S(1)}, bf16[32,6144]{1,0:T(8,128)(2,1)S(1)}, u32[]{:S(2)}, u32[]{:S(2)}) collective-permute-start(bf16[32,6144]{1,0:T(8,128)(2,1)S(1)} %pad_maximum_fusion.6), channel_id=1, source_target_pairs={{0,64},{64,128},{128,192},{192,0},{1,65},{65,129},{129,193},{193,1... | collective-permute-start | bytes 1179656 | tf_op jit(solution)/shard_map/ppermute | solution.py:21
  144.8 5.0 %copy-start.17 = (s32[4,4,2]{1,2,0:T(2,128)S(1)}, s32[4,4,2]{1,2,0:T(2,128)}, u32[]{:S(2)}) copy-start(s32[4,4,2]{1,2,0:T(2,128)} %param.17) | copy-start | bytes 388
  144.8 5.2 %copy-start.9 = (bf16[64,384]{1,0:T(8,128)(2,1)S(1)}, bf16[64,384]{1,0:T(8,128)(2,1)}, u32[]{:S(2)}) copy-start(bf16[64,384]{1,0:T(8,128)(2,1)} %copy-done.8) | copy-start | bytes 147460
  144.8 12.0 %copy-start.4 = (bf16[32,6144]{1,0:T(8,128)(2,1)S(1)}, bf16[32,6144]{1,0:T(8,128)(2,1)}, u32[]{:S(2)}) copy-start(bf16[32,6144]{1,0:T(8,128)(2,1)} %copy-done.3) | copy-start | bytes 1179652
  145.0 8.1 %collective-permute-start.19 = (bf16[32,6144]{1,0:T(8,128)(2,1)S(1)}, bf16[32,6144]{1,0:T(8,128)(2,1)S(1)}, u32[]{:S(2)}, u32[]{:S(2)}) collective-permute-start(bf16[32,6144]{1,0:T(8,128)(2,1)S(1)} %add_convert_fusion.4), channel_id=1, source_target_pairs={{0,192},{64,0},{128,64},{192,128},{1,193},{65,1},{129,65},{193,129... | collective-permute-start | bytes 1179656 | tf_op jit(solution)/shard_map/ppermute | solution.py:21
  148.0 8.8 %collective-permute-start.22 = (bf16[32,6144]{1,0:T(8,128)(2,1)S(1)}, bf16[32,6144]{1,0:T(8,128)(2,1)S(1)}, u32[]{:S(2)}, u32[]{:S(2)}) collective-permute-start(bf16[32,6144]{1,0:T(8,128)(2,1)S(1)} %add_convert_fusion.3), channel_id=1, source_target_pairs={{0,64},{64,128},{128,192},{192,0},{1,65},{65,129},{129,193},{193,1... | collective-permute-start | bytes 1179656 | tf_op jit(solution)/shard_map/ppermute | solution.py:21
  148.1 8.7 %collective-permute-start.23 = (bf16[32,6144]{1,0:T(8,128)(2,1)S(1)}, bf16[32,6144]{1,0:T(8,128)(2,1)S(1)}, u32[]{:S(2)}, u32[]{:S(2)}) collective-permute-start(bf16[32,6144]{1,0:T(8,128)(2,1)S(1)} %add_convert_fusion.2), channel_id=1, source_target_pairs={{0,2},{2,0},{1,3},{3,1},{4,6},{6,4},{5,7},{7,5},{8,10},{10,8},{9,1... | collective-permute-start | bytes 1179656 | tf_op jit(solution)/shard_map/ppermute | solution.py:21
  156.8 7.1 %copy-start.18 = (f32[8]{0:T(128)S(1)}, f32[8]{0:T(128)}, u32[]{:S(2)}) copy-start(f32[8]{0:T(128)} %forget_ref.1) | copy-start | bytes 100
  158.6 29.6 %copy-start.15 = (bf16[4,4,1024]{2,1,0:T(4,128)(2,1)S(1)}, bf16[4,4,1024]{2,1,0:T(4,128)(2,1)}, u32[]{:S(2)}) copy-start(bf16[4,4,1024]{2,1,0:T(4,128)(2,1)} %param.12) | copy-start | bytes 98308
  158.6 29.6 %copy-start.16 = (bf16[4,4,1024]{2,1,0:T(4,128)(2,1)S(1)}, bf16[4,4,1024]{2,1,0:T(4,128)(2,1)}, u32[]{:S(2)}) copy-start(bf16[4,4,1024]{2,1,0:T(4,128)(2,1)} %param.13) | copy-start | bytes 98308
  158.6 29.7 %copy-start.5 = (bf16[4,8,128,128]{3,2,1,0:T(8,128)(2,1)S(1)}, bf16[4,8,128,128]{3,2,1,0:T(8,128)(2,1)}, u32[]{:S(2)}) copy-start(bf16[4,8,128,128]{3,2,1,0:T(8,128)(2,1)} %state_ref.1) | copy-start | bytes 3145732
  158.6 19.0 %all-to-all-start.2 = ((bf16[16,2,6912]{2,1,0:T(2,128)(2,1)}), bf16[16,2,6912]{2,1,0:T(2,128)(2,1)S(1)}, u32[]{:S(2)}, u32[]{:S(2)}) async-start(bf16[16,2,6912]{2,1,0:T(2,128)(2,1)} %pad_maximum_fusion.1), calls=%async_computation.2 | async-start | bytes 884736 | tf_op jit(solution)/shard_map/all_to_all | solution.py:286
  179.2 14.9 %all-to-all-start.3 = ((bf16[4,8,6144]{2,1,0:T(8,128)(2,1)}), bf16[4,8,6144]{2,1,0:T(8,128)(2,1)S(1)}, u32[]{:S(2)}, u32[]{:S(2)}) async-start(bf16[4,8,6144]{2,1,0:T(8,128)(2,1)} %broadcast_in_dim.5), calls=%async_computation.3 | async-start | bytes 786432 | tf_op jit(solution)/shard_map/all_to_all | solution.py:27

commit v4 on v2

--- a/solution.py
+++ b/solution.py
@@ -7,8 +7,9 @@
 from jax.experimental.pallas import tpu as pltpu
 from jax.sharding import Mesh, PartitionSpec as P
 
-BLOCKS = ("y", "zp")
-EXPERT = ("y", "zp", "zl", "core")
+BLOCKS = ("yh", "yl", "zp")
+PEERS = ("yh", "zp")
+EXPERT = BLOCKS + ("zl", "core")
 BF16 = jnp.bfloat16
 F32 = jnp.float32
 LANES = 128
@@ -103,35 +104,41 @@
     return add(own, shift(left, "head", -1), shift(right, "head", 1), shift(across, "zl", 1))
 
 
+def across_lanes(one, other):
+    return lax.dot_general(one, other, (((1,), (1,)), ((), ())), preferred_element_type=F32)
+
+
 def ffn_kernel(count, inner, *refs):
     rows, refs = refs[:count], refs[count:]
-    gate, up, down = refs[0:2], refs[2:4], refs[4:6]
-    outs, refs = refs[6 : 6 + count], refs[6 + count :]
-    gated, lifted, hidden = refs
+    wide, down, refs = refs[:4], refs[4:6], refs[6:]
+    outs, (sums, hidden) = refs[:count], refs[count:]
     step = pl.program_id(0)
-
-    @pl.when(step == 0)
-    def _():
-        gated[...] = jnp.zeros_like(gated)
-        lifted[...] = jnp.zeros_like(lifted)
 
     @pl.when(step < inner)
     def _():
         block = jnp.concatenate([r[...] for r in rows], axis=0)
-        for i in range(2):
-            gated[i] += jnp.dot(block, gate[i][...], preferred_element_type=F32)
-            lifted[i] += jnp.dot(block, up[i][...], preferred_element_type=F32)
+        weights = jnp.concatenate([w[...] for w in wide], axis=0)
+        product = across_lanes(block, weights)
+
+        @pl.when(step == 0)
+        def _():
+            sums[...] = product
+
+        @pl.when(step > 0)
+        def _():
+            sums[...] += product
 
     @pl.when(step == inner - 1)
     def _():
-        value = gated[...]
-        hidden[...] = (value / (1.0 + jnp.exp(-value)) * lifted[...]).astype(BF16)
+        value = sums[...]
+        width = value.shape[1] // 2
+        gated, lifted = value[:, :width], value[:, width:]
+        hidden[...] = (gated / (1.0 + jnp.exp(-gated)) * lifted).astype(BF16)
 
     @pl.when(step >= inner)
     def _():
-        total = jnp.dot(hidden[0], down[0][...], preferred_element_type=F32)
-        total += jnp.dot(hidden[1], down[1][...], preferred_element_type=F32)
-        total = total.astype(BF16)
+        weights = jnp.concatenate([w[...] for w in down], axis=0)
+        total = jnp.dot(hidden[...], weights, preferred_element_type=F32).astype(BF16)
         start = 0
         for out in outs:
             out[...] = total[start : start + out.shape[0]]
@@ -139,31 +146,30 @@
 
 
 def expert_ffn(parts, gate, up, down):
-    features, width = gate[0].shape
+    width, features = gate[0].shape
     total_rows = sum(p.shape[0] for p in parts)
-    tile = min(features, 1024)
+    tile = min(features, 2048)
     inner = features // tile
 
     def first(i):
-        return jnp.minimum(i, inner - 1)
+        return (0, jnp.minimum(i, inner - 1))
 
     def second(i):
-        return jnp.maximum(i - inner, 0)
+        return (0, jnp.maximum(i - inner, 0))
 
     return pl.pallas_call(
         functools.partial(ffn_kernel, len(parts), inner),
         grid=(2 * inner,),
-        in_specs=[pl.BlockSpec((p.shape[0], tile), lambda i: (0, first(i))) for p in parts]
-        + [pl.BlockSpec((tile, width), lambda i: (first(i), 0))] * 4
-        + [pl.BlockSpec((width, tile), lambda i: (0, second(i)))] * 2,
-        out_specs=[pl.BlockSpec((p.shape[0], tile), lambda i: (0, second(i))) for p in parts],
+        in_specs=[pl.BlockSpec((p.shape[0], tile), first) for p in parts]
+        + [pl.BlockSpec((width, tile), first)] * 4
+        + [pl.BlockSpec((width, tile), second)] * 2,
+        out_specs=[pl.BlockSpec((p.shape[0], tile), second) for p in parts],
         out_shape=[jax.ShapeDtypeStruct(p.shape, BF16) for p in parts],
         scratch_shapes=[
-            pltpu.VMEM((2, total_rows, width), F32),
-            pltpu.VMEM((2, total_rows, width), F32),
-            pltpu.VMEM((2, total_rows, width), BF16),
+            pltpu.VMEM((total_rows, 4 * width), F32),
+            pltpu.VMEM((total_rows, 2 * width), BF16),
         ],
-        compiler_params=pltpu.CompilerParams(vmem_limit_bytes=32 * 1024 * 1024),
+        compiler_params=pltpu.CompilerParams(vmem_limit_bytes=28 * 1024 * 1024),
         cost_estimate=pl.CostEstimate(
             flops=12 * total_rows * features * width,
             bytes_accessed=12 * features * width + 4 * total_rows * features,
@@ -172,18 +178,20 @@
     )(*parts, *gate, *up, *down)
 
 
-def block_columns(out_weight):
-    width = out_weight.shape[1]
-
-    def ordered(own, other, axis):
-        first = lax.axis_index(axis) == 0
-        return jnp.where(first, own, other), jnp.where(first, other, own)
-
-    pair = jnp.concatenate(ordered(out_weight, shift(out_weight, "zl", 1), "zl"), axis=1)
-    low, high = ordered(pair, shift(pair, "core", 1), "core")
-    return jnp.concatenate(
-        [low[:, :width], high[:, :width], low[:, width:], high[:, width:]], axis=1
-    )
+def peer_columns(columns):
+    def ordered(shape, own, other, axis, where):
+        index = lax.axis_index(axis)
+        whole = jnp.zeros(shape, own.dtype)
+        for part, position in ((own, index), (other, 1 - index)):
+            whole = lax.dynamic_update_slice_in_dim(whole, part, position, where)
+        return whole
+
+    here, depth = columns.shape
+    columns = columns[None]
+    columns = ordered((2, here, depth), columns, shift(columns, "zl", 1), "zl", 0)[None]
+    columns = ordered((2, 2, here, depth), columns, shift(columns, "yl", 1), "yl", 0)[:, :, None]
+    columns = ordered((2, 2, 2, here, depth), columns, shift(columns, "core", 1), "core", 2)
+    return columns.reshape(8 * here, depth)
 
 
 def shards(
@@ -199,55 +207,64 @@
     up_weight,
     down_weight,
 ):
-    steps, rows, _ = query_rows.shape
-    blocks = lax.axis_size("y") * lax.axis_size("zp")
+    steps, rows, depth = query_rows.shape
+    peers = lax.axis_size("yh") * lax.axis_size("zp")
+    blocks = 2 * peers
     experts = blocks
     capacity = rows // 2
     head = lax.axis_index("head")
 
     gate, up, down = (
-        (w[0], shift(w[0], "core", 1)) for w in (gate_weight, up_weight, down_weight)
-    )
-    columns = block_columns(out_weight)
-    width = columns.shape[1]
-    features = width * blocks
+        (w, shift(w, "core", 1)) for w in (gate_weight[0].T, up_weight[0].T, down_weight[0])
+    )
+    columns = peer_columns(out_weight.T)
+    width = columns.shape[0]
+    piece_width = width // 2
+    features = width * peers
 
     attended, state_out = attention(query_rows, key_rows, value_rows, forget, head_state)
 
-    depth = attended.shape[1]
     ids = jnp.pad(route_ids.reshape(steps * rows, 2).astype(BF16), ((0, 0), (0, LANES - 2)))
-    peers = spread(jnp.concatenate([attended, ids], axis=1), BLOCKS)
-    peers = peers.reshape(blocks, steps, rows, depth + LANES)
-    peer_ids = peers[..., depth : depth + 2].astype(jnp.int32)
-    peers = jnp.transpose(peers[..., :depth], (1, 2, 0, 3)).reshape(steps * rows * blocks, depth)
-    partial = jnp.dot(peers, columns, preferred_element_type=F32)
-    partial = partial.reshape(steps, rows * blocks, width)
+    gathered = spread(jnp.concatenate([attended, ids], axis=1), PEERS)
+    gathered, gate, up, down = lax.optimization_barrier((gathered, gate, up, down))
+    gathered = gathered.reshape(peers * steps * rows, depth + LANES)
+    partial = lax.dot_general(
+        gathered[:, :depth], columns, (((1,), (1,)), ((), ())), preferred_element_type=F32
+    )
+    partial = partial.reshape(peers, steps, rows, width)
+    peer_ids = gathered[:, depth : depth + 2].astype(jnp.int32).reshape(peers, steps, rows, 2)
 
     def of_step(array, axis, there=head):
         return lax.dynamic_index_in_dim(array, there, axis, keepdims=False)
 
-    projected = of_step(partial, 0)
+    projected = of_step(partial, 1)
     for distance in range(1, steps):
         there = lax.rem(head + distance, steps)
-        projected = projected + shift(of_step(partial, 0, there), "head", distance)
-    projected = projected.astype(BF16).reshape(rows, blocks, width)
+        projected = projected + shift(of_step(partial, 1, there), "head", distance)
+    projected = projected.astype(BF16)
 
     placed = jnp.sum(place(of_step(peer_ids, 1), experts, capacity), axis=-1)
     packed = sum(
-        placed[:, :, :, r, None] * projected[r].astype(F32)[None, None] for r in range(rows)
+        placed[:, :, :, r, None] * projected[:, r].astype(F32)[None, None] for r in range(rows)
     ).astype(BF16)
     packed = lax.all_to_all(packed, BLOCKS, split_axis=0, concat_axis=0, tiled=True)
-    piece = jnp.transpose(packed, (1, 2, 0, 3)).reshape(capacity * blocks, features)
-
-    result = scatter_block(expert_ffn(gather_block(piece), gate, up, down))
-
-    result = jnp.transpose(result.reshape(capacity, blocks, features), (1, 0, 2))
-    mixed = jnp.transpose(projected, (1, 0, 2)).reshape(blocks, capacity, 2 * width)
+    packed = packed.reshape(2, 2, peers // 2, capacity, peers, 2, piece_width)
+    piece = jnp.transpose(packed, (1, 3, 4, 0, 5, 2, 6)).reshape(capacity * blocks, features)
+
+    pieces = gather_block(piece)
+    pieces[-1], state_out = lax.optimization_barrier((pieces[-1], state_out))
+    result = scatter_block(expert_ffn(pieces, gate, up, down))
+
+    result = result.reshape(2, capacity, 2, peers // 2, features)
+    result = jnp.transpose(result, (2, 0, 3, 1, 4)).reshape(blocks, capacity, features)
+    mixed = projected.reshape(2, 1, peers // 2, capacity, 2 * width)
+    mixed = jnp.broadcast_to(mixed, (2, 2) + mixed.shape[2:]).reshape(blocks, capacity, 2 * width)
     result = lax.all_to_all(
         jnp.concatenate([result, mixed], axis=2), BLOCKS, split_axis=0, concat_axis=0, tiled=True
     )
-    mixed = result[..., features:].reshape(blocks, rows, width)
-    mixed = jnp.transpose(mixed, (1, 0, 2)).reshape(rows, features)
+    mixed = result[..., features:].reshape(2, 2, peers // 2, rows, 2, piece_width)
+    mixed = lax.dynamic_index_in_dim(mixed, lax.axis_index("yl"), 1, keepdims=False)
+    mixed = jnp.transpose(mixed, (2, 0, 3, 1, 4)).reshape(rows, features)
     weights = jnp.sum(
         place(of_step(route_ids, 0), experts, capacity) * of_step(route_gate, 0), axis=-1
     )
@@ -261,7 +278,7 @@
 def solution(mesh):
     shape = dict(mesh.shape)
     heads, peers = shape["head"], shape["expert"]
-    split = (4, peers // 16, 2, 2)
+    split = (2, 2, peers // 16, 2, 2)
     fine = Mesh(mesh.devices.reshape((heads,) + split), ("head",) + EXPERT)
     return jax.shard_map(
         shards,

time: 229 us -> 212 us (0.926)
  blocking collectives: 17.5 us -> 34 us
  local copies, waits for them, and re-layouts: 50 us -> 38.2 us
  waiting for transfers between devices: 73.8 us -> 62.2 us
  starting transfers between devices: 54.1 us -> 45.2 us
  Pallas kernels: 16.4 us -> 11.6 us
  matrix products: 5.72 us -> 8.09 us
    unnamed x61 -> x33, local copies, waits for them, and re-layouts: 25.9 us -> 3.34 us
    all_to_all x0 -> x1, blocking collectives: none -> 16.6 us  [spread(): return lax.all_to_all(copies, axis, split_axis=0, concat_axis=0, tiled=True)]
    ppermute x2 -> x0, local copies, waits for them, and re-layouts: 12.6 us -> none  [shift(): return lax.ppermute(array, axis, pairs)]
    all_to_all x2 -> x1, waiting for transfers between devices: 20.2 us -> 8.19 us  [spread(): return lax.all_to_all(copies, axis, split_axis=0, concat_axis=0, tiled=True)]
    all_to_all x2 -> x1, starting transfers between devices: 20.3 us -> 10.2 us  [spread(): return lax.all_to_all(copies, axis, split_axis=0, concat_axis=0, tiled=True)]
    dynamic_update_slice x0 -> x6, local copies, waits for them, and re-layouts: none -> 7.6 us  [ordered(): whole = lax.dynamic_update_slice_in_dim(whole, part, position, where)]
    pallas_call x1, Pallas kernels: 16.4 us -> 11.6 us  [expert_ffn(): pl.pallas_call(functools.partial(ffn_kernel, len(parts), inner), grid=(2...]
    ppermute x24 -> x25, starting transfers between devices: 27.8 us -> 31.4 us  [shift(): return lax.ppermute(array, axis, pairs)]
  transfers between devices with their start and end apart: 27 -> 27, of which waited for: 14 -> 13; matrix products, arithmetic and copies ran while one was open for 19% -> 17% of each run, Pallas kernels for 0% -> 0%
where the time goes in v4:
time: 212 us; the launch traced here: 210 us
  waiting for transfers between devices  62.2 us (29%)
  starting transfers between devices  45.2 us (21%)
  local copies, waits for them, and re-layouts  38.2 us (18%)
  blocking collectives  34 us (16%)
  Pallas kernels  11.6 us (5%)
  other arithmetic  9.43 us (4%)
  matrix products  8.09 us (4%)
    ppermute x25, waiting for transfers between devices, shift(): return lax.ppermute(array, axis, pairs)  39.4 us
    ppermute x25, starting transfers between devices, shift(): return lax.ppermute(array, axis, pairs)  31.4 us
    all_to_all x1, blocking collectives, shards(): lax.all_to_all(packed, BLOCKS, split_axis=0, concat_axis=0, tiled=True)  17.4 us
    all_to_all x1, blocking collectives, spread(): return lax.all_to_all(copies, axis, split_axis=0, concat_axis=0, tiled=True)  16.6 us
    all_to_all x1, waiting for transfers between devices, shards(): lax.all_to_all(jnp.concatenate([result, mixed], axis=2), BLOCKS, split_ax...  14.6 us
    pallas_call x1, Pallas kernels, expert_ffn(): pl.pallas_call(functools.partial(ffn_kernel, len(parts), inner), grid=(2...  11.6 us
    all_to_all x1, starting transfers between devices, spread(): return lax.all_to_all(copies, axis, split_axis=0, concat_axis=0, tiled=True)  10.2 us
    all_to_all x1, waiting for transfers between devices, spread(): return lax.all_to_all(copies, axis, split_axis=0, concat_axis=0, tiled=True)  8.19 us
  transfers between devices with their start and end apart: 27, of which 13 were waited for; matrix products, arithmetic and copies ran while one was open for 17% of the time, Pallas kernels for 0%

profile of v4, /device:TPU:2, one launch (start us, length us, event | category | flops | bytes accessed | tf_op | source)
XLA Modules:
  0.0 209.8 jit_solution(16851333106434422340)
XLA Ops:
  1.3 1.9 collective-permute-start.3
  3.3 1.4 reshape.221
  4.7 1.4 reshape.222
  6.7 1.4 reshape.223
  8.1 1.4 convert_element_type.174
  10.8 1.0 fusion.1
  11.9 0.9 bitcast_dynamic-update-slice_fusion.2
  12.9 0.9 bitcast_dynamic-update-slice_fusion.3
  13.9 1.7 collective-permute-start.4
  15.5 0.8 slice_bitcast_fusion.3
  16.3 1.0 broadcast_in_dim.40
  17.3 0.8 bitcast_dynamic-update-slice_fusion.1
  18.1 7.1 %collective-permute-done.4 = bf16[1,2,96,1024]{3,2,1,0:T(8,128)(2,1)S(1)} collective-permute-done((bf16[1,2,96,1024]{3,2,1,0:T(8,128)(2,1)S(1)}, bf16[1,2,96,1024]{3,2,1,0:T(8,128)(2,1)S(1)}, u32[]{:S(2)}, u32[]{:S(2)}) %collective-permute-start.4) | collective-permute-done | bytes 393248 | tf_op jit(solution)/shard_map/ppermute | solution.py:22
  25.1 0.8 bitcast_dynamic-update-slice_fusion
  27.5 0.8 copy.262
  28.3 0.8 fusion.14
  29.8 10.2 %all-to-all-start = ((bf16[8,16,1152]{2,1,0:T(8,128)(2,1)}), bf16[8,16,1152]{2,1,0:T(8,128)(2,1)}, u32[]{:S(2)}, u32[]{:S(2)}) async-start(bf16[8,16,1152]{2,1,0:T(8,128)(2,1)} %broadcast_in_dim.38), calls=%async_computation | async-start | bytes 589824 | tf_op jit(solution)/shard_map/all_to_all | solution.py:28
  40.0 1.4 broadcast_in_dim.39
  41.4 2.1 constant_dynamic-update-slice_fusion.1
  43.5 2.1 constant_dynamic-update-slice_fusion
  45.6 8.2 %all-to-all-done = bf16[8,16,1152]{2,1,0:T(8,128)(2,1)} async-done(((bf16[8,16,1152]{2,1,0:T(8,128)(2,1)}), bf16[8,16,1152]{2,1,0:T(8,128)(2,1)}, u32[]{:S(2)}, u32[]{:S(2)}) %all-to-all-start) | async-done | bytes 294944 | tf_op jit(solution)/shard_map/all_to_all | solution.py:28
  53.8 1.9 slice.182
  55.7 1.4 slice_convert_fusion
  57.1 1.8 dot_general.19
  58.9 2.2 %fusion.6 = f32[8,4,4,768]{3,0,2,1:T(8,128)S(1)} fusion(bf16[768,1024,1,1]{1,0,3,2:T(8,128)(2,1)} %bitcast.32, bf16[8,4,4,1024]{3,2,1,0:T(4,128)(2,1)} %dot_general.19), kind=kOutput, calls=%fused_computation.26 | convolution fusion | flops 201326592 | bytes 2228224 | tf_op jit(solution)/shard_map/dot_general | solution.py:231
  61.1 0.8 dynamic-slice_bitcast_fusion.2
  61.9 1.5 collective-permute-start.6
  63.4 1.1 collective-permute-start.7
  64.5 2.2 %collective-permute-start.8 = (f32[8,4,768]{2,0,1:T(8,128)}, f32[8,4,768]{2,0,1:T(8,128)S(1)}, u32[]{:S(2)}, u32[]{:S(2)}) collective-permute-start(f32[8,4,768]{2,0,1:T(8,128)} %get-tuple-element.54), channel_id=1, source_target_pairs={{0,192},{64,0},{128,64},{192,128},{1,193},{65,1},{129,65},{193,129... | collective-permute-start | bytes 294920 | tf_op jit(solution)/shard_map/ppermute | solution.py:22
  66.7 1.1 copy.287
  70.9 0.9 fusion.10
  72.4 1.2 add_convert_fusion.5
  73.6 17.4 %all_to_all.20 = bf16[16,2,8,768]{3,2,1,0:T(8,128)(2,1)} all-to-all(bf16[16,2,8,768]{3,2,1,0:T(8,128)(2,1)S(1)} %add_convert_fusion.5), channel_id=1, replica_groups=mesh['head'=4,'yh'=2,'yl'=2,'zp'=4,'zl'=2,'core'=2] {'yh','yl','zp'}, dimensions={0} | all-to-all | bytes 786432 | tf_op jit(solution)/shard_map/all_to_all | solution.py:250
  91.0 1.8 reshape.229
  92.8 1.8 copy.247
  94.6 1.4 collective-permute-start.10
  96.7 0.8 copy.249
  97.4 2.6 %collective-permute-start.11 = (bf16[32,6144]{1,0:T(8,128)(2,1)}, bf16[32,6144]{1,0:T(8,128)(2,1)S(1)}, u32[]{:S(2)}, u32[]{:S(2)}) collective-permute-start(bf16[32,6144]{1,0:T(8,128)(2,1)} %bitcast.45.refs_0_), channel_id=1, source_target_pairs={{0,2},{2,0},{1,3},{3,1},{4,6},{6,4},{5,7},{7,5},{8,10},{10,8},{9,1... | collective-permute-start | bytes 1179656 | tf_op jit(solution)/shard_map/ppermute | solution.py:22
  100.6 3.7 %collective-permute-done.10.refs_2_ = bf16[32,6144]{1,0:T(8,128)(2,1)} collective-permute-done((bf16[32,6144]{1,0:T(8,128)(2,1)}, bf16[32,6144]{1,0:T(8,128)(2,1)}, u32[]{:S(2)}, u32[]{:S(2)}) %collective-permute-start.10) | collective-permute-done | bytes 393248 | tf_op jit(solution)/shard_map/ppermute | solution.py:22
  104.3 1.2 fusion.38
  105.5 1.3 collective-permute-done.11.refs_3_
  106.9 1.5 collective-permute-start.13
  108.4 0.9 collective-permute-start.12
  109.4 1.2 collective-permute-start.14
  110.6 5.8 %collective-permute-done.13.refs_5_ = bf16[32,6144]{1,0:T(8,128)(2,1)S(1)} collective-permute-done((bf16[32,6144]{1,0:T(8,128)(2,1)S(1)}, bf16[32,6144]{1,0:T(8,128)(2,1)S(1)}, u32[]{:S(2)}, u32[]{:S(2)}) %collective-permute-start.13) | collective-permute-done | bytes 393248 | tf_op jit(solution)/shard_map/ppermute | solution.py:22
  116.4 1.6 collective-permute-start.16
  118.6 4.2 %add_convert_fusion = bf16[4,8,128,128]{3,2,1,0:T(8,128)(2,1)} fusion(bf16[4,8,128,128]{3,2,1,0:T(8,128)(2,1)} %param.15, f32[8]{0:T(128)S(1)} %slice_bitcast_fusion.12, bf16[4,4,8,128]{3,2,1,0:T(8,128)(2,1)} %reshape.223, f32[4,8]{0,1:T(8,128)S(1)} %copy.249, bf16[4,4,8,128]{3,2,1,0:T(8,128)(2,1)} %reshape.222), kind=kOutput, calls=%fused_computation.2 | convolution fusion | flops 27295744 | bytes 2162848 | tf_op jit(solution)/shard_map/trhi,trhj->rhij/dot_general | solution.py:51
  122.8 2.3 %collective-permute-done.15.refs_7_ = bf16[16,6144]{1,0:T(8,128)(2,1)S(1)} collective-permute-done((bf16[16,6144]{1,0:T(8,128)(2,1)S(1)}, bf16[16,6144]{1,0:T(8,128)(2,1)S(1)}, u32[]{:S(2)}, u32[]{:S(2)}) %collective-permute-start.15) | collective-permute-done | bytes 196640 | tf_op jit(solution)/shard_map/ppermute | solution.py:22
  125.2 2.0 copy-done.5
  127.1 11.6 %shard_map.130 = (bf16[32,6144]{1,0:T(8,128)(2,1)S(1)}, bf16[32,6144]{1,0:T(8,128)(2,1)S(1)}, bf16[32,6144]{1,0:T(8,128)(2,1)S(1)}, bf16[32,6144]{1,0:T(8,128)(2...) custom-call(bf16[32,6144]{1,0:T(8,128)(2,1)} %bitcast.45.refs_0_, ...), custom_call_target="tpu_custom_call" | custom-call | flops 5435817984 | bytes 27525120 | tf_op jit(solution)/shard_map/pallas_call | solution.py:160
  138.8 3.3 %collective-permute-start.17 = (bf16[16,6144]{1,0:T(8,128)(2,1)S(1)}, bf16[16,6144]{1,0:T(8,128)(2,1)S(1)}, u32[]{:S(2)}, u32[]{:S(2)}) collective-permute-start(bf16[16,6144]{1,0:T(8,128)(2,1)S(1)} %get-tuple-element.32), channel_id=1, source_target_pairs={{0,192},{64,0},{128,64},{192,128},{1,193},{65,1},{129,65},{193,129... | collective-permute-start | bytes 589832 | tf_op jit(solution)/shard_map/ppermute | solution.py:22
  142.1 1.4 collective-permute-start.19
  143.5 3.4 %collective-permute-done.17 = bf16[16,6144]{1,0:T(8,128)(2,1)S(1)} collective-permute-done((bf16[16,6144]{1,0:T(8,128)(2,1)S(1)}, bf16[16,6144]{1,0:T(8,128)(2,1)S(1)}, u32[]{:S(2)}, u32[]{:S(2)}) %collective-permute-start.17) | collective-permute-done | bytes 196640 | tf_op jit(solution)/shard_map/ppermute | solution.py:22
  147.0 2.6 %collective-permute-start.18 = (bf16[32,6144]{1,0:T(8,128)(2,1)S(1)}, bf16[32,6144]{1,0:T(8,128)(2,1)S(1)}, u32[]{:S(2)}, u32[]{:S(2)}) collective-permute-start(bf16[32,6144]{1,0:T(8,128)(2,1)S(1)} %pad_maximum_fusion.4), channel_id=1, source_target_pairs={{0,192},{64,0},{128,64},{192,128},{1,193},{65,1},{129,65},{193,129... | collective-permute-start | bytes 1179656 | tf_op jit(solution)/shard_map/ppermute | solution.py:22
  150.1 8.4 %collective-permute-done.18 = bf16[32,6144]{1,0:T(8,128)(2,1)S(1)} collective-permute-done((bf16[32,6144]{1,0:T(8,128)(2,1)S(1)}, bf16[32,6144]{1,0:T(8,128)(2,1)S(1)}, u32[]{:S(2)}, u32[]{:S(2)}) %collective-permute-start.18) | collective-permute-done | bytes 393248 | tf_op jit(solution)/shard_map/ppermute | solution.py:22
  158.7 2.2 %collective-permute-start.20 = (bf16[32,6144]{1,0:T(8,128)(2,1)S(1)}, bf16[32,6144]{1,0:T(8,128)(2,1)S(1)}, u32[]{:S(2)}, u32[]{:S(2)}) collective-permute-start(bf16[32,6144]{1,0:T(8,128)(2,1)S(1)} %add_convert_fusion.4), channel_id=1, source_target_pairs={{0,192},{64,0},{128,64},{192,128},{1,193},{65,1},{129,65},{193,129... | collective-permute-start | bytes 1179656 | tf_op jit(solution)/shard_map/ppermute | solution.py:22
  162.1 1.9 collective-permute-start.24
  164.3 2.6 %collective-permute-done.20 = bf16[32,6144]{1,0:T(8,128)(2,1)S(1)} collective-permute-done((bf16[32,6144]{1,0:T(8,128)(2,1)S(1)}, bf16[32,6144]{1,0:T(8,128)(2,1)S(1)}, u32[]{:S(2)}, u32[]{:S(2)}) %collective-permute-start.20) | collective-permute-done | bytes 393248 | tf_op jit(solution)/shard_map/ppermute | solution.py:22
  166.8 4.0 %collective-permute-done.23 = bf16[32,6144]{1,0:T(8,128)(2,1)S(1)} collective-permute-done((bf16[32,6144]{1,0:T(8,128)(2,1)S(1)}, bf16[32,6144]{1,0:T(8,128)(2,1)S(1)}, u32[]{:S(2)}, u32[]{:S(2)}) %collective-permute-start.23) | collective-permute-done | bytes 393248 | tf_op jit(solution)/shard_map/ppermute | solution.py:22
  171.6 1.2 pad_maximum_fusion
  172.9 3.6 %all-to-all-start.2 = ((bf16[16,2,7680]{2,1,0:T(2,128)(2,1)}), bf16[16,2,7680]{2,1,0:T(2,128)(2,1)S(1)}, u32[]{:S(2)}, u32[]{:S(2)}) async-start(bf16[16,2,7680]{2,1,0:T(2,128)(2,1)} %pad_maximum_fusion), calls=%async_computation.2 | async-start | bytes 983040 | tf_op jit(solution)/shard_map/all_to_all | solution.py:262
  176.7 14.6 %all-to-all-done.2 = bf16[16,2,7680]{2,1,0:T(2,128)(2,1)S(1)} async-done(((bf16[16,2,7680]{2,1,0:T(2,128)(2,1)}), bf16[16,2,7680]{2,1,0:T(2,128)(2,1)S(1)}, u32[]{:S(2)}, u32[]{:S(2)}) %all-to-all-start.2) | async-done | bytes 491552 | tf_op jit(solution)/shard_map/all_to_all | solution.py:262
  192.4 16.6 %all_to_all.21 = bf16[4,8,6144]{2,1,0:T(8,128)(2,1)S(1)} all-to-all(bf16[4,8,6144]{2,1,0:T(8,128)(2,1)S(1)} %broadcast_in_dim.89), channel_id=1, replica_groups=mesh['head'=4,'yh'=2,'yl'=2,'zp'=4,'zl'=2,'core'=2] {'head'}, dimensions={0} | all-to-all | bytes 786432 | tf_op jit(solution)/shard_map/all_to_all | solution.py:28
  209.0 0.9 fusion.33
  (129 shorter events, 15.2 us)
Async XLA Ops:
  0.6 175.9 %copy-start = (f32[4,4,2]{1,2,0:T(2,128)S(1)}, f32[4,4,2]{1,2,0:T(2,128)}, u32[]{:S(2)}) copy-start(f32[4,4,2]{1,2,0:T(2,128)} %param.18) | copy-start | bytes 388
  0.6 53.1 %collective-permute-start = (bf16[288,6144]{1,0:T(8,128)(2,1)}, bf16[288,6144]{1,0:T(8,128)(2,1)S(1)}, u32[]{:S(2)}, u32[]{:S(2)}) collective-permute-start(bf16[288,6144]{1,0:T(8,128)(2,1)} %bitcast.131), channel_id=1, source_target_pairs={{0,1},{1,0},{2,3},{3,2},{4,5},{5,4},{6,7},{7,6},{8,9},{9,8},{10,11... | collective-permute-start | bytes 10616840 | tf_op jit(solution)/shard_map/ppermute | solution.py:22
  0.7 53.0 %collective-permute-start.1 = (bf16[288,6144]{1,0:T(8,128)(2,1)}, bf16[288,6144]{1,0:T(8,128)(2,1)}, u32[]{:S(2)}, u32[]{:S(2)}) collective-permute-start(bf16[288,6144]{1,0:T(8,128)(2,1)} %bitcast.133), channel_id=1, source_target_pairs={{0,1},{1,0},{2,3},{3,2},{4,5},{5,4},{6,7},{7,6},{8,9},{9,8},{10,11... | collective-permute-start | bytes 10616840 | tf_op jit(solution)/shard_map/ppermute | solution.py:22
  1.2 52.5 %collective-permute-start.2 = (bf16[288,6144]{1,0:T(8,128)(2,1)}, bf16[288,6144]{1,0:T(8,128)(2,1)}, u32[]{:S(2)}, u32[]{:S(2)}) collective-permute-start(bf16[288,6144]{1,0:T(8,128)(2,1)} %bitcast.135), channel_id=1, source_target_pairs={{0,1},{1,0},{2,3},{3,2},{4,5},{5,4},{6,7},{7,6},{8,9},{9,8},{10,11... | collective-permute-start | bytes 10616840 | tf_op jit(solution)/shard_map/ppermute | solution.py:22
  1.3 11.6 %collective-permute-start.3 = (bf16[1,96,1024]{2,1,0:T(8,128)(2,1)}, bf16[1,96,1024]{2,1,0:T(8,128)(2,1)}, u32[]{:S(2)}, u32[]{:S(2)}) collective-permute-start(bf16[1,96,1024]{2,1,0:T(8,128)(2,1)} %bitcast.142), channel_id=1, source_target_pairs={{0,2},{2,0},{1,3},{3,1},{4,6},{6,4},{5,7},{7,5},{8,10},{10,8},{9,1... | collective-permute-start | bytes 589832 | tf_op jit(solution)/shard_map/ppermute | solution.py:22
  10.7 15.2 %copy-start.15 = (f32[4,8]{0,1:T(8,128)S(1)}, f32[4,8]{0,1:T(8,128)}, u32[]{:S(2)}) copy-start(f32[4,8]{0,1:T(8,128)} %copy.223) | copy-start | bytes 388
  10.7 15.2 %copy-start.8 = (bf16[4,8,128,128]{3,2,1,0:T(8,128)(2,1)S(1)}, bf16[4,8,128,128]{3,2,1,0:T(8,128)(2,1)}, u32[]{:S(2)}) copy-start(bf16[4,8,128,128]{3,2,1,0:T(8,128)(2,1)} %param.15) | copy-start | bytes 3145732
  10.7 15.2 %copy-start.12 = (bf16[4,4,8,128]{3,2,1,0:T(8,128)(2,1)S(1)}, bf16[4,4,8,128]{3,2,1,0:T(8,128)(2,1)}, u32[]{:S(2)}) copy-start(bf16[4,4,8,128]{3,2,1,0:T(8,128)(2,1)} %reshape.221) | copy-start | bytes 98308
  13.9 11.3 %collective-permute-start.4 = (bf16[1,2,96,1024]{3,2,1,0:T(8,128)(2,1)S(1)}, bf16[1,2,96,1024]{3,2,1,0:T(8,128)(2,1)S(1)}, u32[]{:S(2)}, u32[]{:S(2)}) collective-permute-start(bf16[1,2,96,1024]{3,2,1,0:T(8,128)(2,1)S(1)} %bitcast_dynamic-update-slice_fusion.3), channel_id=1, source_target_pairs={{0,16},{16,0},{1,17},{17,1},{2,18},{18,2},{3,19},{19,3},{4,20},{20... | collective-permute-start | bytes 1179656 | tf_op jit(solution)/shard_map/ppermute | solution.py:22
  16.3 10.6 %copy-start.13 = (s32[4,4,2]{1,2,0:T(2,128)S(1)}, s32[4,4,2]{1,2,0:T(2,128)}, u32[]{:S(2)}) copy-start(s32[4,4,2]{1,2,0:T(2,128)} %param.17) | copy-start | bytes 388
  25.9 17.6 %collective-permute-start.5 = (bf16[2,2,1,96,1024]{4,3,2,1,0:T(8,128)(2,1)}, bf16[2,2,1,96,1024]{4,3,2,1,0:T(8,128)(2,1)}, u32[]{:S(2)}, u32[]{:S(2)}) collective-permute-start(bf16[2,2,1,96,1024]{4,3,2,1,0:T(8,128)(2,1)} %bitcast_dynamic-update-slice_fusion), channel_id=1, source_target_pairs={{0,1},{1,0},{2,3},{3,2},{4,5},{5,4},{6,7},{7,6},{8,9},{9,8},{10,11... | collective-permute-start | bytes 2359304 | tf_op jit(solution)/shard_map/ppermute | solution.py:22
  29.8 23.9 %all-to-all-start = ((bf16[8,16,1152]{2,1,0:T(8,128)(2,1)}), bf16[8,16,1152]{2,1,0:T(8,128)(2,1)}, u32[]{:S(2)}, u32[]{:S(2)}) async-start(bf16[8,16,1152]{2,1,0:T(8,128)(2,1)} %broadcast_in_dim.38), calls=%async_computation | async-start | bytes 589824 | tf_op jit(solution)/shard_map/all_to_all | solution.py:28
  53.8 8.1 %copy-start.4 = (bf16[288,6144]{1,0:T(8,128)(2,1)}, bf16[288,6144]{1,0:T(8,128)(2,1)S(1)}, u32[]{:S(2)}) copy-start(bf16[288,6144]{1,0:T(8,128)(2,1)S(1)} %collective-permute-done.refs_10_) | copy-start | bytes 10616836
  61.0 0.8 copy-start.11
  61.8 34.2 %copy-start.14 = (f32[4,8]{1,0:T(4,128)S(1)}, f32[4,8]{1,0:T(4,128)}, u32[]{:S(2)}) copy-start(f32[4,8]{1,0:T(4,128)} %get-tuple-element.72) | copy-start | bytes 388
  61.9 9.0 %collective-permute-start.6 = (f32[8,4,768]{2,0,1:T(8,128)}, f32[8,4,768]{2,0,1:T(8,128)S(1)}, u32[]{:S(2)}, u32[]{:S(2)}) collective-permute-start(f32[8,4,768]{2,0,1:T(8,128)} %get-tuple-element.53), channel_id=1, source_target_pairs={{0,64},{64,128},{128,192},{192,0},{1,65},{65,129},{129,193},{193,1... | collective-permute-start | bytes 294920 | tf_op jit(solution)/shard_map/ppermute | solution.py:22
  63.4 7.5 %collective-permute-start.7 = (f32[8,4,768]{2,0,1:T(8,128)}, f32[8,4,768]{2,0,1:T(8,128)S(1)}, u32[]{:S(2)}, u32[]{:S(2)}) collective-permute-start(f32[8,4,768]{2,0,1:T(8,128)} %get-tuple-element.55), channel_id=1, source_target_pairs={{0,128},{64,192},{128,0},{192,64},{1,129},{65,193},{129,1},{193,65... | collective-permute-start | bytes 294920 | tf_op jit(solution)/shard_map/ppermute | solution.py:22
  64.5 6.4 %collective-permute-start.8 = (f32[8,4,768]{2,0,1:T(8,128)}, f32[8,4,768]{2,0,1:T(8,128)S(1)}, u32[]{:S(2)}, u32[]{:S(2)}) collective-permute-start(f32[8,4,768]{2,0,1:T(8,128)} %get-tuple-element.54), channel_id=1, source_target_pairs={{0,192},{64,0},{128,64},{192,128},{1,193},{65,1},{129,65},{193,129... | collective-permute-start | bytes 294920 | tf_op jit(solution)/shard_map/ppermute | solution.py:22
  71.8 0.6 copy-start.9
  72.4 52.7 %copy-start.3 = (bf16[1,288,6144]{2,1,0:T(8,128)(2,1)S(1)}, bf16[1,288,6144]{2,1,0:T(8,128)(2,1)}, u32[]{:S(2)}) copy-start(bf16[1,288,6144]{2,1,0:T(8,128)(2,1)} %param.21) | copy-start | bytes 10616836
  94.6 9.7 %collective-permute-start.10 = (bf16[32,6144]{1,0:T(8,128)(2,1)}, bf16[32,6144]{1,0:T(8,128)(2,1)}, u32[]{:S(2)}, u32[]{:S(2)}) collective-permute-start(bf16[32,6144]{1,0:T(8,128)(2,1)} %bitcast.45.refs_0_), channel_id=1, source_target_pairs={{0,192},{64,0},{128,64},{192,128},{1,193},{65,1},{129,65},{193,129... | collective-permute-start | bytes 1179656 | tf_op jit(solution)/shard_map/ppermute | solution.py:22
  97.4 9.4 %collective-permute-start.11 = (bf16[32,6144]{1,0:T(8,128)(2,1)}, bf16[32,6144]{1,0:T(8,128)(2,1)S(1)}, u32[]{:S(2)}, u32[]{:S(2)}) collective-permute-start(bf16[32,6144]{1,0:T(8,128)(2,1)} %bitcast.45.refs_0_), channel_id=1, source_target_pairs={{0,2},{2,0},{1,3},{3,1},{4,6},{6,4},{5,7},{7,5},{8,10},{10,8},{9,1... | collective-permute-start | bytes 1179656 | tf_op jit(solution)/shard_map/ppermute | solution.py:22
  100.0 8.4 %collective-permute-start.9 = (bf16[32,6144]{1,0:T(8,128)(2,1)}, bf16[32,6144]{1,0:T(8,128)(2,1)S(1)}, u32[]{:S(2)}, u32[]{:S(2)}) collective-permute-start(bf16[32,6144]{1,0:T(8,128)(2,1)} %bitcast.45.refs_0_), channel_id=1, source_target_pairs={{0,64},{64,128},{128,192},{192,0},{1,65},{65,129},{129,193},{193,1... | collective-permute-start | bytes 1179656 | tf_op jit(solution)/shard_map/ppermute | solution.py:22
  104.3 20.8 %copy-start.2 = (bf16[1,6144,288]{1,2,0:T(8,128)(2,1)S(1)}, bf16[1,6144,288]{1,2,0:T(8,128)(2,1)}, u32[]{:S(2)}) copy-start(bf16[1,6144,288]{1,2,0:T(8,128)(2,1)} %param.20) | copy-start | bytes 10616836
  106.9 9.5 %collective-permute-start.13 = (bf16[32,6144]{1,0:T(8,128)(2,1)S(1)}, bf16[32,6144]{1,0:T(8,128)(2,1)S(1)}, u32[]{:S(2)}, u32[]{:S(2)}) collective-permute-start(bf16[32,6144]{1,0:T(8,128)(2,1)S(1)} %pad_maximum_fusion.2), channel_id=1, source_target_pairs={{0,192},{64,0},{128,64},{192,128},{1,193},{65,1},{129,65},{193,129... | collective-permute-start | bytes 1179656 | tf_op jit(solution)/shard_map/ppermute | solution.py:22
  108.4 16.8 %copy-start.1 = (bf16[1,6144,288]{1,2,0:T(8,128)(2,1)S(1)}, bf16[1,6144,288]{1,2,0:T(8,128)(2,1)}, u32[]{:S(2)}) copy-start(bf16[1,6144,288]{1,2,0:T(8,128)(2,1)} %param.19) | copy-start | bytes 10616836
  108.4 9.6 %collective-permute-start.12 = (bf16[32,6144]{1,0:T(8,128)(2,1)S(1)}, bf16[32,6144]{1,0:T(8,128)(2,1)S(1)}, u32[]{:S(2)}, u32[]{:S(2)}) collective-permute-start(bf16[32,6144]{1,0:T(8,128)(2,1)S(1)} %pad_maximum_fusion.1), channel_id=1, source_target_pairs={{0,64},{64,128},{128,192},{192,0},{1,65},{65,129},{129,193},{193,1... | collective-permute-start | bytes 1179656 | tf_op jit(solution)/shard_map/ppermute | solution.py:22
  109.4 13.5 %collective-permute-start.14 = (bf16[32,6144]{1,0:T(8,128)(2,1)S(1)}, bf16[32,6144]{1,0:T(8,128)(2,1)S(1)}, u32[]{:S(2)}, u32[]{:S(2)}) collective-permute-start(bf16[32,6144]{1,0:T(8,128)(2,1)S(1)} %pad_maximum_fusion.3), channel_id=1, source_target_pairs={{0,2},{2,0},{1,3},{3,1},{4,6},{6,4},{5,7},{7,5},{8,10},{10,8},{9,1... | collective-permute-start | bytes 1179656 | tf_op jit(solution)/shard_map/ppermute | solution.py:22
  116.4 6.4 %collective-permute-start.16 = (bf16[16,6144]{1,0:T(8,128)(2,1)S(1)}, bf16[16,6144]{1,0:T(8,128)(2,1)S(1)}, u32[]{:S(2)}, u32[]{:S(2)}) collective-permute-start(bf16[16,6144]{1,0:T(8,128)(2,1)S(1)} %slice.197), channel_id=1, source_target_pairs={{0,192},{64,0},{128,64},{192,128},{1,193},{65,1},{129,65},{193,129... | collective-permute-start | bytes 589832 | tf_op jit(solution)/shard_map/ppermute | solution.py:22
  118.0 7.1 %collective-permute-start.15 = (bf16[16,6144]{1,0:T(8,128)(2,1)S(1)}, bf16[16,6144]{1,0:T(8,128)(2,1)S(1)}, u32[]{:S(2)}, u32[]{:S(2)}) collective-permute-start(bf16[16,6144]{1,0:T(8,128)(2,1)S(1)} %slice.196), channel_id=1, source_target_pairs={{0,64},{64,128},{128,192},{192,0},{1,65},{65,129},{129,193},{193,1... | collective-permute-start | bytes 589832 | tf_op jit(solution)/shard_map/ppermute | solution.py:22
  125.1 2.0 copy-start.5
  138.8 11.3 %copy-start.6 = (bf16[32,6144]{1,0:T(8,128)(2,1)}, bf16[32,6144]{1,0:T(8,128)(2,1)S(1)}, u32[]{:S(2)}) copy-start(bf16[32,6144]{1,0:T(8,128)(2,1)S(1)} %get-tuple-element.29) | copy-start | bytes 1179652
  138.8 8.1 %collective-permute-start.17 = (bf16[16,6144]{1,0:T(8,128)(2,1)S(1)}, bf16[16,6144]{1,0:T(8,128)(2,1)S(1)}, u32[]{:S(2)}, u32[]{:S(2)}) collective-permute-start(bf16[16,6144]{1,0:T(8,128)(2,1)S(1)} %get-tuple-element.32), channel_id=1, source_target_pairs={{0,192},{64,0},{128,64},{192,128},{1,193},{65,1},{129,65},{193,129... | collective-permute-start | bytes 589832 | tf_op jit(solution)/shard_map/ppermute | solution.py:22
  142.1 8.0 %collective-permute-start.19 = (bf16[32,6144]{1,0:T(8,128)(2,1)S(1)}, bf16[32,6144]{1,0:T(8,128)(2,1)S(1)}, u32[]{:S(2)}, u32[]{:S(2)}) collective-permute-start(bf16[32,6144]{1,0:T(8,128)(2,1)S(1)} %get-tuple-element.33), channel_id=1, source_target_pairs={{0,2},{2,0},{1,3},{3,1},{4,6},{6,4},{5,7},{7,5},{8,10},{10,8},{9,1... | collective-permute-start | bytes 1179656 | tf_op jit(solution)/shard_map/ppermute | solution.py:22
  143.5 6.1 %collective-permute-start.21 = (bf16[16,6144]{1,0:T(8,128)(2,1)S(1)}, bf16[16,6144]{1,0:T(8,128)(2,1)S(1)}, u32[]{:S(2)}, u32[]{:S(2)}) collective-permute-start(bf16[16,6144]{1,0:T(8,128)(2,1)S(1)} %get-tuple-element.36), channel_id=1, source_target_pairs={{0,64},{64,128},{128,192},{192,0},{1,65},{65,129},{129,193},{193,1... | collective-permute-start | bytes 589832 | tf_op jit(solution)/shard_map/ppermute | solution.py:22
  147.0 11.6 %collective-permute-start.18 = (bf16[32,6144]{1,0:T(8,128)(2,1)S(1)}, bf16[32,6144]{1,0:T(8,128)(2,1)S(1)}, u32[]{:S(2)}, u32[]{:S(2)}) collective-permute-start(bf16[32,6144]{1,0:T(8,128)(2,1)S(1)} %pad_maximum_fusion.4), channel_id=1, source_target_pairs={{0,192},{64,0},{128,64},{192,128},{1,193},{65,1},{129,65},{193,129... | collective-permute-start | bytes 1179656 | tf_op jit(solution)/shard_map/ppermute | solution.py:22
  149.7 11.9 %collective-permute-start.22 = (bf16[32,6144]{1,0:T(8,128)(2,1)S(1)}, bf16[32,6144]{1,0:T(8,128)(2,1)S(1)}, u32[]{:S(2)}, u32[]{:S(2)}) collective-permute-start(bf16[32,6144]{1,0:T(8,128)(2,1)S(1)} %pad_maximum_fusion.5), channel_id=1, source_target_pairs={{0,64},{64,128},{128,192},{192,0},{1,65},{65,129},{129,193},{193,1... | collective-permute-start | bytes 1179656 | tf_op jit(solution)/shard_map/ppermute | solution.py:22
  158.6 5.6 %copy-start.10 = (bf16[8,4,768]{2,0,1:T(8,128)(2,1)S(1)}, bf16[8,4,768]{2,0,1:T(8,128)(2,1)}, u32[]{:S(2)}) copy-start(bf16[8,4,768]{2,0,1:T(8,128)(2,1)} %copy-done.9) | copy-start | bytes 147460
  158.6 12.2 %copy-start.7 = (bf16[32,6144]{1,0:T(8,128)(2,1)S(1)}, bf16[32,6144]{1,0:T(8,128)(2,1)}, u32[]{:S(2)}) copy-start(bf16[32,6144]{1,0:T(8,128)(2,1)} %copy-done.6) | copy-start | bytes 1179652
  158.7 8.1 %collective-permute-start.20 = (bf16[32,6144]{1,0:T(8,128)(2,1)S(1)}, bf16[32,6144]{1,0:T(8,128)(2,1)S(1)}, u32[]{:S(2)}, u32[]{:S(2)}) collective-permute-start(bf16[32,6144]{1,0:T(8,128)(2,1)S(1)} %add_convert_fusion.4), channel_id=1, source_target_pairs={{0,192},{64,0},{128,64},{192,128},{1,193},{65,1},{129,65},{193,129... | collective-permute-start | bytes 1179656 | tf_op jit(solution)/shard_map/ppermute | solution.py:22
  161.7 9.1 %collective-permute-start.23 = (bf16[32,6144]{1,0:T(8,128)(2,1)S(1)}, bf16[32,6144]{1,0:T(8,128)(2,1)S(1)}, u32[]{:S(2)}, u32[]{:S(2)}) collective-permute-start(bf16[32,6144]{1,0:T(8,128)(2,1)S(1)} %add_convert_fusion.3), channel_id=1, source_target_pairs={{0,64},{64,128},{128,192},{192,0},{1,65},{65,129},{129,193},{193,1... | collective-permute-start | bytes 1179656 | tf_op jit(solution)/shard_map/ppermute | solution.py:22
  162.1 8.7 %collective-permute-start.24 = (bf16[32,6144]{1,0:T(8,128)(2,1)S(1)}, bf16[32,6144]{1,0:T(8,128)(2,1)S(1)}, u32[]{:S(2)}, u32[]{:S(2)}) collective-permute-start(bf16[32,6144]{1,0:T(8,128)(2,1)S(1)} %add_convert_fusion.2), channel_id=1, source_target_pairs={{0,2},{2,0},{1,3},{3,1},{4,6},{6,4},{5,7},{7,5},{8,10},{10,8},{9,1... | collective-permute-start | bytes 1179656 | tf_op jit(solution)/shard_map/ppermute | solution.py:22
  172.9 18.5 %all-to-all-start.2 = ((bf16[16,2,7680]{2,1,0:T(2,128)(2,1)}), bf16[16,2,7680]{2,1,0:T(2,128)(2,1)S(1)}, u32[]{:S(2)}, u32[]{:S(2)}) async-start(bf16[16,2,7680]{2,1,0:T(2,128)(2,1)} %pad_maximum_fusion), calls=%async_computation.2 | async-start | bytes 983040 | tf_op jit(solution)/shard_map/all_to_all | solution.py:262

commit v5 on v4

--- a/solution.py
+++ b/solution.py
@@ -28,30 +28,121 @@
     return lax.all_to_all(copies, axis, split_axis=0, concat_axis=0, tiled=True)
 
 
-def attention(query_rows, key_rows, value_rows, forget, head_state):
+def split(array):
+    high = array.astype(BF16)
+    return high, (array - high.astype(F32)).astype(BF16)
+
+
+def attend_kernel(capacity, forget_ref, ids_ref, *refs):
+    sources, out_ref, flat, landed, arrived = refs[:4], refs[4], refs[5], refs[6:10], refs[10]
+    copies = [
+        pltpu.make_async_copy(source, target, arrived.at[i])
+        for i, (source, target) in enumerate(zip(sources, landed))
+    ]
+    for copy in copies:
+        copy.start()
+    query_ref, key_ref, value_ref, state_ref = landed
+    steps, rows, width = query_ref.shape
+    heads, size = state_ref.shape[1], state_ref.shape[2]
+    count = steps * rows
+    shape = (count, LANES)
+    row, lane = (lax.broadcasted_iota(jnp.int32, shape, i) for i in range(2))
+    tail = jnp.zeros(shape, jnp.int32)
+    for t in range(steps):
+        ids = [ids_ref[t, i // 2, i % 2] for i in range(2 * rows)]
+        for i in range(2 * rows):
+            slot = sum((jnp.where(ids[j] == ids[i], 1, 0) for j in range(i)), jnp.int32(0))
+            here = (row == t * rows + i // 2) & (lane == i % 2)
+            tail = jnp.where(here, ids[i] * capacity + slot, tail)
+    tail = tail.astype(F32).astype(BF16)
+    for copy in copies:
+        copy.wait()
+    for i, ref in enumerate((query_ref, key_ref, value_ref)):
+        for t in range(steps):
+            flat[i, t * rows : (t + 1) * rows] = ref[t].astype(F32)
+    row_of = lax.broadcasted_iota(jnp.int32, (count, 1), 0)
+    age = (row_of // rows + 1).astype(F32)
+    member = row_of % rows
+    one = lax.broadcasted_iota(jnp.int32, (count, count), 0)
+    other = lax.broadcasted_iota(jnp.int32, (count, count), 1)
+    lag = one // rows - other // rows
+    seen = (lag >= 0) & (one % rows == other % rows)
+    gap = jnp.maximum(lag, 0).astype(F32)
+    for h in range(heads):
+        lanes = slice(h * size, (h + 1) * size)
+        rate = forget_ref[h]
+        query, key, value = (flat[i, :, lanes].astype(BF16) for i in range(3))
+        from_state = jnp.zeros((count, size), F32)
+        for r in range(rows):
+            product = jnp.dot(query, state_ref[r, h], preferred_element_type=F32)
+            from_state += jnp.where(member == r, product, 0.0)
+        scores = across_lanes(query, key) * jnp.where(seen, jnp.exp(-rate * gap), 0.0)
+        from_steps = sum(jnp.dot(s, value, preferred_element_type=F32) for s in split(scores))
+        attended = (jnp.exp(-rate * age) * from_state + from_steps).astype(BF16)
+        for i in range(out_ref.shape[0]):
+            out_ref[i, :, lanes] = attended
+    for i in range(out_ref.shape[0]):
+        out_ref[i, :, width:] = tail
+
+
+def attend(query_rows, key_rows, value_rows, forget, head_state, route_ids, capacity, copies):
     steps, rows, width = query_rows.shape
-    heads = forget.shape[0]
-    size = width // heads
-    shape = (steps, rows, heads, size)
-    query, key, value = (a.reshape(shape) for a in (query_rows, key_rows, value_rows))
-    times = jnp.arange(steps, dtype=F32)
-    power = jnp.exp(-forget[None, :] * jnp.arange(steps + 1, dtype=F32)[:, None])
-    lag = times[:, None] - times[None, :]
-    causal = jnp.where(
-        lag[..., None] >= 0, jnp.exp(-forget * jnp.maximum(lag, 0.0)[..., None]), 0.0
-    )
-    from_state = jnp.einsum("trhi,rhij->trhj", query, head_state, preferred_element_type=F32)
-    scores = jnp.einsum("trhi,srhi->tsrh", query, key, preferred_element_type=F32)
-    scores = scores * causal[:, :, None, :]
-    value_float = value.astype(F32)
-    from_steps = sum(scores[:, s, :, :, None] * value_float[s][None] for s in range(steps))
-    attended = power[1:, None, :, None] * from_state + from_steps
-    attended = attended.astype(BF16).reshape(steps * rows, width)
-    scaled_key = key.astype(F32) * power[steps - 1 :: -1][:steps, None, :, None]
-    state = power[steps][None, :, None, None] * head_state.astype(F32) + jnp.einsum(
-        "trhi,trhj->rhij", scaled_key, value_float, precision=EXACT
-    )
-    return attended, state.astype(BF16)
+    count = steps * rows
+    whole = pl.BlockSpec(memory_space=pltpu.VMEM)
+    return pl.pallas_call(
+        functools.partial(attend_kernel, capacity),
+        in_specs=[pl.BlockSpec(memory_space=pltpu.SMEM)] * 2
+        + [pl.BlockSpec(memory_space=pltpu.HBM)] * 4,
+        out_specs=whole,
+        out_shape=jax.ShapeDtypeStruct((copies, count, width + LANES), BF16),
+        scratch_shapes=[pltpu.VMEM((3, count, width), F32)]
+        + [pltpu.VMEM(query_rows.shape, BF16)] * 3
+        + [pltpu.VMEM(head_state.shape, BF16), pltpu.SemaphoreType.DMA((4,))],
+        compiler_params=pltpu.CompilerParams(vmem_limit_bytes=54 * 1024 * 1024),
+    )(forget, route_ids, query_rows, key_rows, value_rows, head_state)
+
+
+def state_kernel(forget_ref, key_ref, value_ref, state_ref, out_ref, flat):
+    steps, rows, width = key_ref.shape
+    heads, size = state_ref.shape[1], state_ref.shape[2]
+    count = steps * rows
+    for i, ref in enumerate((key_ref, value_ref)):
+        for t in range(steps):
+            flat[i, t * rows : (t + 1) * rows] = ref[t].astype(F32)
+    row_of = lax.broadcasted_iota(jnp.int32, (count, 1), 0)
+    left = (steps - 1 - row_of // rows).astype(F32)
+    member = row_of % rows
+    for h in range(heads):
+        lanes = slice(h * size, (h + 1) * size)
+        rate = forget_ref[h]
+        decay = jnp.exp(-rate * jnp.full((1, 1), steps, F32))
+        scaled = flat[0, :, lanes] * jnp.exp(-rate * left)
+        value = flat[1, :, lanes].astype(BF16)
+        values = jnp.concatenate([value, value], axis=0)
+        for r in range(rows):
+            terms = jnp.concatenate(split(jnp.where(member == r, scaled, 0.0)), axis=0)
+            added = lax.dot_general(
+                terms, values, (((0,), (0,)), ((), ())), preferred_element_type=F32
+            )
+            out_ref[r, h] = (decay * state_ref[r, h].astype(F32) + added).astype(BF16)
+
+
+def last_state(key_rows, value_rows, forget, head_state):
+    steps, rows, width = key_rows.shape
+    whole = pl.BlockSpec(memory_space=pltpu.VMEM)
+    return pl.pallas_call(
+        state_kernel,
+        in_specs=[pl.BlockSpec(memory_space=pltpu.SMEM)] + [whole] * 3,
+        out_specs=whole,
+        out_shape=jax.ShapeDtypeStruct(head_state.shape, BF16),
+        scratch_shapes=[pltpu.VMEM((2, steps * rows, width), F32)],
+        compiler_params=pltpu.CompilerParams(vmem_limit_bytes=12 * 1024 * 1024),
+        cost_estimate=pl.CostEstimate(
+            flops=4 * steps * rows * head_state.size,
+            bytes_accessed=4 * head_state.size,
+            transcendentals=0,
+        ),
+    )(forget, key_rows, value_rows, head_state)
 
 
 def place(ids, experts, capacity):
@@ -148,7 +239,7 @@
 def expert_ffn(parts, gate, up, down):
     width, features = gate[0].shape
     total_rows = sum(p.shape[0] for p in parts)
-    tile = min(features, 2048)
+    tile = min(features, 3072)
     inner = features // tile
 
     def first(i):
@@ -169,7 +260,7 @@
             pltpu.VMEM((total_rows, 4 * width), F32),
             pltpu.VMEM((total_rows, 2 * width), BF16),
         ],
-        compiler_params=pltpu.CompilerParams(vmem_limit_bytes=28 * 1024 * 1024),
+        compiler_params=pltpu.CompilerParams(vmem_limit_bytes=40 * 1024 * 1024),
         cost_estimate=pl.CostEstimate(
             flops=12 * total_rows * features * width,
             bytes_accessed=12 * features * width + 4 * total_rows * features,
@@ -178,20 +269,59 @@
     )(*parts, *gate, *up, *down)
 
 
-def peer_columns(columns):
-    def ordered(shape, own, other, axis, where):
-        index = lax.axis_index(axis)
-        whole = jnp.zeros(shape, own.dtype)
-        for part, position in ((own, index), (other, 1 - index)):
-            whole = lax.dynamic_update_slice_in_dim(whole, part, position, where)
-        return whole
-
+def peer_columns(columns, payload, weights):
     here, depth = columns.shape
-    columns = columns[None]
-    columns = ordered((2, here, depth), columns, shift(columns, "zl", 1), "zl", 0)[None]
-    columns = ordered((2, 2, here, depth), columns, shift(columns, "yl", 1), "yl", 0)[:, :, None]
-    columns = ordered((2, 2, 2, here, depth), columns, shift(columns, "core", 1), "core", 2)
-    return columns.reshape(8 * here, depth)
+    yl, zl, core = (lax.axis_index(axis) == 0 for axis in ("yl", "zl", "core"))
+    by_zl, by_yl = shift(columns, "zl", 1), shift(columns, "yl", 1)
+    by_both = lax.ppermute(columns, ("yl", "zl"), [(i, 3 - i) for i in range(4)])
+
+    def ordered(first, own, other):
+        return jnp.where(first, own, other), jnp.where(first, other, own)
+
+    low, high = ordered(zl, columns, by_zl), ordered(zl, by_yl, by_both)
+    first, second = ordered(yl, low[0], high[0]), ordered(yl, low[1], high[1])
+    quad = jnp.stack([first[0], second[0], first[1], second[1]])
+    quad, weights, _ = lax.optimization_barrier((quad, weights, payload))
+    whole = jnp.stack(ordered(core, quad, shift(quad, "core", 1)), axis=1)
+    return jnp.pad(whole.reshape(8 * here, depth), ((0, 0), (0, LANES))), weights
+
+
+def pack_kernel(code_ref, *refs):
+    terms, (sum_ref, out_ref, flat) = refs[:-3], refs[-3:]
+    peers, rows, width = terms[0].shape
+    experts, halves, places, half = out_ref.shape
+    for p in range(peers):
+        flat[p * rows : (p + 1) * rows] = sum(term[p] for term in terms)
+    total = flat[...].astype(BF16)
+    sum_ref[...] = total
+    shape = (peers * rows, experts * places)
+    lane = lax.broadcasted_iota(jnp.int32, shape, 1)
+    peer = lax.broadcasted_iota(jnp.int32, shape, 0) // rows
+    slot = (lane // peers).astype(F32)
+    hit = (slot == code_ref[:, 0:1]) | (slot == code_ref[:, 1:2])
+    route = jnp.where(hit & (lane % peers == peer), 1.0, 0.0).astype(BF16)
+    packed = lax.dot_general(
+        route, total, (((0,), (0,)), ((), ())), preferred_element_type=F32
+    ).astype(BF16)
+    for e in range(experts):
+        for i in range(halves):
+            out_ref[e, i] = packed[e * places : (e + 1) * places, i * half : (i + 1) * half]
+
+
+def pack(codes, terms, experts, capacity):
+    peers, rows, width = terms[0].shape
+    whole = pl.BlockSpec(memory_space=pltpu.VMEM)
+    return pl.pallas_call(
+        pack_kernel,
+        in_specs=[whole] * (1 + len(terms)),
+        out_specs=[whole] * 2,
+        out_shape=[
+            jax.ShapeDtypeStruct((peers * rows, width), BF16),
+            jax.ShapeDtypeStruct((experts, 2, capacity * peers, width // 2), BF16),
+        ],
+        scratch_shapes=[pltpu.VMEM((peers * rows, width), F32)],
+        compiler_params=pltpu.CompilerParams(vmem_limit_bytes=8 * 1024 * 1024),
+    )(codes, *terms)
 
 
 def shards(
@@ -214,42 +344,41 @@
     capacity = rows // 2
     head = lax.axis_index("head")
 
-    gate, up, down = (
-        (w, shift(w, "core", 1)) for w in (gate_weight[0].T, up_weight[0].T, down_weight[0])
+    payload = attend(
+        query_rows, key_rows, value_rows, forget, head_state, route_ids, capacity, peers
     )
-    columns = peer_columns(out_weight.T)
+    state_out = last_state(key_rows, value_rows, forget, head_state)
+    own = (gate_weight[0].T, up_weight[0].T, down_weight[0])
+    columns, own = peer_columns(out_weight.T, payload, own)
     width = columns.shape[0]
     piece_width = width // 2
     features = width * peers
-
-    attended, state_out = attention(query_rows, key_rows, value_rows, forget, head_state)
-
-    ids = jnp.pad(route_ids.reshape(steps * rows, 2).astype(BF16), ((0, 0), (0, LANES - 2)))
-    gathered = spread(jnp.concatenate([attended, ids], axis=1), PEERS)
-    gathered, gate, up, down = lax.optimization_barrier((gathered, gate, up, down))
-    gathered = gathered.reshape(peers * steps * rows, depth + LANES)
+    gathered = lax.all_to_all(payload, PEERS, split_axis=0, concat_axis=0, tiled=True)
+    other = tuple(shift(w, "core", 1) for w in own)
+    gathered, other = lax.optimization_barrier((gathered, other))
+    gate, up, down = zip(own, other)
+
     partial = lax.dot_general(
-        gathered[:, :depth], columns, (((1,), (1,)), ((), ())), preferred_element_type=F32
-    )
-    partial = partial.reshape(peers, steps, rows, width)
-    peer_ids = gathered[:, depth : depth + 2].astype(jnp.int32).reshape(peers, steps, rows, 2)
-
-    def of_step(array, axis, there=head):
-        return lax.dynamic_index_in_dim(array, there, axis, keepdims=False)
-
-    projected = of_step(partial, 1)
+        gathered.reshape(peers * steps * rows, depth + LANES),
+        columns,
+        (((1,), (1,)), ((), ())),
+        preferred_element_type=F32,
+    ).reshape(peers, steps * rows, width)
+    partial = lax.optimization_barrier(partial)
+
+    def of_step(array, axis, there=head, size=1):
+        return lax.dynamic_slice_in_dim(array, there * size, size, axis)
+
+    terms = [of_step(partial, 1, size=rows)]
     for distance in range(1, steps):
         there = lax.rem(head + distance, steps)
-        projected = projected + shift(of_step(partial, 1, there), "head", distance)
-    projected = projected.astype(BF16)
-
-    placed = jnp.sum(place(of_step(peer_ids, 1), experts, capacity), axis=-1)
-    packed = sum(
-        placed[:, :, :, r, None] * projected[:, r].astype(F32)[None, None] for r in range(rows)
-    ).astype(BF16)
+        terms.append(shift(of_step(partial, 1, there, rows), "head", distance))
+    codes = of_step(gathered[..., depth:], 1, size=rows).reshape(peers * rows, LANES)
+
+    projected, packed = pack(codes.astype(F32), terms, experts, capacity)
     packed = lax.all_to_all(packed, BLOCKS, split_axis=0, concat_axis=0, tiled=True)
-    packed = packed.reshape(2, 2, peers // 2, capacity, peers, 2, piece_width)
-    piece = jnp.transpose(packed, (1, 3, 4, 0, 5, 2, 6)).reshape(capacity * blocks, features)
+    packed = packed.reshape(2, 2, peers // 2, 2, capacity, peers, piece_width)
+    piece = jnp.transpose(packed, (1, 4, 5, 0, 3, 2, 6)).reshape(capacity * blocks, features)
 
     pieces = gather_block(piece)
     pieces[-1], state_out = lax.optimization_barrier((pieces[-1], state_out))
@@ -266,7 +395,7 @@
     mixed = lax.dynamic_index_in_dim(mixed, lax.axis_index("yl"), 1, keepdims=False)
     mixed = jnp.transpose(mixed, (2, 0, 3, 1, 4)).reshape(rows, features)
     weights = jnp.sum(
-        place(of_step(route_ids, 0), experts, capacity) * of_step(route_gate, 0), axis=-1
+        place(of_step(route_ids, 0)[0], experts, capacity) * of_step(route_gate, 0)[0], axis=-1
     )
     combined = jnp.einsum(
         "esr,esd->rd", weights, result[..., :features].astype(F32), precision=EXACT

time: 212 us -> 187 us (0.88)
  local copies, waits for them, and re-layouts: 38.2 us -> 6.17 us
  Pallas kernels: 11.6 us -> 19.4 us
  blocking collectives: 34 us -> 40.4 us
  waiting for transfers between devices: 62.2 us -> 68.4 us
  matrix products: 8.09 us -> 2.54 us
  other arithmetic: 9.43 us -> 6.15 us
  starting transfers between devices: 45.2 us -> 42.6 us
    ppermute x25, waiting for transfers between devices: 39.4 us -> 51 us  [shift(): return lax.ppermute(array, axis, pairs)]
    dynamic_update_slice x6 -> x0, local copies, waits for them, and re-layouts: 7.6 us -> none  [ordered(): whole = lax.dynamic_update_slice_in_dim(whole, part, position, where)]
    reshape x5 -> x1, local copies, waits for them, and re-layouts: 7.13 us -> 0.05 us  [shards(): packed = packed.reshape(2, 2, peers // 2, 2, capacity, peers, piece_width)]
    pallas_call x0 -> x3, Pallas kernels: none -> 6.91 us  [the longest x1 4.52 us: attend(): pl.pallas_call(functools.partial(attend_kernel, capacity), in_specs=[pl.B...]
    dot_general x4 -> x1, matrix products: 7.73 us -> 2.18 us  [shards(): lax.dot_general(gathered.reshape(peers * steps * rows, depth + LANES), co...]
    all_to_all x1, blocking collectives: 17.4 us -> 22.1 us  [shards(): lax.all_to_all(packed, BLOCKS, split_axis=0, concat_axis=0, tiled=True)]
    all_to_all x1, waiting for transfers between devices: 8.19 us -> 3.91 us  [shards(): lax.all_to_all(payload, PEERS, split_axis=0, concat_axis=0, tiled=True)]
    convert_element_type x5 -> x1, other arithmetic: 4.1 us -> 0.01 us  [shards(): projected, packed = pack(codes.astype(F32), terms, experts, capacity)]
  transfers between devices with their start and end apart: 27 -> 28, of which waited for: 13 -> 18; matrix products, arithmetic and copies ran while one was open for 17% -> 3% of each run, Pallas kernels for 0% -> 4%
where the time goes in v5:
time: 187 us
  waiting for transfers between devices  68.4 us (37%)
  starting transfers between devices  42.6 us (23%)
  blocking collectives  40.4 us (22%)
  Pallas kernels  19.4 us (10%)
  local copies, waits for them, and re-layouts  6.17 us (3%)
  other arithmetic  6.15 us (3%)
  matrix products  2.54 us (1%)
    ppermute x25, waiting for transfers between devices, shift(): return lax.ppermute(array, axis, pairs)  51 us
    ppermute x25, starting transfers between devices, shift(): return lax.ppermute(array, axis, pairs)  28.7 us
    all_to_all x1, blocking collectives, shards(): lax.all_to_all(packed, BLOCKS, split_axis=0, concat_axis=0, tiled=True)  22.1 us
    all_to_all x1, blocking collectives, spread(): return lax.all_to_all(copies, axis, split_axis=0, concat_axis=0, tiled=True)  18.3 us
    all_to_all x1, waiting for transfers between devices, shards(): lax.all_to_all(jnp.concatenate([result, mixed], axis=2), BLOCKS, split_ax...  13.5 us
    pallas_call x1, Pallas kernels, expert_ffn(): pl.pallas_call(functools.partial(ffn_kernel, len(parts), inner), grid=(2...  12.5 us
    all_to_all x1, starting transfers between devices, shards(): lax.all_to_all(payload, PEERS, split_axis=0, concat_axis=0, tiled=True)  10.2 us
    pallas_call x1, Pallas kernels, attend(): pl.pallas_call(functools.partial(attend_kernel, capacity), in_specs=[pl.B...  4.52 us
  transfers between devices with their start and end apart: 28, of which 18 were waited for; matrix products, arithmetic and copies ran while one was open for 3% of the time, Pallas kernels for 4%

profile of v5, /device:TPU:2, one launch (start us, length us, event | category | flops | bytes accessed | tf_op | source)
XLA Modules:
  0.0 186.8 jit_solution(15252855245239646473)
XLA Ops:
  0.6 2.0 %collective-permute-start = (bf16[96,1024]{1,0:T(8,128)(2,1)}, bf16[96,1024]{1,0:T(8,128)(2,1)}, u32[]{:S(2)}, u32[]{:S(2)}) collective-permute-start(bf16[96,1024]{1,0:T(8,128)(2,1)} %bitcast.69), channel_id=1, source_target_pairs={{0,2},{2,0},{1,3},{3,1},{4,6},{6,4},{5,7},{7,5},{8,10},{10,8},{9,1... | collective-permute-start | bytes 589832 | tf_op jit(solution)/shard_map/ppermute | solution.py:22
  2.6 1.6 collective-permute-start.1
  4.2 1.4 copy.54.ids_ref
  5.6 4.5 %shard_map.130 = bf16[8,16,1152]{2,1,0:T(8,128)(2,1)} custom-call(f32[8]{0:T(128)} %forget_ref.3, s32[4,4,2]{2,1,0:T(4,128)} %copy.54.ids_ref, bf16[4,4,1024]{2,1,0:T(4,128)(2,1)} %refs_0_.1, bf16[4,4,1024]{2,1,0:T(4,128)(2,1)} %key_ref.1, bf16[4,4,1024]{2,1,0:T(4,128)(2,1)} %value_ref.1, bf16[4,8,128,128]{3,2,1,0:T(8,128)(2,1)} %state_ref.1), custom_call_target="tpu_custom_call" | custom-call | tf_op jit(solution)/shard_map/pallas_call | solution.py:92
  10.1 3.4 %collective-permute-done.1 = bf16[96,1024]{1,0:T(8,128)(2,1)} collective-permute-done((bf16[96,1024]{1,0:T(8,128)(2,1)}, bf16[96,1024]{1,0:T(8,128)(2,1)}, u32[]{:S(2)}, u32[]{:S(2)}) %collective-permute-start.1) | collective-permute-done | bytes 196640 | tf_op jit(solution)/shard_map/ppermute | solution.py:22
  13.5 1.3 select_bitcast_fusion.5
  14.8 1.0 pad_maximum_fusion.1
  15.8 0.5 collective-permute-start.4
  16.3 0.5 collective-permute-start.6
  16.8 10.2 %all-to-all-start = ((bf16[8,16,1152]{2,1,0:T(8,128)(2,1)}), bf16[8,16,1152]{2,1,0:T(8,128)(2,1)}, u32[]{:S(2)}, u32[]{:S(2)}) async-start(bf16[8,16,1152]{2,1,0:T(8,128)(2,1)} %shard_map.130), calls=%async_computation | async-start | bytes 589824 | tf_op jit(solution)/shard_map/all_to_all | solution.py:356
  27.0 6.6 %collective-permute-done.6 = bf16[4,96,1024]{2,1,0:T(8,128)(2,1)} collective-permute-done((bf16[4,96,1024]{2,1,0:T(8,128)(2,1)}, bf16[4,96,1024]{2,1,0:T(8,128)(2,1)}, u32[]{:S(2)}, u32[]{:S(2)}) %collective-permute-start.6) | collective-permute-done | bytes 786464 | tf_op jit(solution)/shard_map/ppermute | solution.py:22
  33.6 1.5 select_bitcast_fusion.1
  35.1 0.1 pad_maximum_fusion
  35.3 1.4 copy.55
  36.6 3.9 %all-to-all-done = bf16[8,16,1152]{2,1,0:T(8,128)(2,1)} async-done(((bf16[8,16,1152]{2,1,0:T(8,128)(2,1)}), bf16[8,16,1152]{2,1,0:T(8,128)(2,1)}, u32[]{:S(2)}, u32[]{:S(2)}) %all-to-all-start) | async-done | bytes 294944 | tf_op jit(solution)/shard_map/all_to_all | solution.py:356
  40.5 0.8 slice.69
  41.3 2.2 %fusion.1 = f32[8,16,768]{2,1,0:T(8,128)S(1)} fusion(bf16[8,16,1152]{2,1,0:T(8,128)(2,1)} %all-to-all-done, bf16[768,1024]{1,0:T(8,128)(2,1)} %bitcast.60), kind=kOutput, calls=%fused_computation.2 | convolution fusion | flops 226492416 | bytes 2260992 | tf_op jit(solution)/shard_map/dot_general | solution.py:361
  43.6 1.6 collective-permute-start.7
  45.2 1.1 collective-permute-start.8
  46.3 2.2 %collective-permute-start.9 = (f32[8,4,768]{2,1,0:T(4,128)S(1)}, f32[8,4,768]{2,1,0:T(4,128)S(1)}, u32[]{:S(2)}, u32[]{:S(2)}) collective-permute-start(f32[8,4,768]{2,1,0:T(4,128)S(1)} %get-tuple-element.65), channel_id=1, source_target_pairs={{0,192},{64,0},{128,64},{192,128},{1,193},{65,1},{129,65},{193,129... | collective-permute-start | bytes 294920 | tf_op jit(solution)/shard_map/ppermute | solution.py:22
  48.5 2.9 %collective-permute-done.8.refs_2_ = f32[8,4,768]{2,1,0:T(4,128)S(1)} collective-permute-done((f32[8,4,768]{2,1,0:T(4,128)S(1)}, f32[8,4,768]{2,1,0:T(4,128)S(1)}, u32[]{:S(2)}, u32[]{:S(2)}) %collective-permute-start.8) | collective-permute-done | bytes 98336 | tf_op jit(solution)/shard_map/ppermute | solution.py:22
  51.4 0.5 collective-permute-done.9.refs_3_
  51.9 0.4 shard_map.131
  52.3 22.1 %all_to_all.20 = bf16[16,2,16,384]{3,2,1,0:T(8,128)(2,1)S(1)} all-to-all(bf16[16,2,16,384]{3,2,1,0:T(8,128)(2,1)S(1)} %get-tuple-element.29), channel_id=1, replica_groups=mesh['head'=4,'yh'=2,'yl'=2,'zp'=4,'zl'=2,'core'=2] {'yh','yl','zp'}, dimensions={0} | all-to-all | bytes 786432 | tf_op jit(solution)/shard_map/all_to_all | solution.py:379
  74.5 1.0 collective-permute-start.11
  75.5 1.0 collective-permute-start.12
  76.5 1.0 collective-permute-start.10
  77.5 5.0 %collective-permute-done.11.refs_2_ = bf16[32,6144]{1,0:T(8,128)(2,1)S(1)} collective-permute-done((bf16[32,6144]{1,0:T(8,128)(2,1)S(1)}, bf16[32,6144]{1,0:T(8,128)(2,1)S(1)}, u32[]{:S(2)}, u32[]{:S(2)}) %collective-permute-start.11) | collective-permute-done | bytes 393248 | tf_op jit(solution)/shard_map/ppermute | solution.py:22
  82.6 1.8 collective-permute-done.12.refs_3_
  84.5 1.5 collective-permute-start.14
  86.1 0.9 collective-permute-start.13
  87.0 1.2 collective-permute-start.15
  88.2 5.6 %collective-permute-done.14.refs_5_ = bf16[32,6144]{1,0:T(8,128)(2,1)S(1)} collective-permute-done((bf16[32,6144]{1,0:T(8,128)(2,1)S(1)}, bf16[32,6144]{1,0:T(8,128)(2,1)S(1)}, u32[]{:S(2)}, u32[]{:S(2)}) %collective-permute-start.14) | collective-permute-done | bytes 393248 | tf_op jit(solution)/shard_map/ppermute | solution.py:22
  93.8 2.1 %collective-permute-start.17 = (bf16[16,6144]{1,0:T(8,128)(2,1)S(1)}, bf16[16,6144]{1,0:T(8,128)(2,1)S(1)}, u32[]{:S(2)}, u32[]{:S(2)}) collective-permute-start(bf16[16,6144]{1,0:T(8,128)(2,1)S(1)} %slice.99), channel_id=1, source_target_pairs={{0,192},{64,0},{128,64},{192,128},{1,193},{65,1},{129,65},{193,129... | collective-permute-start | bytes 589832 | tf_op jit(solution)/shard_map/ppermute | solution.py:22
  96.1 2.0 %shard_map.132 = bf16[4,8,128,128]{3,2,1,0:T(8,128)(2,1)} custom-call(f32[8]{0:T(128)S(1)} %copy-done.9, bf16[4,4,1024]{2,1,0:T(4,128)(2,1)S(1)} %copy-done.5, bf16[4,4,1024]{2,1,0:T(4,128)(2,1)S(1)} %copy-done.6, bf16[4,8,128,128]{3,2,1,0:T(8,128)(2,1)S(1)} %copy-done.1), custom_call_target="tpu_custom_call" | custom-call | flops 33554432 | bytes 2097152 | tf_op jit(solution)/shard_map/pallas_call | solution.py:133
  98.1 1.5 collective-permute-done.17.refs_8_
  99.6 2.5 %collective-permute-done.16.refs_7_ = bf16[16,6144]{1,0:T(8,128)(2,1)S(1)} collective-permute-done((bf16[16,6144]{1,0:T(8,128)(2,1)S(1)}, bf16[16,6144]{1,0:T(8,128)(2,1)S(1)}, u32[]{:S(2)}, u32[]{:S(2)}) %collective-permute-start.16) | collective-permute-done | bytes 196640 | tf_op jit(solution)/shard_map/ppermute | solution.py:22
  102.0 12.5 %shard_map.133 = (bf16[32,6144]{1,0:T(8,128)(2,1)S(1)}, bf16[32,6144]{1,0:T(8,128)(2,1)S(1)}, bf16[32,6144]{1,0:T(8,128)(2,1)S(1)}, bf16[32,6144]{1,0:T(8,128)(2...) custom-call(bf16[32,6144]{1,0:T(8,128)(2,1)S(1)} %bitcast.59, ...), custom_call_target="tpu_custom_call" | custom-call | flops 5435817984 | bytes 27525120 | tf_op jit(solution)/shard_map/pallas_call | solution.py:251
  114.6 3.3 %collective-permute-start.18 = (bf16[16,6144]{1,0:T(8,128)(2,1)S(1)}, bf16[16,6144]{1,0:T(8,128)(2,1)S(1)}, u32[]{:S(2)}, u32[]{:S(2)}) collective-permute-start(bf16[16,6144]{1,0:T(8,128)(2,1)S(1)} %get-tuple-element.37), channel_id=1, source_target_pairs={{0,192},{64,0},{128,64},{192,128},{1,193},{65,1},{129,65},{193,129... | collective-permute-start | bytes 589832 | tf_op jit(solution)/shard_map/ppermute | solution.py:22
  117.9 0.8 collective-permute-start.20
  118.7 4.5 %collective-permute-done.18 = bf16[16,6144]{1,0:T(8,128)(2,1)S(1)} collective-permute-done((bf16[16,6144]{1,0:T(8,128)(2,1)S(1)}, bf16[16,6144]{1,0:T(8,128)(2,1)S(1)}, u32[]{:S(2)}, u32[]{:S(2)}) %collective-permute-start.18) | collective-permute-done | bytes 196640 | tf_op jit(solution)/shard_map/ppermute | solution.py:22
  123.3 2.6 %collective-permute-start.19 = (bf16[32,6144]{1,0:T(8,128)(2,1)S(1)}, bf16[32,6144]{1,0:T(8,128)(2,1)S(1)}, u32[]{:S(2)}, u32[]{:S(2)}) collective-permute-start(bf16[32,6144]{1,0:T(8,128)(2,1)S(1)} %pad_maximum_fusion.6), channel_id=1, source_target_pairs={{0,192},{64,0},{128,64},{192,128},{1,193},{65,1},{129,65},{193,129... | collective-permute-start | bytes 1179656 | tf_op jit(solution)/shard_map/ppermute | solution.py:22
  125.9 0.7 collective-permute-done.22
  126.8 8.4 %collective-permute-done.19 = bf16[32,6144]{1,0:T(8,128)(2,1)S(1)} collective-permute-done((bf16[32,6144]{1,0:T(8,128)(2,1)S(1)}, bf16[32,6144]{1,0:T(8,128)(2,1)S(1)}, u32[]{:S(2)}, u32[]{:S(2)}) %collective-permute-start.19) | collective-permute-done | bytes 393248 | tf_op jit(solution)/shard_map/ppermute | solution.py:22
  135.3 0.1 add_convert_fusion.3
  135.4 2.3 %collective-permute-start.21 = (bf16[32,6144]{1,0:T(8,128)(2,1)S(1)}, bf16[32,6144]{1,0:T(8,128)(2,1)S(1)}, u32[]{:S(2)}, u32[]{:S(2)}) collective-permute-start(bf16[32,6144]{1,0:T(8,128)(2,1)S(1)} %add_convert_fusion.3), channel_id=1, source_target_pairs={{0,192},{64,0},{128,64},{192,128},{1,193},{65,1},{129,65},{193,129... | collective-permute-start | bytes 1179656 | tf_op jit(solution)/shard_map/ppermute | solution.py:22
  137.7 1.0 collective-permute-done.23
  138.7 0.1 add_convert_fusion.2
  138.9 0.1 add_convert_fusion.1
  139.0 1.3 collective-permute-start.25
  140.3 0.1 copy.59
  140.5 2.7 %collective-permute-done.21 = bf16[32,6144]{1,0:T(8,128)(2,1)S(1)} collective-permute-done((bf16[32,6144]{1,0:T(8,128)(2,1)S(1)}, bf16[32,6144]{1,0:T(8,128)(2,1)S(1)}, u32[]{:S(2)}, u32[]{:S(2)}) %collective-permute-start.21) | collective-permute-done | bytes 393248 | tf_op jit(solution)/shard_map/ppermute | solution.py:22
  143.2 3.4 %collective-permute-done.24 = bf16[32,6144]{1,0:T(8,128)(2,1)S(1)} collective-permute-done((bf16[32,6144]{1,0:T(8,128)(2,1)S(1)}, bf16[32,6144]{1,0:T(8,128)(2,1)S(1)}, u32[]{:S(2)}, u32[]{:S(2)}) %collective-permute-start.24) | collective-permute-done | bytes 393248 | tf_op jit(solution)/shard_map/ppermute | solution.py:22
  146.6 0.4 collective-permute-done.25
  147.0 0.2 add_convert_fusion
  147.2 0.2 reshape.106
  147.4 0.4 copy.57
  147.9 1.2 pad_maximum_fusion.2
  149.1 3.7 %all-to-all-start.2 = ((bf16[16,2,7680]{2,1,0:T(2,128)(2,1)}), bf16[16,2,7680]{2,1,0:T(2,128)(2,1)S(1)}, u32[]{:S(2)}, u32[]{:S(2)}) async-start(bf16[16,2,7680]{2,1,0:T(2,128)(2,1)} %pad_maximum_fusion.2), calls=%async_computation.2 | async-start | bytes 983040 | tf_op jit(solution)/shard_map/all_to_all | solution.py:391
  153.1 13.5 %all-to-all-done.2 = bf16[16,2,7680]{2,1,0:T(2,128)(2,1)S(1)} async-done(((bf16[16,2,7680]{2,1,0:T(2,128)(2,1)}), bf16[16,2,7680]{2,1,0:T(2,128)(2,1)S(1)}, u32[]{:S(2)}, u32[]{:S(2)}) %all-to-all-start.2) | async-done | bytes 491552 | tf_op jit(solution)/shard_map/all_to_all | solution.py:391
  166.9 0.3 slice.107
  167.2 0.4 fusion
  167.6 18.3 %all_to_all.21 = bf16[4,8,6144]{2,1,0:T(8,128)(2,1)S(1)} all-to-all(bf16[4,8,6144]{2,1,0:T(8,128)(2,1)S(1)} %broadcast_in_dim.8), channel_id=1, replica_groups=mesh['head'=4,'yh'=2,'yl'=2,'zp'=4,'zl'=2,'core'=2] {'head'}, dimensions={0} | all-to-all | bytes 786432 | tf_op jit(solution)/shard_map/all_to_all | solution.py:28
  185.9 0.9 fusion.9
  (79 shorter events, 1.7 us)
Async XLA Ops:
  0.6 152.3 %copy-start = (f32[4,4,2]{1,2,0:T(2,128)S(1)}, f32[4,4,2]{1,2,0:T(2,128)}, u32[]{:S(2)}) copy-start(f32[4,4,2]{1,2,0:T(2,128)} %param.18) | copy-start | bytes 388
  0.6 9.5 %collective-permute-start = (bf16[96,1024]{1,0:T(8,128)(2,1)}, bf16[96,1024]{1,0:T(8,128)(2,1)}, u32[]{:S(2)}, u32[]{:S(2)}) collective-permute-start(bf16[96,1024]{1,0:T(8,128)(2,1)} %bitcast.69), channel_id=1, source_target_pairs={{0,2},{2,0},{1,3},{3,1},{4,6},{6,4},{5,7},{7,5},{8,10},{10,8},{9,1... | collective-permute-start | bytes 589832 | tf_op jit(solution)/shard_map/ppermute | solution.py:22
  2.6 10.9 %collective-permute-start.1 = (bf16[96,1024]{1,0:T(8,128)(2,1)}, bf16[96,1024]{1,0:T(8,128)(2,1)}, u32[]{:S(2)}, u32[]{:S(2)}) collective-permute-start(bf16[96,1024]{1,0:T(8,128)(2,1)} %bitcast.70), channel_id=1, source_target_pairs={{0,16},{16,0},{1,17},{17,1},{2,18},{18,2},{3,19},{19,3},{4,20},{20... | collective-permute-start | bytes 589832 | tf_op jit(solution)/shard_map/ppermute | solution.py:22
  4.2 9.3 %collective-permute-start.2 = (bf16[96,1024]{1,0:T(8,128)(2,1)}, bf16[96,1024]{1,0:T(8,128)(2,1)}, u32[]{:S(2)}, u32[]{:S(2)}) collective-permute-start(bf16[96,1024]{1,0:T(8,128)(2,1)} %bitcast.71), channel_id=1, source_target_pairs={{0,18},{2,16},{16,2},{18,0},{1,19},{3,17},{17,3},{19,1},{4,22},{6,... | collective-permute-start | bytes 589832 | tf_op jit(solution)/shard_map/ppermute | solution.py:276
  5.6 10.2 %copy-start.2 = (bf16[1,6144,288]{1,2,0:T(8,128)(2,1)S(1)}, bf16[1,6144,288]{1,2,0:T(8,128)(2,1)}, u32[]{:S(2)}) copy-start(bf16[1,6144,288]{1,2,0:T(8,128)(2,1)} %param.19) | copy-start | bytes 10616836
  15.8 24.7 %collective-permute-start.3 = (bf16[288,6144]{1,0:T(8,128)(2,1)S(1)}, bf16[288,6144]{1,0:T(8,128)(2,1)}, u32[]{:S(2)}, u32[]{:S(2)}) collective-permute-start(bf16[288,6144]{1,0:T(8,128)(2,1)S(1)} %bitcast.54), channel_id=1, source_target_pairs={{0,1},{1,0},{2,3},{3,2},{4,5},{5,4},{6,7},{7,6},{8,9},{9,8},{10,11... | collective-permute-start | bytes 10616840 | tf_op jit(solution)/shard_map/ppermute | solution.py:22
  15.8 24.7 %collective-permute-start.4 = (bf16[288,6144]{1,0:T(8,128)(2,1)}, bf16[288,6144]{1,0:T(8,128)(2,1)}, u32[]{:S(2)}, u32[]{:S(2)}) collective-permute-start(bf16[288,6144]{1,0:T(8,128)(2,1)} %bitcast.61), channel_id=1, source_target_pairs={{0,1},{1,0},{2,3},{3,2},{4,5},{5,4},{6,7},{7,6},{8,9},{9,8},{10,11... | collective-permute-start | bytes 10616840 | tf_op jit(solution)/shard_map/ppermute | solution.py:22
  16.3 24.2 %collective-permute-start.5 = (bf16[288,6144]{1,0:T(8,128)(2,1)}, bf16[288,6144]{1,0:T(8,128)(2,1)}, u32[]{:S(2)}, u32[]{:S(2)}) collective-permute-start(bf16[288,6144]{1,0:T(8,128)(2,1)} %bitcast.63), channel_id=1, source_target_pairs={{0,1},{1,0},{2,3},{3,2},{4,5},{5,4},{6,7},{7,6},{8,9},{9,8},{10,11... | collective-permute-start | bytes 10616840 | tf_op jit(solution)/shard_map/ppermute | solution.py:22
  16.3 17.3 %collective-permute-start.6 = (bf16[4,96,1024]{2,1,0:T(8,128)(2,1)}, bf16[4,96,1024]{2,1,0:T(8,128)(2,1)}, u32[]{:S(2)}, u32[]{:S(2)}) collective-permute-start(bf16[4,96,1024]{2,1,0:T(8,128)(2,1)} %pad_maximum_fusion.1), channel_id=1, source_target_pairs={{0,1},{1,0},{2,3},{3,2},{4,5},{5,4},{6,7},{7,6},{8,9},{9,8},{10,11... | collective-permute-start | bytes 2359304 | tf_op jit(solution)/shard_map/ppermute | solution.py:22
  16.8 23.7 %all-to-all-start = ((bf16[8,16,1152]{2,1,0:T(8,128)(2,1)}), bf16[8,16,1152]{2,1,0:T(8,128)(2,1)}, u32[]{:S(2)}, u32[]{:S(2)}) async-start(bf16[8,16,1152]{2,1,0:T(8,128)(2,1)} %shard_map.130), calls=%async_computation | async-start | bytes 589824 | tf_op jit(solution)/shard_map/all_to_all | solution.py:356
  43.6 4.9 %collective-permute-start.7 = (f32[8,4,768]{2,1,0:T(4,128)S(1)}, f32[8,4,768]{2,1,0:T(4,128)S(1)}, u32[]{:S(2)}, u32[]{:S(2)}) collective-permute-start(f32[8,4,768]{2,1,0:T(4,128)S(1)} %get-tuple-element.67), channel_id=1, source_target_pairs={{0,64},{64,128},{128,192},{192,0},{1,65},{65,129},{129,193},{193,1... | collective-permute-start | bytes 294920 | tf_op jit(solution)/shard_map/ppermute | solution.py:22
  45.2 6.2 %collective-permute-start.8 = (f32[8,4,768]{2,1,0:T(4,128)S(1)}, f32[8,4,768]{2,1,0:T(4,128)S(1)}, u32[]{:S(2)}, u32[]{:S(2)}) collective-permute-start(f32[8,4,768]{2,1,0:T(4,128)S(1)} %get-tuple-element.66), channel_id=1, source_target_pairs={{0,128},{64,192},{128,0},{192,64},{1,129},{65,193},{129,1},{193,65... | collective-permute-start | bytes 294920 | tf_op jit(solution)/shard_map/ppermute | solution.py:22
  46.3 5.7 %collective-permute-start.9 = (f32[8,4,768]{2,1,0:T(4,128)S(1)}, f32[8,4,768]{2,1,0:T(4,128)S(1)}, u32[]{:S(2)}, u32[]{:S(2)}) collective-permute-start(f32[8,4,768]{2,1,0:T(4,128)S(1)} %get-tuple-element.65), channel_id=1, source_target_pairs={{0,192},{64,0},{128,64},{192,128},{1,193},{65,1},{129,65},{193,129... | collective-permute-start | bytes 294920 | tf_op jit(solution)/shard_map/ppermute | solution.py:22
  52.3 22.1 %copy-start.7 = (bf16[32,768]{1,0:T(8,128)(2,1)}, bf16[32,768]{1,0:T(8,128)(2,1)S(1)}, u32[]{:S(2)}) copy-start(bf16[32,768]{1,0:T(8,128)(2,1)S(1)} %get-tuple-element.43) | copy-start | bytes 147460
  74.5 8.1 %collective-permute-start.11 = (bf16[32,6144]{1,0:T(8,128)(2,1)S(1)}, bf16[32,6144]{1,0:T(8,128)(2,1)S(1)}, u32[]{:S(2)}, u32[]{:S(2)}) collective-permute-start(bf16[32,6144]{1,0:T(8,128)(2,1)S(1)} %bitcast.56), channel_id=1, source_target_pairs={{0,192},{64,0},{128,64},{192,128},{1,193},{65,1},{129,65},{193,129... | collective-permute-start | bytes 1179656 | tf_op jit(solution)/shard_map/ppermute | solution.py:22
  75.5 9.0 %collective-permute-start.12 = (bf16[32,6144]{1,0:T(8,128)(2,1)S(1)}, bf16[32,6144]{1,0:T(8,128)(2,1)S(1)}, u32[]{:S(2)}, u32[]{:S(2)}) collective-permute-start(bf16[32,6144]{1,0:T(8,128)(2,1)S(1)} %bitcast.57), channel_id=1, source_target_pairs={{0,2},{2,0},{1,3},{3,1},{4,6},{6,4},{5,7},{7,5},{8,10},{10,8},{9,1... | collective-permute-start | bytes 1179656 | tf_op jit(solution)/shard_map/ppermute | solution.py:22
  76.5 9.5 %collective-permute-start.10 = (bf16[32,6144]{1,0:T(8,128)(2,1)S(1)}, bf16[32,6144]{1,0:T(8,128)(2,1)S(1)}, u32[]{:S(2)}, u32[]{:S(2)}) collective-permute-start(bf16[32,6144]{1,0:T(8,128)(2,1)S(1)} %bitcast.58), channel_id=1, source_target_pairs={{0,64},{64,128},{128,192},{192,0},{1,65},{65,129},{129,193},{193,1... | collective-permute-start | bytes 1179656 | tf_op jit(solution)/shard_map/ppermute | solution.py:22
  84.5 11.5 %copy-start.1 = (bf16[4,8,128,128]{3,2,1,0:T(8,128)(2,1)S(1)}, bf16[4,8,128,128]{3,2,1,0:T(8,128)(2,1)}, u32[]{:S(2)}) copy-start(bf16[4,8,128,128]{3,2,1,0:T(8,128)(2,1)} %state_ref.1) | copy-start | bytes 3145732
  84.5 11.5 %copy-start.5 = (bf16[4,4,1024]{2,1,0:T(4,128)(2,1)S(1)}, bf16[4,4,1024]{2,1,0:T(4,128)(2,1)}, u32[]{:S(2)}) copy-start(bf16[4,4,1024]{2,1,0:T(4,128)(2,1)} %key_ref.1) | copy-start | bytes 98308
  84.5 11.5 %copy-start.6 = (bf16[4,4,1024]{2,1,0:T(4,128)(2,1)S(1)}, bf16[4,4,1024]{2,1,0:T(4,128)(2,1)}, u32[]{:S(2)}) copy-start(bf16[4,4,1024]{2,1,0:T(4,128)(2,1)} %value_ref.1) | copy-start | bytes 98308
  84.5 11.5 %copy-start.9 = (f32[8]{0:T(128)S(1)}, f32[8]{0:T(128)}, u32[]{:S(2)}) copy-start(f32[8]{0:T(128)} %forget_ref.3) | copy-start | bytes 100
  84.5 9.3 %collective-permute-start.14 = (bf16[32,6144]{1,0:T(8,128)(2,1)S(1)}, bf16[32,6144]{1,0:T(8,128)(2,1)S(1)}, u32[]{:S(2)}, u32[]{:S(2)}) collective-permute-start(bf16[32,6144]{1,0:T(8,128)(2,1)S(1)} %pad_maximum_fusion.4), channel_id=1, source_target_pairs={{0,192},{64,0},{128,64},{192,128},{1,193},{65,1},{129,65},{193,129... | collective-permute-start | bytes 1179656 | tf_op jit(solution)/shard_map/ppermute | solution.py:22
  86.1 9.8 %collective-permute-start.13 = (bf16[32,6144]{1,0:T(8,128)(2,1)S(1)}, bf16[32,6144]{1,0:T(8,128)(2,1)S(1)}, u32[]{:S(2)}, u32[]{:S(2)}) collective-permute-start(bf16[32,6144]{1,0:T(8,128)(2,1)S(1)} %pad_maximum_fusion.3), channel_id=1, source_target_pairs={{0,64},{64,128},{128,192},{192,0},{1,65},{65,129},{129,193},{193,1... | collective-permute-start | bytes 1179656 | tf_op jit(solution)/shard_map/ppermute | solution.py:22
  87.0 12.6 %collective-permute-start.15 = (bf16[32,6144]{1,0:T(8,128)(2,1)S(1)}, bf16[32,6144]{1,0:T(8,128)(2,1)S(1)}, u32[]{:S(2)}, u32[]{:S(2)}) collective-permute-start(bf16[32,6144]{1,0:T(8,128)(2,1)S(1)} %pad_maximum_fusion.5), channel_id=1, source_target_pairs={{0,2},{2,0},{1,3},{3,1},{4,6},{6,4},{5,7},{7,5},{8,10},{10,8},{9,1... | collective-permute-start | bytes 1179656 | tf_op jit(solution)/shard_map/ppermute | solution.py:22
  93.8 5.7 %collective-permute-start.17 = (bf16[16,6144]{1,0:T(8,128)(2,1)S(1)}, bf16[16,6144]{1,0:T(8,128)(2,1)S(1)}, u32[]{:S(2)}, u32[]{:S(2)}) collective-permute-start(bf16[16,6144]{1,0:T(8,128)(2,1)S(1)} %slice.99), channel_id=1, source_target_pairs={{0,192},{64,0},{128,64},{192,128},{1,193},{65,1},{129,65},{193,129... | collective-permute-start | bytes 589832 | tf_op jit(solution)/shard_map/ppermute | solution.py:22
  96.0 6.1 %collective-permute-start.16 = (bf16[16,6144]{1,0:T(8,128)(2,1)S(1)}, bf16[16,6144]{1,0:T(8,128)(2,1)S(1)}, u32[]{:S(2)}, u32[]{:S(2)}) collective-permute-start(bf16[16,6144]{1,0:T(8,128)(2,1)S(1)} %slice.98), channel_id=1, source_target_pairs={{0,64},{64,128},{128,192},{192,0},{1,65},{65,129},{129,193},{193,1... | collective-permute-start | bytes 589832 | tf_op jit(solution)/shard_map/ppermute | solution.py:22
  114.6 12.1 %copy-start.3 = (bf16[32,6144]{1,0:T(8,128)(2,1)}, bf16[32,6144]{1,0:T(8,128)(2,1)S(1)}, u32[]{:S(2)}) copy-start(bf16[32,6144]{1,0:T(8,128)(2,1)S(1)} %get-tuple-element.34) | copy-start | bytes 1179652
  114.6 8.7 %collective-permute-start.18 = (bf16[16,6144]{1,0:T(8,128)(2,1)S(1)}, bf16[16,6144]{1,0:T(8,128)(2,1)S(1)}, u32[]{:S(2)}, u32[]{:S(2)}) collective-permute-start(bf16[16,6144]{1,0:T(8,128)(2,1)S(1)} %get-tuple-element.37), channel_id=1, source_target_pairs={{0,192},{64,0},{128,64},{192,128},{1,193},{65,1},{129,65},{193,129... | collective-permute-start | bytes 589832 | tf_op jit(solution)/shard_map/ppermute | solution.py:22
  117.9 8.8 %collective-permute-start.20 = (bf16[32,6144]{1,0:T(8,128)(2,1)S(1)}, bf16[32,6144]{1,0:T(8,128)(2,1)S(1)}, u32[]{:S(2)}, u32[]{:S(2)}) collective-permute-start(bf16[32,6144]{1,0:T(8,128)(2,1)S(1)} %get-tuple-element.38), channel_id=1, source_target_pairs={{0,2},{2,0},{1,3},{3,1},{4,6},{6,4},{5,7},{7,5},{8,10},{10,8},{9,1... | collective-permute-start | bytes 1179656 | tf_op jit(solution)/shard_map/ppermute | solution.py:22
  118.7 7.8 %collective-permute-start.22 = (bf16[16,6144]{1,0:T(8,128)(2,1)S(1)}, bf16[16,6144]{1,0:T(8,128)(2,1)S(1)}, u32[]{:S(2)}, u32[]{:S(2)}) collective-permute-start(bf16[16,6144]{1,0:T(8,128)(2,1)S(1)} %get-tuple-element.41), channel_id=1, source_target_pairs={{0,64},{64,128},{128,192},{192,0},{1,65},{65,129},{129,193},{193,1... | collective-permute-start | bytes 589832 | tf_op jit(solution)/shard_map/ppermute | solution.py:22
  123.3 11.9 %collective-permute-start.19 = (bf16[32,6144]{1,0:T(8,128)(2,1)S(1)}, bf16[32,6144]{1,0:T(8,128)(2,1)S(1)}, u32[]{:S(2)}, u32[]{:S(2)}) collective-permute-start(bf16[32,6144]{1,0:T(8,128)(2,1)S(1)} %pad_maximum_fusion.6), channel_id=1, source_target_pairs={{0,192},{64,0},{128,64},{192,128},{1,193},{65,1},{129,65},{193,129... | collective-permute-start | bytes 1179656 | tf_op jit(solution)/shard_map/ppermute | solution.py:22
  126.7 12.0 %collective-permute-start.23 = (bf16[32,6144]{1,0:T(8,128)(2,1)S(1)}, bf16[32,6144]{1,0:T(8,128)(2,1)S(1)}, u32[]{:S(2)}, u32[]{:S(2)}) collective-permute-start(bf16[32,6144]{1,0:T(8,128)(2,1)S(1)} %pad_maximum_fusion.7), channel_id=1, source_target_pairs={{0,64},{64,128},{128,192},{192,0},{1,65},{65,129},{129,193},{193,1... | collective-permute-start | bytes 1179656 | tf_op jit(solution)/shard_map/ppermute | solution.py:22
  135.4 4.9 %copy-start.10 = (s32[4,4,2]{1,2,0:T(2,128)S(1)}, s32[4,4,2]{1,2,0:T(2,128)}, u32[]{:S(2)}) copy-start(s32[4,4,2]{1,2,0:T(2,128)} %param.17) | copy-start | bytes 388
  135.4 5.1 %copy-start.8 = (bf16[32,768]{1,0:T(8,128)(2,1)S(1)}, bf16[32,768]{1,0:T(8,128)(2,1)}, u32[]{:S(2)}) copy-start(bf16[32,768]{1,0:T(8,128)(2,1)} %copy-done.7) | copy-start | bytes 147460
  135.4 11.7 %copy-start.4 = (bf16[32,6144]{1,0:T(8,128)(2,1)S(1)}, bf16[32,6144]{1,0:T(8,128)(2,1)}, u32[]{:S(2)}) copy-start(bf16[32,6144]{1,0:T(8,128)(2,1)} %copy-done.3) | copy-start | bytes 1179652
  135.4 7.9 %collective-permute-start.21 = (bf16[32,6144]{1,0:T(8,128)(2,1)S(1)}, bf16[32,6144]{1,0:T(8,128)(2,1)S(1)}, u32[]{:S(2)}, u32[]{:S(2)}) collective-permute-start(bf16[32,6144]{1,0:T(8,128)(2,1)S(1)} %add_convert_fusion.3), channel_id=1, source_target_pairs={{0,192},{64,0},{128,64},{192,128},{1,193},{65,1},{129,65},{193,129... | collective-permute-start | bytes 1179656 | tf_op jit(solution)/shard_map/ppermute | solution.py:22
  138.8 7.9 %collective-permute-start.24 = (bf16[32,6144]{1,0:T(8,128)(2,1)S(1)}, bf16[32,6144]{1,0:T(8,128)(2,1)S(1)}, u32[]{:S(2)}, u32[]{:S(2)}) collective-permute-start(bf16[32,6144]{1,0:T(8,128)(2,1)S(1)} %add_convert_fusion.2), channel_id=1, source_target_pairs={{0,64},{64,128},{128,192},{192,0},{1,65},{65,129},{129,193},{193,1... | collective-permute-start | bytes 1179656 | tf_op jit(solution)/shard_map/ppermute | solution.py:22
  139.0 8.1 %collective-permute-start.25 = (bf16[32,6144]{1,0:T(8,128)(2,1)S(1)}, bf16[32,6144]{1,0:T(8,128)(2,1)S(1)}, u32[]{:S(2)}, u32[]{:S(2)}) collective-permute-start(bf16[32,6144]{1,0:T(8,128)(2,1)S(1)} %add_convert_fusion.1), channel_id=1, source_target_pairs={{0,2},{2,0},{1,3},{3,1},{4,6},{6,4},{5,7},{7,5},{8,10},{10,8},{9,1... | collective-permute-start | bytes 1179656 | tf_op jit(solution)/shard_map/ppermute | solution.py:22
  149.1 17.5 %all-to-all-start.2 = ((bf16[16,2,7680]{2,1,0:T(2,128)(2,1)}), bf16[16,2,7680]{2,1,0:T(2,128)(2,1)S(1)}, u32[]{:S(2)}, u32[]{:S(2)}) async-start(bf16[16,2,7680]{2,1,0:T(2,128)(2,1)} %pad_maximum_fusion.2), calls=%async_computation.2 | async-start | bytes 983040 | tf_op jit(solution)/shard_map/all_to_all | solution.py:391

commit v6 on v5

--- a/solution.py
+++ b/solution.py
@@ -199,77 +199,64 @@
     return lax.dot_general(one, other, (((1,), (1,)), ((), ())), preferred_element_type=F32)
 
 
-def ffn_kernel(count, inner, *refs):
+def ffn_kernel(count, tile, *refs):
     rows, refs = refs[:count], refs[count:]
     wide, down, refs = refs[:4], refs[4:6], refs[6:]
     outs, (sums, hidden) = refs[:count], refs[count:]
-    step = pl.program_id(0)
-
-    @pl.when(step < inner)
-    def _():
-        block = jnp.concatenate([r[...] for r in rows], axis=0)
-        weights = jnp.concatenate([w[...] for w in wide], axis=0)
-        product = across_lanes(block, weights)
-
-        @pl.when(step == 0)
-        def _():
-            sums[...] = product
-
-        @pl.when(step > 0)
-        def _():
-            sums[...] += product
-
-    @pl.when(step == inner - 1)
-    def _():
-        value = sums[...]
-        width = value.shape[1] // 2
-        gated, lifted = value[:, :width], value[:, width:]
-        hidden[...] = (gated / (1.0 + jnp.exp(-gated)) * lifted).astype(BF16)
-
-    @pl.when(step >= inner)
-    def _():
-        weights = jnp.concatenate([w[...] for w in down], axis=0)
+    width, features = down[0].shape
+
+    def first(step, carry):
+        lanes = pl.ds(pl.multiple_of(step * tile, tile), tile)
+        block = jnp.concatenate([r[:, lanes] for r in rows], axis=0).T
+        for i, w in enumerate(wide):
+            here = slice(i * width, (i + 1) * width)
+            product = jnp.dot(w[:, lanes], block, preferred_element_type=F32)
+            sums[here] = jnp.where(step == 0, 0.0, sums[here]) + product
+        return carry
+
+    lax.fori_loop(0, features // tile, first, 0)
+    value = sums[...]
+    gated, lifted = value[: 2 * width], value[2 * width :]
+    hidden[...] = (gated / (1.0 + jnp.exp(-gated)) * lifted).T.astype(BF16)
+
+    def second(step, carry):
+        lanes = pl.ds(pl.multiple_of(step * tile, tile), tile)
+        weights = jnp.concatenate([w[:, lanes] for w in down], axis=0)
         total = jnp.dot(hidden[...], weights, preferred_element_type=F32).astype(BF16)
         start = 0
         for out in outs:
-            out[...] = total[start : start + out.shape[0]]
+            out[:, lanes] = total[start : start + out.shape[0]]
             start += out.shape[0]
+        return carry
+
+    lax.fori_loop(0, features // tile, second, 0)
 
 
 def expert_ffn(parts, gate, up, down):
     width, features = gate[0].shape
     total_rows = sum(p.shape[0] for p in parts)
-    tile = min(features, 3072)
-    inner = features // tile
-
-    def first(i):
-        return (0, jnp.minimum(i, inner - 1))
-
-    def second(i):
-        return (0, jnp.maximum(i - inner, 0))
-
+    tile = min(features, 2048)
+    weights = [pltpu.with_memory_space_constraint(w, pltpu.VMEM) for w in gate + up + down]
+    whole = pl.BlockSpec(memory_space=pltpu.VMEM)
     return pl.pallas_call(
-        functools.partial(ffn_kernel, len(parts), inner),
-        grid=(2 * inner,),
-        in_specs=[pl.BlockSpec((p.shape[0], tile), first) for p in parts]
-        + [pl.BlockSpec((width, tile), first)] * 4
-        + [pl.BlockSpec((width, tile), second)] * 2,
-        out_specs=[pl.BlockSpec((p.shape[0], tile), second) for p in parts],
+        functools.partial(ffn_kernel, len(parts), tile),
+        in_specs=[whole] * (len(parts) + 6),
+        out_specs=[whole] * len(parts),
         out_shape=[jax.ShapeDtypeStruct(p.shape, BF16) for p in parts],
         scratch_shapes=[
-            pltpu.VMEM((total_rows, 4 * width), F32),
+            pltpu.VMEM((4 * width, total_rows), F32),
             pltpu.VMEM((total_rows, 2 * width), BF16),
         ],
-        compiler_params=pltpu.CompilerParams(vmem_limit_bytes=40 * 1024 * 1024),
+        compiler_params=pltpu.CompilerParams(vmem_limit_bytes=16 * 1024 * 1024),
         cost_estimate=pl.CostEstimate(
             flops=12 * total_rows * features * width,
-            bytes_accessed=12 * features * width + 4 * total_rows * features,
+            bytes_accessed=4 * total_rows * features,
             transcendentals=2 * total_rows * width,
         ),
-    )(*parts, *gate, *up, *down)
-
-
-def peer_columns(columns, payload, weights):
+    )(*parts, *weights)
+
+
+def peer_columns(columns, payload):
     here, depth = columns.shape
     yl, zl, core = (lax.axis_index(axis) == 0 for axis in ("yl", "zl", "core"))
     by_zl, by_yl = shift(columns, "zl", 1), shift(columns, "yl", 1)
@@ -281,9 +268,9 @@
     low, high = ordered(zl, columns, by_zl), ordered(zl, by_yl, by_both)
     first, second = ordered(yl, low[0], high[0]), ordered(yl, low[1], high[1])
     quad = jnp.stack([first[0], second[0], first[1], second[1]])
-    quad, weights, _ = lax.optimization_barrier((quad, weights, payload))
+    quad, _ = lax.optimization_barrier((quad, payload))
     whole = jnp.stack(ordered(core, quad, shift(quad, "core", 1)), axis=1)
-    return jnp.pad(whole.reshape(8 * here, depth), ((0, 0), (0, LANES))), weights
+    return jnp.pad(whole.reshape(8 * here, depth), ((0, 0), (0, LANES)))
 
 
 def pack_kernel(code_ref, *refs):
@@ -348,15 +335,11 @@
         query_rows, key_rows, value_rows, forget, head_state, route_ids, capacity, peers
     )
     state_out = last_state(key_rows, value_rows, forget, head_state)
-    own = (gate_weight[0].T, up_weight[0].T, down_weight[0])
-    columns, own = peer_columns(out_weight.T, payload, own)
+    columns = peer_columns(out_weight.T, payload)
     width = columns.shape[0]
     piece_width = width // 2
     features = width * peers
     gathered = lax.all_to_all(payload, PEERS, split_axis=0, concat_axis=0, tiled=True)
-    other = tuple(shift(w, "core", 1) for w in own)
-    gathered, other = lax.optimization_barrier((gathered, other))
-    gate, up, down = zip(own, other)
 
     partial = lax.dot_general(
         gathered.reshape(peers * steps * rows, depth + LANES),
@@ -376,7 +359,12 @@
     codes = of_step(gathered[..., depth:], 1, size=rows).reshape(peers * rows, LANES)
 
     projected, packed = pack(codes.astype(F32), terms, experts, capacity)
+    own, packed = lax.optimization_barrier(
+        ((gate_weight[0].T, up_weight[0].T, down_weight[0]), packed)
+    )
     packed = lax.all_to_all(packed, BLOCKS, split_axis=0, concat_axis=0, tiled=True)
+    other, packed = lax.optimization_barrier((tuple(shift(w, "core", 1) for w in own), packed))
+    gate, up, down = zip(own, other)
     packed = packed.reshape(2, 2, peers // 2, 2, capacity, peers, piece_width)
     piece = jnp.transpose(packed, (1, 4, 5, 0, 3, 2, 6)).reshape(capacity * blocks, features)
 

time: 187 us -> 177 us (0.947)
  Pallas kernels: 19.4 us -> 14.1 us
  blocking collectives: 40.4 us -> 36.2 us
  other arithmetic: 6.15 us -> 3.62 us
  starting transfers between devices: 42.6 us -> 45.1 us
  waiting for transfers between devices: 68.4 us -> 70.9 us
  local copies, waits for them, and re-layouts: 6.17 us -> 4.17 us
    all_to_all x1, waiting for transfers between devices: 3.91 us -> 13.6 us  [shards(): lax.all_to_all(payload, PEERS, split_axis=0, concat_axis=0, tiled=True)]
    ppermute x25, waiting for transfers between devices: 51 us -> 43.8 us  [shift(): return lax.ppermute(array, axis, pairs)]
    pallas_call x1, Pallas kernels: 12.5 us -> 7.45 us  [expert_ffn(): pl.pallas_call(functools.partial(ffn_kernel, len(parts), tile), in_specs=...]
    ppermute x25, starting transfers between devices: 28.7 us -> 31.1 us  [shift(): return lax.ppermute(array, axis, pairs)]
    all_to_all x1, blocking collectives: 18.3 us -> 15.9 us  [spread(): return lax.all_to_all(copies, axis, split_axis=0, concat_axis=0, tiled=True)]
  transfers between devices with their start and end apart: 28 -> 28, of which waited for: 18 -> 19; matrix products, arithmetic and copies ran while one was open for 3% -> 1% of each run, Pallas kernels for 4% -> 4%
where the time goes in v6:
time: 177 us; the launch traced here: 176 us
  waiting for transfers between devices  70.9 us (40%)
  starting transfers between devices  45.1 us (25%)
  blocking collectives  36.2 us (20%)
  Pallas kernels  14.1 us (8%)
  local copies, waits for them, and re-layouts  4.17 us (2%)
  other arithmetic  3.62 us (2%)
    ppermute x25, waiting for transfers between devices, shift(): return lax.ppermute(array, axis, pairs)  43.8 us
    ppermute x25, starting transfers between devices, shift(): return lax.ppermute(array, axis, pairs)  31.1 us
    all_to_all x1, blocking collectives, shards(): lax.all_to_all(packed, BLOCKS, split_axis=0, concat_axis=0, tiled=True)  20.3 us
    all_to_all x1, blocking collectives, spread(): return lax.all_to_all(copies, axis, split_axis=0, concat_axis=0, tiled=True)  15.9 us
    all_to_all x1, waiting for transfers between devices, shards(): lax.all_to_all(payload, PEERS, split_axis=0, concat_axis=0, tiled=True)  13.6 us
    all_to_all x1, waiting for transfers between devices, shards(): lax.all_to_all(jnp.concatenate([result, mixed], axis=2), BLOCKS, split_ax...  13.5 us
    all_to_all x1, starting transfers between devices, shards(): lax.all_to_all(payload, PEERS, split_axis=0, concat_axis=0, tiled=True)  10.2 us
    pallas_call x1, Pallas kernels, expert_ffn(): pl.pallas_call(functools.partial(ffn_kernel, len(parts), tile), in_specs=...  7.45 us
  transfers between devices with their start and end apart: 28, of which 19 were waited for; matrix products, arithmetic and copies ran while one was open for 1% of the time, Pallas kernels for 4%

profile of v6, /device:TPU:2, one launch (start us, length us, event | category | flops | bytes accessed | tf_op | source)
XLA Modules:
  0.0 176.2 jit_solution(8438554066360379177)
XLA Ops:
  0.6 2.0 %collective-permute-start = (bf16[96,1024]{1,0:T(8,128)(2,1)}, bf16[96,1024]{1,0:T(8,128)(2,1)S(1)}, u32[]{:S(2)}, u32[]{:S(2)}) collective-permute-start(bf16[96,1024]{1,0:T(8,128)(2,1)} %bitcast.69), channel_id=1, source_target_pairs={{0,2},{2,0},{1,3},{3,1},{4,6},{6,4},{5,7},{7,5},{8,10},{10,8},{9,1... | collective-permute-start | bytes 589832 | tf_op jit(solution)/shard_map/ppermute | solution.py:22
  2.6 1.6 collective-permute-start.1
  4.2 1.4 copy.54.ids_ref
  5.6 4.2 %shard_map.130 = bf16[8,16,1152]{2,1,0:T(8,128)(2,1)} custom-call(f32[8]{0:T(128)} %forget_ref.3, s32[4,4,2]{2,1,0:T(4,128)} %copy.54.ids_ref, bf16[4,4,1024]{2,1,0:T(4,128)(2,1)} %refs_0_.1, bf16[4,4,1024]{2,1,0:T(4,128)(2,1)} %key_ref.1, bf16[4,4,1024]{2,1,0:T(4,128)(2,1)} %value_ref.1, bf16[4,8,128,128]{3,2,1,0:T(8,128)(2,1)} %state_ref.1), custom_call_target="tpu_custom_call" | custom-call | tf_op jit(solution)/shard_map/pallas_call | solution.py:92
  9.9 3.6 %collective-permute-done.1 = bf16[96,1024]{1,0:T(8,128)(2,1)S(1)} collective-permute-done((bf16[96,1024]{1,0:T(8,128)(2,1)}, bf16[96,1024]{1,0:T(8,128)(2,1)S(1)}, u32[]{:S(2)}, u32[]{:S(2)}) %collective-permute-start.1) | collective-permute-done | bytes 196640 | tf_op jit(solution)/shard_map/ppermute | solution.py:22
  13.4 1.0 select_bitcast_fusion.5
  14.4 0.1 pad_maximum_fusion.1
  14.7 10.2 %all-to-all-start = ((bf16[8,16,1152]{2,1,0:T(8,128)(2,1)}), bf16[8,16,1152]{2,1,0:T(8,128)(2,1)S(1)}, u32[]{:S(2)}, u32[]{:S(2)}) async-start(bf16[8,16,1152]{2,1,0:T(8,128)(2,1)} %shard_map.130), calls=%async_computation | async-start | bytes 589824 | tf_op jit(solution)/shard_map/all_to_all | solution.py:342
  24.9 13.6 %all-to-all-done = bf16[8,16,1152]{2,1,0:T(8,128)(2,1)S(1)} async-done(((bf16[8,16,1152]{2,1,0:T(8,128)(2,1)}), bf16[8,16,1152]{2,1,0:T(8,128)(2,1)S(1)}, u32[]{:S(2)}, u32[]{:S(2)}) %all-to-all-start) | async-done | bytes 294944 | tf_op jit(solution)/shard_map/all_to_all | solution.py:342
  38.5 0.1 select_bitcast_fusion.1
  38.7 0.1 pad_maximum_fusion
  38.8 0.1 copy.55
  39.0 0.7 fusion.1
  39.7 1.6 collective-permute-start.4
  41.3 1.1 collective-permute-start.5
  42.4 2.2 %collective-permute-start.6 = (f32[8,4,768]{2,1,0:T(4,128)S(1)}, f32[8,4,768]{2,1,0:T(4,128)S(1)}, u32[]{:S(2)}, u32[]{:S(2)}) collective-permute-start(f32[8,4,768]{2,1,0:T(4,128)S(1)} %get-tuple-element.67), channel_id=1, source_target_pairs={{0,192},{64,0},{128,64},{192,128},{1,193},{65,1},{129,65},{193,129... | collective-permute-start | bytes 294920 | tf_op jit(solution)/shard_map/ppermute | solution.py:22
  44.6 0.7 collective-permute-done.4.refs_1_
  45.3 2.2 %collective-permute-done.5.refs_2_ = f32[8,4,768]{2,1,0:T(4,128)S(1)} collective-permute-done((f32[8,4,768]{2,1,0:T(4,128)S(1)}, f32[8,4,768]{2,1,0:T(4,128)S(1)}, u32[]{:S(2)}, u32[]{:S(2)}) %collective-permute-start.5) | collective-permute-done | bytes 98336 | tf_op jit(solution)/shard_map/ppermute | solution.py:22
  47.5 0.6 collective-permute-done.6.refs_3_
  48.1 0.4 shard_map.131
  48.6 0.5 collective-permute-start.8
  49.1 0.1 collective-permute-start.9
  49.2 20.3 %all_to_all.20 = bf16[16,2,16,384]{3,2,1,0:T(8,128)(2,1)S(1)} all-to-all(bf16[16,2,16,384]{3,2,1,0:T(8,128)(2,1)S(1)} %get-tuple-element.30), channel_id=1, replica_groups=mesh['head'=4,'yh'=2,'yl'=2,'zp'=4,'zl'=2,'core'=2] {'yh','yl','zp'}, dimensions={0} | all-to-all | bytes 786432 | tf_op jit(solution)/shard_map/all_to_all | solution.py:365
  69.5 0.7 collective-permute-start.11
  70.2 1.6 collective-permute-start.12
  71.8 1.3 collective-permute-start.10
  73.1 5.1 %collective-permute-done.11.refs_2_ = bf16[32,6144]{1,0:T(8,128)(2,1)S(1)} collective-permute-done((bf16[32,6144]{1,0:T(8,128)(2,1)S(1)}, bf16[32,6144]{1,0:T(8,128)(2,1)S(1)}, u32[]{:S(2)}, u32[]{:S(2)}) %collective-permute-start.11) | collective-permute-done | bytes 393248 | tf_op jit(solution)/shard_map/ppermute | solution.py:22
  78.3 2.0 %collective-permute-done.12.refs_3_ = bf16[32,6144]{1,0:T(8,128)(2,1)S(1)} collective-permute-done((bf16[32,6144]{1,0:T(8,128)(2,1)S(1)}, bf16[32,6144]{1,0:T(8,128)(2,1)S(1)}, u32[]{:S(2)}, u32[]{:S(2)}) %collective-permute-start.12) | collective-permute-done | bytes 393248 | tf_op jit(solution)/shard_map/ppermute | solution.py:22
  80.4 2.5 %collective-permute-start.14 = (bf16[32,6144]{1,0:T(8,128)(2,1)S(1)}, bf16[32,6144]{1,0:T(8,128)(2,1)S(1)}, u32[]{:S(2)}, u32[]{:S(2)}) collective-permute-start(bf16[32,6144]{1,0:T(8,128)(2,1)S(1)} %pad_maximum_fusion.4), channel_id=1, source_target_pairs={{0,192},{64,0},{128,64},{192,128},{1,193},{65,1},{129,65},{193,129... | collective-permute-start | bytes 1179656 | tf_op jit(solution)/shard_map/ppermute | solution.py:22
  83.0 0.4 collective-permute-start.13
  83.4 1.7 collective-permute-start.15
  85.1 4.5 %collective-permute-done.14.refs_5_ = bf16[32,6144]{1,0:T(8,128)(2,1)S(1)} collective-permute-done((bf16[32,6144]{1,0:T(8,128)(2,1)S(1)}, bf16[32,6144]{1,0:T(8,128)(2,1)S(1)}, u32[]{:S(2)}, u32[]{:S(2)}) %collective-permute-start.14) | collective-permute-done | bytes 393248 | tf_op jit(solution)/shard_map/ppermute | solution.py:22
  89.6 2.5 %collective-permute-start.17 = (bf16[16,6144]{1,0:T(8,128)(2,1)S(1)}, bf16[16,6144]{1,0:T(8,128)(2,1)S(1)}, u32[]{:S(2)}, u32[]{:S(2)}) collective-permute-start(bf16[16,6144]{1,0:T(8,128)(2,1)S(1)} %slice.100), channel_id=1, source_target_pairs={{0,192},{64,0},{128,64},{192,128},{1,193},{65,1},{129,65},{193,129... | collective-permute-start | bytes 589832 | tf_op jit(solution)/shard_map/ppermute | solution.py:22
  92.2 0.8 collective-permute-done.13.refs_4_
  93.2 2.0 %shard_map.132 = bf16[4,8,128,128]{3,2,1,0:T(8,128)(2,1)} custom-call(f32[8]{0:T(128)S(1)} %copy-done.7, bf16[4,4,1024]{2,1,0:T(4,128)(2,1)S(1)} %copy-done.5, bf16[4,4,1024]{2,1,0:T(4,128)(2,1)S(1)} %copy-done.6, bf16[4,8,128,128]{3,2,1,0:T(8,128)(2,1)S(1)} %copy-done.1), custom_call_target="tpu_custom_call" | custom-call | flops 33554432 | bytes 2097152 | tf_op jit(solution)/shard_map/pallas_call | solution.py:133
  95.2 0.2 collective-permute-done.17.refs_8_
  95.4 4.3 %collective-permute-done.16.refs_7_ = bf16[16,6144]{1,0:T(8,128)(2,1)S(1)} collective-permute-done((bf16[16,6144]{1,0:T(8,128)(2,1)S(1)}, bf16[16,6144]{1,0:T(8,128)(2,1)S(1)}, u32[]{:S(2)}, u32[]{:S(2)}) %collective-permute-start.16) | collective-permute-done | bytes 196640 | tf_op jit(solution)/shard_map/ppermute | solution.py:22
  99.7 7.5 %shard_map.133 = (bf16[32,6144]{1,0:T(8,128)(2,1)S(1)}, bf16[32,6144]{1,0:T(8,128)(2,1)S(1)}, bf16[32,6144]{1,0:T(8,128)(2,1)S(1)}, bf16[32,6144]{1,0:T(8,128)(2...) custom-call(bf16[32,6144]{1,0:T(8,128)(2,1)S(1)} %bitcast.63, ...), custom_call_target="tpu_custom_call" | custom-call | flops 5435817984 | bytes 6291456 | tf_op jit(solution)/shard_map/pallas_call | solution.py:241
  107.2 3.3 %collective-permute-start.18 = (bf16[16,6144]{1,0:T(8,128)(2,1)S(1)}, bf16[16,6144]{1,0:T(8,128)(2,1)S(1)}, u32[]{:S(2)}, u32[]{:S(2)}) collective-permute-start(bf16[16,6144]{1,0:T(8,128)(2,1)S(1)} %get-tuple-element.39), channel_id=1, source_target_pairs={{0,192},{64,0},{128,64},{192,128},{1,193},{65,1},{129,65},{193,129... | collective-permute-start | bytes 589832 | tf_op jit(solution)/shard_map/ppermute | solution.py:22
  110.5 1.2 collective-permute-start.20
  111.7 4.0 %collective-permute-done.18 = bf16[16,6144]{1,0:T(8,128)(2,1)S(1)} collective-permute-done((bf16[16,6144]{1,0:T(8,128)(2,1)S(1)}, bf16[16,6144]{1,0:T(8,128)(2,1)S(1)}, u32[]{:S(2)}, u32[]{:S(2)}) %collective-permute-start.18) | collective-permute-done | bytes 196640 | tf_op jit(solution)/shard_map/ppermute | solution.py:22
  115.9 2.6 %collective-permute-start.19 = (bf16[32,6144]{1,0:T(8,128)(2,1)S(1)}, bf16[32,6144]{1,0:T(8,128)(2,1)S(1)}, u32[]{:S(2)}, u32[]{:S(2)}) collective-permute-start(bf16[32,6144]{1,0:T(8,128)(2,1)S(1)} %pad_maximum_fusion.6), channel_id=1, source_target_pairs={{0,192},{64,0},{128,64},{192,128},{1,193},{65,1},{129,65},{193,129... | collective-permute-start | bytes 1179656 | tf_op jit(solution)/shard_map/ppermute | solution.py:22
  118.4 1.1 collective-permute-done.22
  119.7 7.4 %collective-permute-done.19 = bf16[32,6144]{1,0:T(8,128)(2,1)S(1)} collective-permute-done((bf16[32,6144]{1,0:T(8,128)(2,1)S(1)}, bf16[32,6144]{1,0:T(8,128)(2,1)S(1)}, u32[]{:S(2)}, u32[]{:S(2)}) %collective-permute-start.19) | collective-permute-done | bytes 393248 | tf_op jit(solution)/shard_map/ppermute | solution.py:22
  127.2 0.1 add_convert_fusion.3
  127.3 2.6 %collective-permute-start.21 = (bf16[32,6144]{1,0:T(8,128)(2,1)S(1)}, bf16[32,6144]{1,0:T(8,128)(2,1)S(1)}, u32[]{:S(2)}, u32[]{:S(2)}) collective-permute-start(bf16[32,6144]{1,0:T(8,128)(2,1)S(1)} %add_convert_fusion.3), channel_id=1, source_target_pairs={{0,192},{64,0},{128,64},{192,128},{1,193},{65,1},{129,65},{193,129... | collective-permute-start | bytes 1179656 | tf_op jit(solution)/shard_map/ppermute | solution.py:22
  129.9 0.8 collective-permute-done.23
  130.7 0.1 add_convert_fusion.2
  130.9 0.1 add_convert_fusion.1
  131.0 1.2 collective-permute-start.25
  132.2 0.1 copy.59
  132.4 2.7 %collective-permute-done.21 = bf16[32,6144]{1,0:T(8,128)(2,1)S(1)} collective-permute-done((bf16[32,6144]{1,0:T(8,128)(2,1)S(1)}, bf16[32,6144]{1,0:T(8,128)(2,1)S(1)}, u32[]{:S(2)}, u32[]{:S(2)}) %collective-permute-start.21) | collective-permute-done | bytes 393248 | tf_op jit(solution)/shard_map/ppermute | solution.py:22
  135.1 3.5 %collective-permute-done.24 = bf16[32,6144]{1,0:T(8,128)(2,1)S(1)} collective-permute-done((bf16[32,6144]{1,0:T(8,128)(2,1)S(1)}, bf16[32,6144]{1,0:T(8,128)(2,1)S(1)}, u32[]{:S(2)}, u32[]{:S(2)}) %collective-permute-start.24) | collective-permute-done | bytes 393248 | tf_op jit(solution)/shard_map/ppermute | solution.py:22
  138.7 0.2 collective-permute-done.25
  138.9 0.2 add_convert_fusion
  139.1 0.1 reshape.106
  139.2 0.4 copy.57
  139.7 1.2 pad_maximum_fusion.2
  140.9 3.8 %all-to-all-start.2 = ((bf16[16,2,7680]{2,1,0:T(2,128)(2,1)}), bf16[16,2,7680]{2,1,0:T(2,128)(2,1)S(1)}, u32[]{:S(2)}, u32[]{:S(2)}) async-start(bf16[16,2,7680]{2,1,0:T(2,128)(2,1)} %pad_maximum_fusion.2), calls=%async_computation.2 | async-start | bytes 983040 | tf_op jit(solution)/shard_map/all_to_all | solution.py:379
  145.0 13.5 %all-to-all-done.2 = bf16[16,2,7680]{2,1,0:T(2,128)(2,1)S(1)} async-done(((bf16[16,2,7680]{2,1,0:T(2,128)(2,1)}), bf16[16,2,7680]{2,1,0:T(2,128)(2,1)S(1)}, u32[]{:S(2)}, u32[]{:S(2)}) %all-to-all-start.2) | async-done | bytes 491552 | tf_op jit(solution)/shard_map/all_to_all | solution.py:379
  158.7 0.3 slice.108
  159.0 0.4 fusion
  159.5 15.9 %all_to_all.21 = bf16[4,8,6144]{2,1,0:T(8,128)(2,1)S(1)} all-to-all(bf16[4,8,6144]{2,1,0:T(8,128)(2,1)S(1)} %broadcast_in_dim.8), channel_id=1, replica_groups=mesh['head'=4,'yh'=2,'yl'=2,'zp'=4,'zl'=2,'core'=2] {'head'}, dimensions={0} | all-to-all | bytes 786432 | tf_op jit(solution)/shard_map/all_to_all | solution.py:28
  175.4 0.9 fusion.9
  (75 shorter events, 1.9 us)
Async XLA Ops:
  0.6 144.2 %copy-start = (f32[4,4,2]{1,2,0:T(2,128)S(1)}, f32[4,4,2]{1,2,0:T(2,128)}, u32[]{:S(2)}) copy-start(f32[4,4,2]{1,2,0:T(2,128)} %param.18) | copy-start | bytes 388
  0.6 9.2 %collective-permute-start = (bf16[96,1024]{1,0:T(8,128)(2,1)}, bf16[96,1024]{1,0:T(8,128)(2,1)S(1)}, u32[]{:S(2)}, u32[]{:S(2)}) collective-permute-start(bf16[96,1024]{1,0:T(8,128)(2,1)} %bitcast.69), channel_id=1, source_target_pairs={{0,2},{2,0},{1,3},{3,1},{4,6},{6,4},{5,7},{7,5},{8,10},{10,8},{9,1... | collective-permute-start | bytes 589832 | tf_op jit(solution)/shard_map/ppermute | solution.py:22
  2.6 10.8 %collective-permute-start.1 = (bf16[96,1024]{1,0:T(8,128)(2,1)}, bf16[96,1024]{1,0:T(8,128)(2,1)S(1)}, u32[]{:S(2)}, u32[]{:S(2)}) collective-permute-start(bf16[96,1024]{1,0:T(8,128)(2,1)} %bitcast.70), channel_id=1, source_target_pairs={{0,16},{16,0},{1,17},{17,1},{2,18},{18,2},{3,19},{19,3},{4,20},{20... | collective-permute-start | bytes 589832 | tf_op jit(solution)/shard_map/ppermute | solution.py:22
  4.2 9.2 %collective-permute-start.2 = (bf16[96,1024]{1,0:T(8,128)(2,1)}, bf16[96,1024]{1,0:T(8,128)(2,1)S(1)}, u32[]{:S(2)}, u32[]{:S(2)}) collective-permute-start(bf16[96,1024]{1,0:T(8,128)(2,1)} %bitcast.71), channel_id=1, source_target_pairs={{0,18},{2,16},{16,2},{18,0},{1,19},{3,17},{17,3},{19,1},{4,22},{6,... | collective-permute-start | bytes 589832 | tf_op jit(solution)/shard_map/ppermute | solution.py:263
  14.6 23.9 %collective-permute-start.3 = (bf16[4,96,1024]{2,1,0:T(8,128)(2,1)S(1)}, bf16[4,96,1024]{2,1,0:T(8,128)(2,1)S(1)}, u32[]{:S(2)}, u32[]{:S(2)}) collective-permute-start(bf16[4,96,1024]{2,1,0:T(8,128)(2,1)S(1)} %pad_maximum_fusion.1), channel_id=1, source_target_pairs={{0,1},{1,0},{2,3},{3,2},{4,5},{5,4},{6,7},{7,6},{8,9},{9,8},{10,11... | collective-permute-start | bytes 2359304 | tf_op jit(solution)/shard_map/ppermute | solution.py:22
  14.7 23.8 %all-to-all-start = ((bf16[8,16,1152]{2,1,0:T(8,128)(2,1)}), bf16[8,16,1152]{2,1,0:T(8,128)(2,1)S(1)}, u32[]{:S(2)}, u32[]{:S(2)}) async-start(bf16[8,16,1152]{2,1,0:T(8,128)(2,1)} %shard_map.130), calls=%async_computation | async-start | bytes 589824 | tf_op jit(solution)/shard_map/all_to_all | solution.py:342
  38.5 10.6 %copy-start.4 = (bf16[1,288,6144]{2,1,0:T(8,128)(2,1)S(1)}, bf16[1,288,6144]{2,1,0:T(8,128)(2,1)}, u32[]{:S(2)}) copy-start(bf16[1,288,6144]{2,1,0:T(8,128)(2,1)} %param.21) | copy-start | bytes 10616836
  38.6 9.9 %copy-start.3 = (bf16[1,6144,288]{1,2,0:T(8,128)(2,1)S(1)}, bf16[1,6144,288]{1,2,0:T(8,128)(2,1)}, u32[]{:S(2)}) copy-start(bf16[1,6144,288]{1,2,0:T(8,128)(2,1)} %param.20) | copy-start | bytes 10616836
  38.8 9.7 %copy-start.2 = (bf16[1,6144,288]{1,2,0:T(8,128)(2,1)S(1)}, bf16[1,6144,288]{1,2,0:T(8,128)(2,1)}, u32[]{:S(2)}) copy-start(bf16[1,6144,288]{1,2,0:T(8,128)(2,1)} %param.19) | copy-start | bytes 10616836
  39.7 5.6 %collective-permute-start.4 = (f32[8,4,768]{2,1,0:T(4,128)S(1)}, f32[8,4,768]{2,1,0:T(4,128)S(1)}, u32[]{:S(2)}, u32[]{:S(2)}) collective-permute-start(f32[8,4,768]{2,1,0:T(4,128)S(1)} %get-tuple-element.69), channel_id=1, source_target_pairs={{0,64},{64,128},{128,192},{192,0},{1,65},{65,129},{129,193},{193,1... | collective-permute-start | bytes 294920 | tf_op jit(solution)/shard_map/ppermute | solution.py:22
  41.3 6.2 %collective-permute-start.5 = (f32[8,4,768]{2,1,0:T(4,128)S(1)}, f32[8,4,768]{2,1,0:T(4,128)S(1)}, u32[]{:S(2)}, u32[]{:S(2)}) collective-permute-start(f32[8,4,768]{2,1,0:T(4,128)S(1)} %get-tuple-element.68), channel_id=1, source_target_pairs={{0,128},{64,192},{128,0},{192,64},{1,129},{65,193},{129,1},{193,65... | collective-permute-start | bytes 294920 | tf_op jit(solution)/shard_map/ppermute | solution.py:22
  42.4 5.7 %collective-permute-start.6 = (f32[8,4,768]{2,1,0:T(4,128)S(1)}, f32[8,4,768]{2,1,0:T(4,128)S(1)}, u32[]{:S(2)}, u32[]{:S(2)}) collective-permute-start(f32[8,4,768]{2,1,0:T(4,128)S(1)} %get-tuple-element.67), channel_id=1, source_target_pairs={{0,192},{64,0},{128,64},{192,128},{1,193},{65,1},{129,65},{193,129... | collective-permute-start | bytes 294920 | tf_op jit(solution)/shard_map/ppermute | solution.py:22
  48.5 21.0 %collective-permute-start.7 = (bf16[288,6144]{1,0:T(8,128)(2,1)S(1)}, bf16[288,6144]{1,0:T(8,128)(2,1)S(1)}, u32[]{:S(2)}, u32[]{:S(2)}) collective-permute-start(bf16[288,6144]{1,0:T(8,128)(2,1)S(1)} %bitcast.54), channel_id=1, source_target_pairs={{0,1},{1,0},{2,3},{3,2},{4,5},{5,4},{6,7},{7,6},{8,9},{9,8},{10,11... | collective-permute-start | bytes 10616840 | tf_op jit(solution)/shard_map/ppermute | solution.py:22
  48.6 20.9 %collective-permute-start.8 = (bf16[288,6144]{1,0:T(8,128)(2,1)S(1)}, bf16[288,6144]{1,0:T(8,128)(2,1)S(1)}, u32[]{:S(2)}, u32[]{:S(2)}) collective-permute-start(bf16[288,6144]{1,0:T(8,128)(2,1)S(1)} %bitcast.56), channel_id=1, source_target_pairs={{0,1},{1,0},{2,3},{3,2},{4,5},{5,4},{6,7},{7,6},{8,9},{9,8},{10,11... | collective-permute-start | bytes 10616840 | tf_op jit(solution)/shard_map/ppermute | solution.py:22
  49.1 20.4 %collective-permute-start.9 = (bf16[288,6144]{1,0:T(8,128)(2,1)S(1)}, bf16[288,6144]{1,0:T(8,128)(2,1)S(1)}, u32[]{:S(2)}, u32[]{:S(2)}) collective-permute-start(bf16[288,6144]{1,0:T(8,128)(2,1)S(1)} %bitcast.58), channel_id=1, source_target_pairs={{0,1},{1,0},{2,3},{3,2},{4,5},{5,4},{6,7},{7,6},{8,9},{9,8},{10,11... | collective-permute-start | bytes 10616840 | tf_op jit(solution)/shard_map/ppermute | solution.py:22
  69.5 8.7 %collective-permute-start.11 = (bf16[32,6144]{1,0:T(8,128)(2,1)S(1)}, bf16[32,6144]{1,0:T(8,128)(2,1)S(1)}, u32[]{:S(2)}, u32[]{:S(2)}) collective-permute-start(bf16[32,6144]{1,0:T(8,128)(2,1)S(1)} %bitcast.60), channel_id=1, source_target_pairs={{0,192},{64,0},{128,64},{192,128},{1,193},{65,1},{129,65},{193,129... | collective-permute-start | bytes 1179656 | tf_op jit(solution)/shard_map/ppermute | solution.py:22
  70.2 10.1 %collective-permute-start.12 = (bf16[32,6144]{1,0:T(8,128)(2,1)S(1)}, bf16[32,6144]{1,0:T(8,128)(2,1)S(1)}, u32[]{:S(2)}, u32[]{:S(2)}) collective-permute-start(bf16[32,6144]{1,0:T(8,128)(2,1)S(1)} %bitcast.61), channel_id=1, source_target_pairs={{0,2},{2,0},{1,3},{3,1},{4,6},{6,4},{5,7},{7,5},{8,10},{10,8},{9,1... | collective-permute-start | bytes 1179656 | tf_op jit(solution)/shard_map/ppermute | solution.py:22
  71.8 11.1 %collective-permute-start.10 = (bf16[32,6144]{1,0:T(8,128)(2,1)S(1)}, bf16[32,6144]{1,0:T(8,128)(2,1)S(1)}, u32[]{:S(2)}, u32[]{:S(2)}) collective-permute-start(bf16[32,6144]{1,0:T(8,128)(2,1)S(1)} %bitcast.62), channel_id=1, source_target_pairs={{0,64},{64,128},{128,192},{192,0},{1,65},{65,129},{129,193},{193,1... | collective-permute-start | bytes 1179656 | tf_op jit(solution)/shard_map/ppermute | solution.py:22
  80.3 12.8 %copy-start.1 = (bf16[4,8,128,128]{3,2,1,0:T(8,128)(2,1)S(1)}, bf16[4,8,128,128]{3,2,1,0:T(8,128)(2,1)}, u32[]{:S(2)}) copy-start(bf16[4,8,128,128]{3,2,1,0:T(8,128)(2,1)} %state_ref.1) | copy-start | bytes 3145732
  80.4 12.8 %copy-start.5 = (bf16[4,4,1024]{2,1,0:T(4,128)(2,1)S(1)}, bf16[4,4,1024]{2,1,0:T(4,128)(2,1)}, u32[]{:S(2)}) copy-start(bf16[4,4,1024]{2,1,0:T(4,128)(2,1)} %key_ref.1) | copy-start | bytes 98308
  80.4 12.8 %copy-start.6 = (bf16[4,4,1024]{2,1,0:T(4,128)(2,1)S(1)}, bf16[4,4,1024]{2,1,0:T(4,128)(2,1)}, u32[]{:S(2)}) copy-start(bf16[4,4,1024]{2,1,0:T(4,128)(2,1)} %value_ref.1) | copy-start | bytes 98308
  80.4 12.8 %copy-start.7 = (f32[8]{0:T(128)S(1)}, f32[8]{0:T(128)}, u32[]{:S(2)}) copy-start(f32[8]{0:T(128)} %forget_ref.3) | copy-start | bytes 100
  80.4 9.2 %collective-permute-start.14 = (bf16[32,6144]{1,0:T(8,128)(2,1)S(1)}, bf16[32,6144]{1,0:T(8,128)(2,1)S(1)}, u32[]{:S(2)}, u32[]{:S(2)}) collective-permute-start(bf16[32,6144]{1,0:T(8,128)(2,1)S(1)} %pad_maximum_fusion.4), channel_id=1, source_target_pairs={{0,192},{64,0},{128,64},{192,128},{1,193},{65,1},{129,65},{193,129... | collective-permute-start | bytes 1179656 | tf_op jit(solution)/shard_map/ppermute | solution.py:22
  83.0 10.0 %collective-permute-start.13 = (bf16[32,6144]{1,0:T(8,128)(2,1)S(1)}, bf16[32,6144]{1,0:T(8,128)(2,1)S(1)}, u32[]{:S(2)}, u32[]{:S(2)}) collective-permute-start(bf16[32,6144]{1,0:T(8,128)(2,1)S(1)} %pad_maximum_fusion.3), channel_id=1, source_target_pairs={{0,64},{64,128},{128,192},{192,0},{1,65},{65,129},{129,193},{193,1... | collective-permute-start | bytes 1179656 | tf_op jit(solution)/shard_map/ppermute | solution.py:22
  83.4 12.0 %collective-permute-start.15 = (bf16[32,6144]{1,0:T(8,128)(2,1)S(1)}, bf16[32,6144]{1,0:T(8,128)(2,1)S(1)}, u32[]{:S(2)}, u32[]{:S(2)}) collective-permute-start(bf16[32,6144]{1,0:T(8,128)(2,1)S(1)} %pad_maximum_fusion.5), channel_id=1, source_target_pairs={{0,2},{2,0},{1,3},{3,1},{4,6},{6,4},{5,7},{7,5},{8,10},{10,8},{9,1... | collective-permute-start | bytes 1179656 | tf_op jit(solution)/shard_map/ppermute | solution.py:22
  89.6 5.7 %collective-permute-start.17 = (bf16[16,6144]{1,0:T(8,128)(2,1)S(1)}, bf16[16,6144]{1,0:T(8,128)(2,1)S(1)}, u32[]{:S(2)}, u32[]{:S(2)}) collective-permute-start(bf16[16,6144]{1,0:T(8,128)(2,1)S(1)} %slice.100), channel_id=1, source_target_pairs={{0,192},{64,0},{128,64},{192,128},{1,193},{65,1},{129,65},{193,129... | collective-permute-start | bytes 589832 | tf_op jit(solution)/shard_map/ppermute | solution.py:22
  93.0 6.7 %collective-permute-start.16 = (bf16[16,6144]{1,0:T(8,128)(2,1)S(1)}, bf16[16,6144]{1,0:T(8,128)(2,1)S(1)}, u32[]{:S(2)}, u32[]{:S(2)}) collective-permute-start(bf16[16,6144]{1,0:T(8,128)(2,1)S(1)} %slice.99), channel_id=1, source_target_pairs={{0,64},{64,128},{128,192},{192,0},{1,65},{65,129},{129,193},{193,1... | collective-permute-start | bytes 589832 | tf_op jit(solution)/shard_map/ppermute | solution.py:22
  107.2 8.6 %collective-permute-start.18 = (bf16[16,6144]{1,0:T(8,128)(2,1)S(1)}, bf16[16,6144]{1,0:T(8,128)(2,1)S(1)}, u32[]{:S(2)}, u32[]{:S(2)}) collective-permute-start(bf16[16,6144]{1,0:T(8,128)(2,1)S(1)} %get-tuple-element.39), channel_id=1, source_target_pairs={{0,192},{64,0},{128,64},{192,128},{1,193},{65,1},{129,65},{193,129... | collective-permute-start | bytes 589832 | tf_op jit(solution)/shard_map/ppermute | solution.py:22
  110.5 9.2 %collective-permute-start.20 = (bf16[32,6144]{1,0:T(8,128)(2,1)S(1)}, bf16[32,6144]{1,0:T(8,128)(2,1)S(1)}, u32[]{:S(2)}, u32[]{:S(2)}) collective-permute-start(bf16[32,6144]{1,0:T(8,128)(2,1)S(1)} %get-tuple-element.40), channel_id=1, source_target_pairs={{0,2},{2,0},{1,3},{3,1},{4,6},{6,4},{5,7},{7,5},{8,10},{10,8},{9,1... | collective-permute-start | bytes 1179656 | tf_op jit(solution)/shard_map/ppermute | solution.py:22
  111.7 7.8 %collective-permute-start.22 = (bf16[16,6144]{1,0:T(8,128)(2,1)S(1)}, bf16[16,6144]{1,0:T(8,128)(2,1)S(1)}, u32[]{:S(2)}, u32[]{:S(2)}) collective-permute-start(bf16[16,6144]{1,0:T(8,128)(2,1)S(1)} %get-tuple-element.43), channel_id=1, source_target_pairs={{0,64},{64,128},{128,192},{192,0},{1,65},{65,129},{129,193},{193,1... | collective-permute-start | bytes 589832 | tf_op jit(solution)/shard_map/ppermute | solution.py:22
  115.9 11.3 %collective-permute-start.19 = (bf16[32,6144]{1,0:T(8,128)(2,1)S(1)}, bf16[32,6144]{1,0:T(8,128)(2,1)S(1)}, u32[]{:S(2)}, u32[]{:S(2)}) collective-permute-start(bf16[32,6144]{1,0:T(8,128)(2,1)S(1)} %pad_maximum_fusion.6), channel_id=1, source_target_pairs={{0,192},{64,0},{128,64},{192,128},{1,193},{65,1},{129,65},{193,129... | collective-permute-start | bytes 1179656 | tf_op jit(solution)/shard_map/ppermute | solution.py:22
  119.6 11.1 %collective-permute-start.23 = (bf16[32,6144]{1,0:T(8,128)(2,1)S(1)}, bf16[32,6144]{1,0:T(8,128)(2,1)S(1)}, u32[]{:S(2)}, u32[]{:S(2)}) collective-permute-start(bf16[32,6144]{1,0:T(8,128)(2,1)S(1)} %pad_maximum_fusion.7), channel_id=1, source_target_pairs={{0,64},{64,128},{128,192},{192,0},{1,65},{65,129},{129,193},{193,1... | collective-permute-start | bytes 1179656 | tf_op jit(solution)/shard_map/ppermute | solution.py:22
  127.3 4.9 %copy-start.8 = (s32[4,4,2]{1,2,0:T(2,128)S(1)}, s32[4,4,2]{1,2,0:T(2,128)}, u32[]{:S(2)}) copy-start(s32[4,4,2]{1,2,0:T(2,128)} %param.17) | copy-start | bytes 388
  127.3 7.9 %collective-permute-start.21 = (bf16[32,6144]{1,0:T(8,128)(2,1)S(1)}, bf16[32,6144]{1,0:T(8,128)(2,1)S(1)}, u32[]{:S(2)}, u32[]{:S(2)}) collective-permute-start(bf16[32,6144]{1,0:T(8,128)(2,1)S(1)} %add_convert_fusion.3), channel_id=1, source_target_pairs={{0,192},{64,0},{128,64},{192,128},{1,193},{65,1},{129,65},{193,129... | collective-permute-start | bytes 1179656 | tf_op jit(solution)/shard_map/ppermute | solution.py:22
  130.8 7.9 %collective-permute-start.24 = (bf16[32,6144]{1,0:T(8,128)(2,1)S(1)}, bf16[32,6144]{1,0:T(8,128)(2,1)S(1)}, u32[]{:S(2)}, u32[]{:S(2)}) collective-permute-start(bf16[32,6144]{1,0:T(8,128)(2,1)S(1)} %add_convert_fusion.2), channel_id=1, source_target_pairs={{0,64},{64,128},{128,192},{192,0},{1,65},{65,129},{129,193},{193,1... | collective-permute-start | bytes 1179656 | tf_op jit(solution)/shard_map/ppermute | solution.py:22
  131.0 7.9 %collective-permute-start.25 = (bf16[32,6144]{1,0:T(8,128)(2,1)S(1)}, bf16[32,6144]{1,0:T(8,128)(2,1)S(1)}, u32[]{:S(2)}, u32[]{:S(2)}) collective-permute-start(bf16[32,6144]{1,0:T(8,128)(2,1)S(1)} %add_convert_fusion.1), channel_id=1, source_target_pairs={{0,2},{2,0},{1,3},{3,1},{4,6},{6,4},{5,7},{7,5},{8,10},{10,8},{9,1... | collective-permute-start | bytes 1179656 | tf_op jit(solution)/shard_map/ppermute | solution.py:22
  140.9 17.5 %all-to-all-start.2 = ((bf16[16,2,7680]{2,1,0:T(2,128)(2,1)}), bf16[16,2,7680]{2,1,0:T(2,128)(2,1)S(1)}, u32[]{:S(2)}, u32[]{:S(2)}) async-start(bf16[16,2,7680]{2,1,0:T(2,128)(2,1)} %pad_maximum_fusion.2), calls=%async_computation.2 | async-start | bytes 983040 | tf_op jit(solution)/shard_map/all_to_all | solution.py:379

commit v7 on v6

--- a/solution.py
+++ b/solution.py
@@ -49,7 +49,7 @@
     row, lane = (lax.broadcasted_iota(jnp.int32, shape, i) for i in range(2))
     tail = jnp.zeros(shape, jnp.int32)
     for t in range(steps):
-        ids = [ids_ref[t, i // 2, i % 2] for i in range(2 * rows)]
+        ids = [ids_ref[t, i % 2, i // 2] for i in range(2 * rows)]
         for i in range(2 * rows):
             slot = sum((jnp.where(ids[j] == ids[i], 1, 0) for j in range(i)), jnp.int32(0))
             here = (row == t * rows + i // 2) & (lane == i % 2)
@@ -99,7 +99,7 @@
         + [pltpu.VMEM(query_rows.shape, BF16)] * 3
         + [pltpu.VMEM(head_state.shape, BF16), pltpu.SemaphoreType.DMA((4,))],
         compiler_params=pltpu.CompilerParams(vmem_limit_bytes=54 * 1024 * 1024),
-    )(forget, route_ids, query_rows, key_rows, value_rows, head_state)
+    )(forget, jnp.swapaxes(route_ids, 1, 2), query_rows, key_rows, value_rows, head_state)
 
 
 def state_kernel(forget_ref, key_ref, value_ref, state_ref, out_ref, flat):
@@ -159,7 +159,7 @@
 
 def gather_block(own):
     half = own.shape[0] // 2
-    left, right, across = shift(own, "head", 1), shift(own, "head", -1), shift(own, "zl", 1)
+    across, left, right = shift(own, "zl", 1), shift(own, "head", 1), shift(own, "head", -1)
 
     def halves(one, other):
         return jnp.concatenate([one, other], axis=0)
@@ -186,13 +186,14 @@
     from_left = shift(last_right, "head", 1)
     by_left = halves(by_left[:half], add(by_left[half:], from_right))
     by_right = halves(by_right[:half], add(by_right[half:], from_left))
+    from_across = shift(by_across, "zl", 1)
     from_right = shift(by_left, "head", -1)
     from_left = shift(by_right, "head", 1)
-    from_across = shift(by_across, "zl", 1)
     left = add(left, halves(from_right[:half], from_across[:half]))
     right = add(right, halves(from_across[half:], from_left[:half]))
     across = add(across, halves(from_right[half:], from_left[half:]))
-    return add(own, shift(left, "head", -1), shift(right, "head", 1), shift(across, "zl", 1))
+    terms = shift(across, "zl", 1), shift(left, "head", -1), shift(right, "head", 1)
+    return add(own, *terms)
 
 
 def across_lanes(one, other):

time: 177 us -> 171 us (0.966)
  blocking collectives: 36.2 us -> 30.5 us
    all_to_all x1, blocking collectives: 15.9 us -> 10.3 us  [spread(): return lax.all_to_all(copies, axis, split_axis=0, concat_axis=0, tiled=True)]
where the time goes in v7:
time: 171 us; the launch traced here: 170 us
  waiting for transfers between devices  72.1 us (42%)
  starting transfers between devices  45.2 us (26%)
  blocking collectives  30.5 us (18%)
  Pallas kernels  14 us (8%)
  other arithmetic  3.62 us (2%)
  local copies, waits for them, and re-layouts  2.79 us (2%)
    ppermute x25, waiting for transfers between devices, shift(): return lax.ppermute(array, axis, pairs)  44.6 us
    ppermute x25, starting transfers between devices, shift(): return lax.ppermute(array, axis, pairs)  31 us
    all_to_all x1, blocking collectives, shards(): lax.all_to_all(packed, BLOCKS, split_axis=0, concat_axis=0, tiled=True)  20.2 us
    all_to_all x1, waiting for transfers between devices, shards(): lax.all_to_all(jnp.concatenate([result, mixed], axis=2), BLOCKS, split_ax...  13.9 us
    all_to_all x1, waiting for transfers between devices, shards(): lax.all_to_all(payload, PEERS, split_axis=0, concat_axis=0, tiled=True)  13.6 us
    all_to_all x1, blocking collectives, spread(): return lax.all_to_all(copies, axis, split_axis=0, concat_axis=0, tiled=True)  10.3 us
    all_to_all x1, starting transfers between devices, shards(): lax.all_to_all(payload, PEERS, split_axis=0, concat_axis=0, tiled=True)  10.2 us
    pallas_call x1, Pallas kernels, expert_ffn(): pl.pallas_call(functools.partial(ffn_kernel, len(parts), tile), in_specs=...  7.46 us
  transfers between devices with their start and end apart: 28, of which 19 were waited for; matrix products, arithmetic and copies ran while one was open for 1% of the time, Pallas kernels for 4%

profile of v7, /device:TPU:2, one launch (start us, length us, event | category | flops | bytes accessed | tf_op | source)
XLA Modules:
  0.0 170.4 jit_solution(9944993886132679845)
XLA Ops:
  0.6 2.0 %collective-permute-start = (bf16[96,1024]{1,0:T(8,128)(2,1)}, bf16[96,1024]{1,0:T(8,128)(2,1)S(1)}, u32[]{:S(2)}, u32[]{:S(2)}) collective-permute-start(bf16[96,1024]{1,0:T(8,128)(2,1)} %bitcast.70), channel_id=1, source_target_pairs={{0,2},{2,0},{1,3},{3,1},{4,6},{6,4},{5,7},{7,5},{8,10},{10,8},{9,1... | collective-permute-start | bytes 589832 | tf_op jit(solution)/shard_map/ppermute | solution.py:22
  2.6 1.6 collective-permute-start.1
  4.2 4.2 %shard_map.130 = bf16[8,16,1152]{2,1,0:T(8,128)(2,1)} custom-call(f32[8]{0:T(128)} %forget_ref.3, s32[4,2,4]{2,1,0:T(2,128)} %bitcast.75, bf16[4,4,1024]{2,1,0:T(4,128)(2,1)} %refs_0_.1, bf16[4,4,1024]{2,1,0:T(4,128)(2,1)} %key_ref.1, bf16[4,4,1024]{2,1,0:T(4,128)(2,1)} %value_ref.1, bf16[4,8,128,128]{3,2,1,0:T(8,128)(2,1)} %state_ref.1), custom_call_target="tpu_custom_call" | custom-call | tf_op jit(solution)/shard_map/pallas_call | solution.py:92
  8.4 0.3 collective-permute-done
  8.7 4.7 %collective-permute-done.1 = bf16[96,1024]{1,0:T(8,128)(2,1)S(1)} collective-permute-done((bf16[96,1024]{1,0:T(8,128)(2,1)}, bf16[96,1024]{1,0:T(8,128)(2,1)S(1)}, u32[]{:S(2)}, u32[]{:S(2)}) %collective-permute-start.1) | collective-permute-done | bytes 196640 | tf_op jit(solution)/shard_map/ppermute | solution.py:22
  13.4 1.0 select_bitcast_fusion.5
  14.5 0.1 pad_maximum_fusion.1
  14.6 0.1 collective-permute-start.3
  14.7 10.2 %all-to-all-start = ((bf16[8,16,1152]{2,1,0:T(8,128)(2,1)}), bf16[8,16,1152]{2,1,0:T(8,128)(2,1)S(1)}, u32[]{:S(2)}, u32[]{:S(2)}) async-start(bf16[8,16,1152]{2,1,0:T(8,128)(2,1)} %shard_map.130), calls=%async_computation | async-start | bytes 589824 | tf_op jit(solution)/shard_map/all_to_all | solution.py:343
  24.9 13.6 %all-to-all-done = bf16[8,16,1152]{2,1,0:T(8,128)(2,1)S(1)} async-done(((bf16[8,16,1152]{2,1,0:T(8,128)(2,1)}), bf16[8,16,1152]{2,1,0:T(8,128)(2,1)S(1)}, u32[]{:S(2)}, u32[]{:S(2)}) %all-to-all-start) | async-done | bytes 294944 | tf_op jit(solution)/shard_map/all_to_all | solution.py:343
  38.5 0.1 select_bitcast_fusion.1
  38.7 0.1 pad_maximum_fusion
  38.8 0.1 copy.50
  39.0 0.7 fusion.1
  39.7 1.6 collective-permute-start.4
  41.3 1.1 collective-permute-start.5
  42.4 2.2 %collective-permute-start.6 = (f32[8,4,768]{2,1,0:T(4,128)S(1)}, f32[8,4,768]{2,1,0:T(4,128)S(1)}, u32[]{:S(2)}, u32[]{:S(2)}) collective-permute-start(f32[8,4,768]{2,1,0:T(4,128)S(1)} %get-tuple-element.67), channel_id=1, source_target_pairs={{0,192},{64,0},{128,64},{192,128},{1,193},{65,1},{129,65},{193,129... | collective-permute-start | bytes 294920 | tf_op jit(solution)/shard_map/ppermute | solution.py:22
  44.6 0.7 collective-permute-done.4.refs_1_
  45.3 2.2 %collective-permute-done.5.refs_2_ = f32[8,4,768]{2,1,0:T(4,128)S(1)} collective-permute-done((f32[8,4,768]{2,1,0:T(4,128)S(1)}, f32[8,4,768]{2,1,0:T(4,128)S(1)}, u32[]{:S(2)}, u32[]{:S(2)}) %collective-permute-start.5) | collective-permute-done | bytes 98336 | tf_op jit(solution)/shard_map/ppermute | solution.py:22
  47.5 0.6 collective-permute-done.6.refs_3_
  48.1 0.4 shard_map.131
  48.6 0.5 collective-permute-start.8
  49.1 0.1 collective-permute-start.9
  49.2 20.2 %all_to_all.20 = bf16[16,2,16,384]{3,2,1,0:T(8,128)(2,1)S(1)} all-to-all(bf16[16,2,16,384]{3,2,1,0:T(8,128)(2,1)S(1)} %get-tuple-element.30), channel_id=1, replica_groups=mesh['head'=4,'yh'=2,'yl'=2,'zp'=4,'zl'=2,'core'=2] {'yh','yl','zp'}, dimensions={0} | all-to-all | bytes 786432 | tf_op jit(solution)/shard_map/all_to_all | solution.py:366
  69.5 0.7 collective-permute-start.11
  70.2 1.6 collective-permute-start.12
  71.8 1.3 collective-permute-start.10
  73.1 5.1 %collective-permute-done.11.refs_2_ = bf16[32,6144]{1,0:T(8,128)(2,1)S(1)} collective-permute-done((bf16[32,6144]{1,0:T(8,128)(2,1)S(1)}, bf16[32,6144]{1,0:T(8,128)(2,1)S(1)}, u32[]{:S(2)}, u32[]{:S(2)}) %collective-permute-start.11) | collective-permute-done | bytes 393248 | tf_op jit(solution)/shard_map/ppermute | solution.py:22
  78.3 2.0 %collective-permute-done.12.refs_3_ = bf16[32,6144]{1,0:T(8,128)(2,1)S(1)} collective-permute-done((bf16[32,6144]{1,0:T(8,128)(2,1)S(1)}, bf16[32,6144]{1,0:T(8,128)(2,1)S(1)}, u32[]{:S(2)}, u32[]{:S(2)}) %collective-permute-start.12) | collective-permute-done | bytes 393248 | tf_op jit(solution)/shard_map/ppermute | solution.py:22
  80.4 2.5 %collective-permute-start.14 = (bf16[32,6144]{1,0:T(8,128)(2,1)S(1)}, bf16[32,6144]{1,0:T(8,128)(2,1)S(1)}, u32[]{:S(2)}, u32[]{:S(2)}) collective-permute-start(bf16[32,6144]{1,0:T(8,128)(2,1)S(1)} %pad_maximum_fusion.4), channel_id=1, source_target_pairs={{0,192},{64,0},{128,64},{192,128},{1,193},{65,1},{129,65},{193,129... | collective-permute-start | bytes 1179656 | tf_op jit(solution)/shard_map/ppermute | solution.py:22
  83.0 0.4 collective-permute-start.13
  83.4 1.7 collective-permute-start.15
  85.1 4.5 %collective-permute-done.14.refs_5_ = bf16[32,6144]{1,0:T(8,128)(2,1)S(1)} collective-permute-done((bf16[32,6144]{1,0:T(8,128)(2,1)S(1)}, bf16[32,6144]{1,0:T(8,128)(2,1)S(1)}, u32[]{:S(2)}, u32[]{:S(2)}) %collective-permute-start.14) | collective-permute-done | bytes 393248 | tf_op jit(solution)/shard_map/ppermute | solution.py:22
  89.7 2.5 %collective-permute-start.17 = (bf16[16,6144]{1,0:T(8,128)(2,1)S(1)}, bf16[16,6144]{1,0:T(8,128)(2,1)S(1)}, u32[]{:S(2)}, u32[]{:S(2)}) collective-permute-start(bf16[16,6144]{1,0:T(8,128)(2,1)S(1)} %slice.100), channel_id=1, source_target_pairs={{0,192},{64,0},{128,64},{192,128},{1,193},{65,1},{129,65},{193,129... | collective-permute-start | bytes 589832 | tf_op jit(solution)/shard_map/ppermute | solution.py:22
  92.2 0.8 collective-permute-done.13.refs_4_
  93.2 2.0 %shard_map.132 = bf16[4,8,128,128]{3,2,1,0:T(8,128)(2,1)} custom-call(f32[8]{0:T(128)S(1)} %copy-done.7, bf16[4,4,1024]{2,1,0:T(4,128)(2,1)S(1)} %copy-done.5, bf16[4,4,1024]{2,1,0:T(4,128)(2,1)S(1)} %copy-done.6, bf16[4,8,128,128]{3,2,1,0:T(8,128)(2,1)S(1)} %copy-done.1), custom_call_target="tpu_custom_call" | custom-call | flops 33554432 | bytes 2097152 | tf_op jit(solution)/shard_map/pallas_call | solution.py:133
  95.2 0.2 collective-permute-done.17.refs_8_
  95.4 4.3 %collective-permute-done.16.refs_7_ = bf16[16,6144]{1,0:T(8,128)(2,1)S(1)} collective-permute-done((bf16[16,6144]{1,0:T(8,128)(2,1)S(1)}, bf16[16,6144]{1,0:T(8,128)(2,1)S(1)}, u32[]{:S(2)}, u32[]{:S(2)}) %collective-permute-start.16) | collective-permute-done | bytes 196640 | tf_op jit(solution)/shard_map/ppermute | solution.py:22
  99.7 7.5 %shard_map.133 = (bf16[32,6144]{1,0:T(8,128)(2,1)S(1)}, bf16[32,6144]{1,0:T(8,128)(2,1)S(1)}, bf16[32,6144]{1,0:T(8,128)(2,1)S(1)}, bf16[32,6144]{1,0:T(8,128)(2...) custom-call(bf16[32,6144]{1,0:T(8,128)(2,1)S(1)} %bitcast.64, ...), custom_call_target="tpu_custom_call" | custom-call | flops 5435817984 | bytes 6291456 | tf_op jit(solution)/shard_map/pallas_call | solution.py:242
  107.2 3.3 %collective-permute-start.18 = (bf16[16,6144]{1,0:T(8,128)(2,1)S(1)}, bf16[16,6144]{1,0:T(8,128)(2,1)S(1)}, u32[]{:S(2)}, u32[]{:S(2)}) collective-permute-start(bf16[16,6144]{1,0:T(8,128)(2,1)S(1)} %get-tuple-element.39), channel_id=1, source_target_pairs={{0,192},{64,0},{128,64},{192,128},{1,193},{65,1},{129,65},{193,129... | collective-permute-start | bytes 589832 | tf_op jit(solution)/shard_map/ppermute | solution.py:22
  110.7 1.2 collective-permute-start.23
  111.8 3.9 %collective-permute-done.18 = bf16[16,6144]{1,0:T(8,128)(2,1)S(1)} collective-permute-done((bf16[16,6144]{1,0:T(8,128)(2,1)S(1)}, bf16[16,6144]{1,0:T(8,128)(2,1)S(1)}, u32[]{:S(2)}, u32[]{:S(2)}) %collective-permute-start.18) | collective-permute-done | bytes 196640 | tf_op jit(solution)/shard_map/ppermute | solution.py:22
  115.8 2.6 %collective-permute-start.19 = (bf16[32,6144]{1,0:T(8,128)(2,1)S(1)}, bf16[32,6144]{1,0:T(8,128)(2,1)S(1)}, u32[]{:S(2)}, u32[]{:S(2)}) collective-permute-start(bf16[32,6144]{1,0:T(8,128)(2,1)S(1)} %pad_maximum_fusion.6), channel_id=1, source_target_pairs={{0,192},{64,0},{128,64},{192,128},{1,193},{65,1},{129,65},{193,129... | collective-permute-start | bytes 1179656 | tf_op jit(solution)/shard_map/ppermute | solution.py:22
  118.5 0.1 collective-permute-start.21
  118.6 5.8 %collective-permute-done.19 = bf16[32,6144]{1,0:T(8,128)(2,1)S(1)} collective-permute-done((bf16[32,6144]{1,0:T(8,128)(2,1)S(1)}, bf16[32,6144]{1,0:T(8,128)(2,1)S(1)}, u32[]{:S(2)}, u32[]{:S(2)}) %collective-permute-start.19) | collective-permute-done | bytes 393248 | tf_op jit(solution)/shard_map/ppermute | solution.py:22
  124.4 2.9 %collective-permute-done.21 = bf16[32,6144]{1,0:T(8,128)(2,1)S(1)} collective-permute-done((bf16[32,6144]{1,0:T(8,128)(2,1)S(1)}, bf16[32,6144]{1,0:T(8,128)(2,1)S(1)}, u32[]{:S(2)}, u32[]{:S(2)}) %collective-permute-start.21) | collective-permute-done | bytes 393248 | tf_op jit(solution)/shard_map/ppermute | solution.py:22
  127.4 0.1 add_convert_fusion.3
  127.5 1.5 collective-permute-start.22
  129.1 1.0 collective-permute-start.24
  130.2 1.2 collective-permute-start.25
  131.4 0.1 copy.54
  131.6 3.8 %collective-permute-done.22 = bf16[32,6144]{1,0:T(8,128)(2,1)S(1)} collective-permute-done((bf16[32,6144]{1,0:T(8,128)(2,1)S(1)}, bf16[32,6144]{1,0:T(8,128)(2,1)S(1)}, u32[]{:S(2)}, u32[]{:S(2)}) %collective-permute-start.22) | collective-permute-done | bytes 393248 | tf_op jit(solution)/shard_map/ppermute | solution.py:22
  135.4 1.6 collective-permute-done.24
  136.9 1.1 collective-permute-done.25
  138.1 0.2 add_convert_fusion
  138.3 0.1 reshape.106
  138.4 0.4 copy.52
  138.9 1.2 pad_maximum_fusion.2
  140.1 3.9 %all-to-all-start.2 = ((bf16[16,2,7680]{2,1,0:T(2,128)(2,1)}), bf16[16,2,7680]{2,1,0:T(2,128)(2,1)S(1)}, u32[]{:S(2)}, u32[]{:S(2)}) async-start(bf16[16,2,7680]{2,1,0:T(2,128)(2,1)} %pad_maximum_fusion.2), calls=%async_computation.2 | async-start | bytes 983040 | tf_op jit(solution)/shard_map/all_to_all | solution.py:380
  144.3 13.9 %all-to-all-done.2 = bf16[16,2,7680]{2,1,0:T(2,128)(2,1)S(1)} async-done(((bf16[16,2,7680]{2,1,0:T(2,128)(2,1)}), bf16[16,2,7680]{2,1,0:T(2,128)(2,1)S(1)}, u32[]{:S(2)}, u32[]{:S(2)}) %all-to-all-start.2) | async-done | bytes 491552 | tf_op jit(solution)/shard_map/all_to_all | solution.py:380
  158.5 0.3 slice.108
  158.7 0.4 fusion
  159.2 10.3 %all_to_all.21 = bf16[4,8,6144]{2,1,0:T(8,128)(2,1)S(1)} all-to-all(bf16[4,8,6144]{2,1,0:T(8,128)(2,1)S(1)} %broadcast_in_dim.8), channel_id=1, replica_groups=mesh['head'=4,'yh'=2,'yl'=2,'zp'=4,'zl'=2,'core'=2] {'head'}, dimensions={0} | all-to-all | bytes 786432 | tf_op jit(solution)/shard_map/all_to_all | solution.py:28
  169.5 0.9 fusion.9
  (74 shorter events, 1.9 us)
Async XLA Ops:
  0.6 143.5 %copy-start = (f32[4,4,2]{1,2,0:T(2,128)S(1)}, f32[4,4,2]{1,2,0:T(2,128)}, u32[]{:S(2)}) copy-start(f32[4,4,2]{1,2,0:T(2,128)} %param.18) | copy-start | bytes 388
  0.6 8.1 %collective-permute-start = (bf16[96,1024]{1,0:T(8,128)(2,1)}, bf16[96,1024]{1,0:T(8,128)(2,1)S(1)}, u32[]{:S(2)}, u32[]{:S(2)}) collective-permute-start(bf16[96,1024]{1,0:T(8,128)(2,1)} %bitcast.70), channel_id=1, source_target_pairs={{0,2},{2,0},{1,3},{3,1},{4,6},{6,4},{5,7},{7,5},{8,10},{10,8},{9,1... | collective-permute-start | bytes 589832 | tf_op jit(solution)/shard_map/ppermute | solution.py:22
  2.6 10.8 %collective-permute-start.1 = (bf16[96,1024]{1,0:T(8,128)(2,1)}, bf16[96,1024]{1,0:T(8,128)(2,1)S(1)}, u32[]{:S(2)}, u32[]{:S(2)}) collective-permute-start(bf16[96,1024]{1,0:T(8,128)(2,1)} %bitcast.71), channel_id=1, source_target_pairs={{0,16},{16,0},{1,17},{17,1},{2,18},{18,2},{3,19},{19,3},{4,20},{20... | collective-permute-start | bytes 589832 | tf_op jit(solution)/shard_map/ppermute | solution.py:22
  4.2 9.2 %collective-permute-start.2 = (bf16[96,1024]{1,0:T(8,128)(2,1)}, bf16[96,1024]{1,0:T(8,128)(2,1)S(1)}, u32[]{:S(2)}, u32[]{:S(2)}) collective-permute-start(bf16[96,1024]{1,0:T(8,128)(2,1)} %bitcast.72), channel_id=1, source_target_pairs={{0,18},{2,16},{16,2},{18,0},{1,19},{3,17},{17,3},{19,1},{4,22},{6,... | collective-permute-start | bytes 589832 | tf_op jit(solution)/shard_map/ppermute | solution.py:264
  14.6 23.9 %collective-permute-start.3 = (bf16[4,96,1024]{2,1,0:T(8,128)(2,1)S(1)}, bf16[4,96,1024]{2,1,0:T(8,128)(2,1)S(1)}, u32[]{:S(2)}, u32[]{:S(2)}) collective-permute-start(bf16[4,96,1024]{2,1,0:T(8,128)(2,1)S(1)} %pad_maximum_fusion.1), channel_id=1, source_target_pairs={{0,1},{1,0},{2,3},{3,2},{4,5},{5,4},{6,7},{7,6},{8,9},{9,8},{10,11... | collective-permute-start | bytes 2359304 | tf_op jit(solution)/shard_map/ppermute | solution.py:22
  14.7 23.8 %all-to-all-start = ((bf16[8,16,1152]{2,1,0:T(8,128)(2,1)}), bf16[8,16,1152]{2,1,0:T(8,128)(2,1)S(1)}, u32[]{:S(2)}, u32[]{:S(2)}) async-start(bf16[8,16,1152]{2,1,0:T(8,128)(2,1)} %shard_map.130), calls=%async_computation | async-start | bytes 589824 | tf_op jit(solution)/shard_map/all_to_all | solution.py:343
  38.5 10.6 %copy-start.4 = (bf16[1,288,6144]{2,1,0:T(8,128)(2,1)S(1)}, bf16[1,288,6144]{2,1,0:T(8,128)(2,1)}, u32[]{:S(2)}) copy-start(bf16[1,288,6144]{2,1,0:T(8,128)(2,1)} %param.21) | copy-start | bytes 10616836
  38.6 9.9 %copy-start.3 = (bf16[1,6144,288]{1,2,0:T(8,128)(2,1)S(1)}, bf16[1,6144,288]{1,2,0:T(8,128)(2,1)}, u32[]{:S(2)}) copy-start(bf16[1,6144,288]{1,2,0:T(8,128)(2,1)} %param.20) | copy-start | bytes 10616836
  38.8 9.7 %copy-start.2 = (bf16[1,6144,288]{1,2,0:T(8,128)(2,1)S(1)}, bf16[1,6144,288]{1,2,0:T(8,128)(2,1)}, u32[]{:S(2)}) copy-start(bf16[1,6144,288]{1,2,0:T(8,128)(2,1)} %param.19) | copy-start | bytes 10616836
  39.7 5.6 %collective-permute-start.4 = (f32[8,4,768]{2,1,0:T(4,128)S(1)}, f32[8,4,768]{2,1,0:T(4,128)S(1)}, u32[]{:S(2)}, u32[]{:S(2)}) collective-permute-start(f32[8,4,768]{2,1,0:T(4,128)S(1)} %get-tuple-element.69), channel_id=1, source_target_pairs={{0,64},{64,128},{128,192},{192,0},{1,65},{65,129},{129,193},{193,1... | collective-permute-start | bytes 294920 | tf_op jit(solution)/shard_map/ppermute | solution.py:22
  41.3 6.2 %collective-permute-start.5 = (f32[8,4,768]{2,1,0:T(4,128)S(1)}, f32[8,4,768]{2,1,0:T(4,128)S(1)}, u32[]{:S(2)}, u32[]{:S(2)}) collective-permute-start(f32[8,4,768]{2,1,0:T(4,128)S(1)} %get-tuple-element.68), channel_id=1, source_target_pairs={{0,128},{64,192},{128,0},{192,64},{1,129},{65,193},{129,1},{193,65... | collective-permute-start | bytes 294920 | tf_op jit(solution)/shard_map/ppermute | solution.py:22
  42.4 5.7 %collective-permute-start.6 = (f32[8,4,768]{2,1,0:T(4,128)S(1)}, f32[8,4,768]{2,1,0:T(4,128)S(1)}, u32[]{:S(2)}, u32[]{:S(2)}) collective-permute-start(f32[8,4,768]{2,1,0:T(4,128)S(1)} %get-tuple-element.67), channel_id=1, source_target_pairs={{0,192},{64,0},{128,64},{192,128},{1,193},{65,1},{129,65},{193,129... | collective-permute-start | bytes 294920 | tf_op jit(solution)/shard_map/ppermute | solution.py:22
  48.5 20.9 %collective-permute-start.7 = (bf16[288,6144]{1,0:T(8,128)(2,1)S(1)}, bf16[288,6144]{1,0:T(8,128)(2,1)S(1)}, u32[]{:S(2)}, u32[]{:S(2)}) collective-permute-start(bf16[288,6144]{1,0:T(8,128)(2,1)S(1)} %bitcast.55), channel_id=1, source_target_pairs={{0,1},{1,0},{2,3},{3,2},{4,5},{5,4},{6,7},{7,6},{8,9},{9,8},{10,11... | collective-permute-start | bytes 10616840 | tf_op jit(solution)/shard_map/ppermute | solution.py:22
  48.6 20.8 %collective-permute-start.8 = (bf16[288,6144]{1,0:T(8,128)(2,1)S(1)}, bf16[288,6144]{1,0:T(8,128)(2,1)S(1)}, u32[]{:S(2)}, u32[]{:S(2)}) collective-permute-start(bf16[288,6144]{1,0:T(8,128)(2,1)S(1)} %bitcast.57), channel_id=1, source_target_pairs={{0,1},{1,0},{2,3},{3,2},{4,5},{5,4},{6,7},{7,6},{8,9},{9,8},{10,11... | collective-permute-start | bytes 10616840 | tf_op jit(solution)/shard_map/ppermute | solution.py:22
  49.1 20.3 %collective-permute-start.9 = (bf16[288,6144]{1,0:T(8,128)(2,1)S(1)}, bf16[288,6144]{1,0:T(8,128)(2,1)S(1)}, u32[]{:S(2)}, u32[]{:S(2)}) collective-permute-start(bf16[288,6144]{1,0:T(8,128)(2,1)S(1)} %bitcast.59), channel_id=1, source_target_pairs={{0,1},{1,0},{2,3},{3,2},{4,5},{5,4},{6,7},{7,6},{8,9},{9,8},{10,11... | collective-permute-start | bytes 10616840 | tf_op jit(solution)/shard_map/ppermute | solution.py:22
  69.5 8.8 %collective-permute-start.11 = (bf16[32,6144]{1,0:T(8,128)(2,1)S(1)}, bf16[32,6144]{1,0:T(8,128)(2,1)S(1)}, u32[]{:S(2)}, u32[]{:S(2)}) collective-permute-start(bf16[32,6144]{1,0:T(8,128)(2,1)S(1)} %bitcast.61), channel_id=1, source_target_pairs={{0,192},{64,0},{128,64},{192,128},{1,193},{65,1},{129,65},{193,129... | collective-permute-start | bytes 1179656 | tf_op jit(solution)/shard_map/ppermute | solution.py:22
  70.2 10.1 %collective-permute-start.12 = (bf16[32,6144]{1,0:T(8,128)(2,1)S(1)}, bf16[32,6144]{1,0:T(8,128)(2,1)S(1)}, u32[]{:S(2)}, u32[]{:S(2)}) collective-permute-start(bf16[32,6144]{1,0:T(8,128)(2,1)S(1)} %bitcast.62), channel_id=1, source_target_pairs={{0,2},{2,0},{1,3},{3,1},{4,6},{6,4},{5,7},{7,5},{8,10},{10,8},{9,1... | collective-permute-start | bytes 1179656 | tf_op jit(solution)/shard_map/ppermute | solution.py:22
  71.8 11.1 %collective-permute-start.10 = (bf16[32,6144]{1,0:T(8,128)(2,1)S(1)}, bf16[32,6144]{1,0:T(8,128)(2,1)S(1)}, u32[]{:S(2)}, u32[]{:S(2)}) collective-permute-start(bf16[32,6144]{1,0:T(8,128)(2,1)S(1)} %bitcast.63), channel_id=1, source_target_pairs={{0,64},{64,128},{128,192},{192,0},{1,65},{65,129},{129,193},{193,1... | collective-permute-start | bytes 1179656 | tf_op jit(solution)/shard_map/ppermute | solution.py:22
  80.3 12.8 %copy-start.1 = (bf16[4,8,128,128]{3,2,1,0:T(8,128)(2,1)S(1)}, bf16[4,8,128,128]{3,2,1,0:T(8,128)(2,1)}, u32[]{:S(2)}) copy-start(bf16[4,8,128,128]{3,2,1,0:T(8,128)(2,1)} %state_ref.1) | copy-start | bytes 3145732
  80.4 12.8 %copy-start.5 = (bf16[4,4,1024]{2,1,0:T(4,128)(2,1)S(1)}, bf16[4,4,1024]{2,1,0:T(4,128)(2,1)}, u32[]{:S(2)}) copy-start(bf16[4,4,1024]{2,1,0:T(4,128)(2,1)} %key_ref.1) | copy-start | bytes 98308
  80.4 12.8 %copy-start.6 = (bf16[4,4,1024]{2,1,0:T(4,128)(2,1)S(1)}, bf16[4,4,1024]{2,1,0:T(4,128)(2,1)}, u32[]{:S(2)}) copy-start(bf16[4,4,1024]{2,1,0:T(4,128)(2,1)} %value_ref.1) | copy-start | bytes 98308
  80.4 12.8 %copy-start.7 = (f32[8]{0:T(128)S(1)}, f32[8]{0:T(128)}, u32[]{:S(2)}) copy-start(f32[8]{0:T(128)} %forget_ref.3) | copy-start | bytes 100
  80.4 9.2 %collective-permute-start.14 = (bf16[32,6144]{1,0:T(8,128)(2,1)S(1)}, bf16[32,6144]{1,0:T(8,128)(2,1)S(1)}, u32[]{:S(2)}, u32[]{:S(2)}) collective-permute-start(bf16[32,6144]{1,0:T(8,128)(2,1)S(1)} %pad_maximum_fusion.4), channel_id=1, source_target_pairs={{0,192},{64,0},{128,64},{192,128},{1,193},{65,1},{129,65},{193,129... | collective-permute-start | bytes 1179656 | tf_op jit(solution)/shard_map/ppermute | solution.py:22
  83.0 10.0 %collective-permute-start.13 = (bf16[32,6144]{1,0:T(8,128)(2,1)S(1)}, bf16[32,6144]{1,0:T(8,128)(2,1)S(1)}, u32[]{:S(2)}, u32[]{:S(2)}) collective-permute-start(bf16[32,6144]{1,0:T(8,128)(2,1)S(1)} %pad_maximum_fusion.3), channel_id=1, source_target_pairs={{0,64},{64,128},{128,192},{192,0},{1,65},{65,129},{129,193},{193,1... | collective-permute-start | bytes 1179656 | tf_op jit(solution)/shard_map/ppermute | solution.py:22
  83.4 12.0 %collective-permute-start.15 = (bf16[32,6144]{1,0:T(8,128)(2,1)S(1)}, bf16[32,6144]{1,0:T(8,128)(2,1)S(1)}, u32[]{:S(2)}, u32[]{:S(2)}) collective-permute-start(bf16[32,6144]{1,0:T(8,128)(2,1)S(1)} %pad_maximum_fusion.5), channel_id=1, source_target_pairs={{0,2},{2,0},{1,3},{3,1},{4,6},{6,4},{5,7},{7,5},{8,10},{10,8},{9,1... | collective-permute-start | bytes 1179656 | tf_op jit(solution)/shard_map/ppermute | solution.py:22
  89.7 5.7 %collective-permute-start.17 = (bf16[16,6144]{1,0:T(8,128)(2,1)S(1)}, bf16[16,6144]{1,0:T(8,128)(2,1)S(1)}, u32[]{:S(2)}, u32[]{:S(2)}) collective-permute-start(bf16[16,6144]{1,0:T(8,128)(2,1)S(1)} %slice.100), channel_id=1, source_target_pairs={{0,192},{64,0},{128,64},{192,128},{1,193},{65,1},{129,65},{193,129... | collective-permute-start | bytes 589832 | tf_op jit(solution)/shard_map/ppermute | solution.py:22
  93.0 6.7 %collective-permute-start.16 = (bf16[16,6144]{1,0:T(8,128)(2,1)S(1)}, bf16[16,6144]{1,0:T(8,128)(2,1)S(1)}, u32[]{:S(2)}, u32[]{:S(2)}) collective-permute-start(bf16[16,6144]{1,0:T(8,128)(2,1)S(1)} %slice.99), channel_id=1, source_target_pairs={{0,64},{64,128},{128,192},{192,0},{1,65},{65,129},{129,193},{193,1... | collective-permute-start | bytes 589832 | tf_op jit(solution)/shard_map/ppermute | solution.py:22
  107.2 8.6 %collective-permute-start.18 = (bf16[16,6144]{1,0:T(8,128)(2,1)S(1)}, bf16[16,6144]{1,0:T(8,128)(2,1)S(1)}, u32[]{:S(2)}, u32[]{:S(2)}) collective-permute-start(bf16[16,6144]{1,0:T(8,128)(2,1)S(1)} %get-tuple-element.39), channel_id=1, source_target_pairs={{0,192},{64,0},{128,64},{192,128},{1,193},{65,1},{129,65},{193,129... | collective-permute-start | bytes 589832 | tf_op jit(solution)/shard_map/ppermute | solution.py:22
  110.6 7.8 %collective-permute-start.20 = (bf16[16,6144]{1,0:T(8,128)(2,1)S(1)}, bf16[16,6144]{1,0:T(8,128)(2,1)S(1)}, u32[]{:S(2)}, u32[]{:S(2)}) collective-permute-start(bf16[16,6144]{1,0:T(8,128)(2,1)S(1)} %get-tuple-element.41), channel_id=1, source_target_pairs={{0,64},{64,128},{128,192},{192,0},{1,65},{65,129},{129,193},{193,1... | collective-permute-start | bytes 589832 | tf_op jit(solution)/shard_map/ppermute | solution.py:22
  110.7 7.9 %collective-permute-start.23 = (bf16[32,6144]{1,0:T(8,128)(2,1)S(1)}, bf16[32,6144]{1,0:T(8,128)(2,1)S(1)}, u32[]{:S(2)}, u32[]{:S(2)}) collective-permute-start(bf16[32,6144]{1,0:T(8,128)(2,1)S(1)} %get-tuple-element.43), channel_id=1, source_target_pairs={{0,2},{2,0},{1,3},{3,1},{4,6},{6,4},{5,7},{7,5},{8,10},{10,8},{9,1... | collective-permute-start | bytes 1179656 | tf_op jit(solution)/shard_map/ppermute | solution.py:22
  115.8 8.6 %collective-permute-start.19 = (bf16[32,6144]{1,0:T(8,128)(2,1)S(1)}, bf16[32,6144]{1,0:T(8,128)(2,1)S(1)}, u32[]{:S(2)}, u32[]{:S(2)}) collective-permute-start(bf16[32,6144]{1,0:T(8,128)(2,1)S(1)} %pad_maximum_fusion.6), channel_id=1, source_target_pairs={{0,192},{64,0},{128,64},{192,128},{1,193},{65,1},{129,65},{193,129... | collective-permute-start | bytes 1179656 | tf_op jit(solution)/shard_map/ppermute | solution.py:22
  118.5 8.9 %collective-permute-start.21 = (bf16[32,6144]{1,0:T(8,128)(2,1)S(1)}, bf16[32,6144]{1,0:T(8,128)(2,1)S(1)}, u32[]{:S(2)}, u32[]{:S(2)}) collective-permute-start(bf16[32,6144]{1,0:T(8,128)(2,1)S(1)} %pad_maximum_fusion.7), channel_id=1, source_target_pairs={{0,64},{64,128},{128,192},{192,0},{1,65},{65,129},{129,193},{193,1... | collective-permute-start | bytes 1179656 | tf_op jit(solution)/shard_map/ppermute | solution.py:22
  127.4 4.0 %copy-start.8 = (s32[4,4,2]{1,2,0:T(2,128)S(1)}, s32[4,4,2]{1,2,0:T(2,128)}, u32[]{:S(2)}) copy-start(s32[4,4,2]{1,2,0:T(2,128)} %param.17) | copy-start | bytes 388
  127.5 7.9 %collective-permute-start.22 = (bf16[32,6144]{1,0:T(8,128)(2,1)S(1)}, bf16[32,6144]{1,0:T(8,128)(2,1)S(1)}, u32[]{:S(2)}, u32[]{:S(2)}) collective-permute-start(bf16[32,6144]{1,0:T(8,128)(2,1)S(1)} %add_convert_fusion.3), channel_id=1, source_target_pairs={{0,2},{2,0},{1,3},{3,1},{4,6},{6,4},{5,7},{7,5},{8,10},{10,8},{9,1... | collective-permute-start | bytes 1179656 | tf_op jit(solution)/shard_map/ppermute | solution.py:22
  129.1 7.9 %collective-permute-start.24 = (bf16[32,6144]{1,0:T(8,128)(2,1)S(1)}, bf16[32,6144]{1,0:T(8,128)(2,1)S(1)}, u32[]{:S(2)}, u32[]{:S(2)}) collective-permute-start(bf16[32,6144]{1,0:T(8,128)(2,1)S(1)} %add_convert_fusion.2), channel_id=1, source_target_pairs={{0,192},{64,0},{128,64},{192,128},{1,193},{65,1},{129,65},{193,129... | collective-permute-start | bytes 1179656 | tf_op jit(solution)/shard_map/ppermute | solution.py:22
  130.2 7.9 %collective-permute-start.25 = (bf16[32,6144]{1,0:T(8,128)(2,1)S(1)}, bf16[32,6144]{1,0:T(8,128)(2,1)S(1)}, u32[]{:S(2)}, u32[]{:S(2)}) collective-permute-start(bf16[32,6144]{1,0:T(8,128)(2,1)S(1)} %add_convert_fusion.1), channel_id=1, source_target_pairs={{0,64},{64,128},{128,192},{192,0},{1,65},{65,129},{129,193},{193,1... | collective-permute-start | bytes 1179656 | tf_op jit(solution)/shard_map/ppermute | solution.py:22
  140.1 18.1 %all-to-all-start.2 = ((bf16[16,2,7680]{2,1,0:T(2,128)(2,1)}), bf16[16,2,7680]{2,1,0:T(2,128)(2,1)S(1)}, u32[]{:S(2)}, u32[]{:S(2)}) async-start(bf16[16,2,7680]{2,1,0:T(2,128)(2,1)} %pad_maximum_fusion.2), calls=%async_computation.2 | async-start | bytes 983040 | tf_op jit(solution)/shard_map/all_to_all | solution.py:380
